TPU v7x, 512 devices: a whole 4x8x8 slice. The times are simulated.
512 devices in a mesh: seq: 64 (over y, z_lo, core), head: 8 (over z_hi, x).
Axes of the slice: x: 4, y: 8, z: 8 (z_hi: 2, z_lo: 4; z = z_hi * 4 + z_lo), core: 2. Of those that a mesh axis runs over, the one named last changes fastest.
Arguments:
- query: bfloat16 [16384, 3072], P('seq', 'head'), may hold values from -19.25 to 19.25
- key_proj: bfloat16 [16384, 3072], P('seq', 'head'), may hold values from -3.203125 to 3.203125
- value: bfloat16 [16384, 3072], P('seq', 'head'), may hold values from -6 to 6
- head_class: int32 [24], P('head'), may hold values from 0 to 1, as said below
- sink_frame: int32 [1], replicated, may hold values from 0 to 7
- out_weight: bfloat16 [3072, 5120], P('head', 'seq'), may hold values from -0.109375 to 0.109375
Outputs:
- projected: bfloat16 [16384, 5120], P('seq', 'head')
Inputs may be any that keep to these rules, and one draw needn't show every extreme that they name: `head_class`: both classes occur among the 24 heads.
All inputs are finite; a program needn't handle non-finite values.
Results may differ from a plain program's by a relative error of at most 0.015.
Values may be sent and summed in bfloat16 or wider, within the bound.
No kernel may reach another device: no remote copies, remote signals or barrier semaphores. Data moves between devices by JAX's collectives and lax.ppermute only.
A program may use at most 64 MiB of HBM per device.

v0:
```python
import jax
import jax.numpy as jnp
from jax import lax
from jax.sharding import PartitionSpec as P

FRAMES = 8
TILE = 4


def passed_along(x, axis, by):
    count = lax.axis_size(axis)
    return lax.ppermute(x, axis, [(i, (i + by) % count) for i in range(count)])


def spread(x, axis, root):
    mine = lax.axis_index(axis) == root
    return lax.psum(jnp.where(mine, x, jnp.zeros_like(x)), axis)


def attend(query_matrix, key_matrix, value_matrix, sink_k, sink_v):
    score_scale = query_matrix.shape[-1] ** (-0.5)
    scores_main = (
        jnp.einsum("qd,kd->qk", query_matrix, key_matrix, preferred_element_type=jnp.float32)
        * score_scale
    )
    scores_sink = (
        jnp.einsum("qd,kd->qk", query_matrix, sink_k, preferred_element_type=jnp.float32)
        * score_scale
    )
    largest = jnp.maximum(jnp.max(scores_main, axis=-1), jnp.max(scores_sink, axis=-1))[:, None]
    weights_main = jnp.exp(scores_main - largest)
    weights_sink = jnp.exp(scores_sink - largest)
    totals = jnp.sum(weights_main, axis=-1) + jnp.sum(weights_sink, axis=-1)
    weight_totals = jnp.einsum(
        "qk,kd->qd",
        weights_main.astype(jnp.bfloat16),
        value_matrix,
        preferred_element_type=jnp.float32,
    )
    weight_totals = weight_totals + jnp.einsum(
        "qk,kd->qd", weights_sink.astype(jnp.bfloat16), sink_v, preferred_element_type=jnp.float32
    )
    return (weight_totals / totals[:, None]).astype(jnp.bfloat16)


def attend_plain(query_matrix, key_matrix, value_matrix):
    score_scale = query_matrix.shape[-1] ** (-0.5)
    logit_scores = (
        jnp.einsum("yzt,yjt->yzj", query_matrix, key_matrix, preferred_element_type=jnp.float32)
        * score_scale
    )
    largest = jnp.max(logit_scores, axis=-1)[..., None]
    softmax_weights = jnp.exp(logit_scores - largest)
    totals = jnp.sum(softmax_weights, axis=-1)
    weight_totals = jnp.einsum(
        "iut,ito->iuo",
        softmax_weights.astype(jnp.bfloat16),
        value_matrix,
        preferred_element_type=jnp.float32,
    )
    return (weight_totals / totals[..., None]).astype(jnp.bfloat16)


def per_device(query, key_proj, value, head_class, sink_frame, out_weight):
    head_count = head_class.shape[0]
    head_width = query.shape[1] // head_count
    row_count = query.shape[0]
    seq_count = lax.axis_size("seq")
    frame_count = FRAMES
    split_count = seq_count // frame_count
    piece_rows = row_count // seq_count
    block_count = piece_rows // TILE
    sink_index = sink_frame[0]
    key_value = jnp.stack((key_proj, value))
    pieces = [key_value]
    moving = key_value
    for step in range(1, split_count):
        moving = passed_along(moving, "seq", frame_count)
        pieces.append(moving)
    frame_pair = jnp.concatenate(pieces, axis=1)
    sink_pieces = []
    for part_index in range(split_count):
        sink_pieces.append(spread(key_value, "seq", part_index * frame_count + sink_index))
    sink_pair = jnp.concatenate(sink_pieces, axis=1)

    def spatial_head(items):
        index, kind = items
        start = index * head_width

        def run_head():
            q_cols = lax.dynamic_slice_in_dim(query, start, head_width, 1)
            k_cols = lax.dynamic_slice_in_dim(frame_pair[0], start, head_width, 1)
            v_cols = lax.dynamic_slice_in_dim(frame_pair[1], start, head_width, 1)
            sink_k = lax.dynamic_slice_in_dim(sink_pair[0], start, head_width, 1)
            sink_v = lax.dynamic_slice_in_dim(sink_pair[1], start, head_width, 1)
            return attend(q_cols, k_cols, v_cols, sink_k, sink_v)

        def skip_head():
            return jnp.zeros((row_count, head_width), jnp.bfloat16)

        return lax.cond(kind == 0, run_head, skip_head)

    spatial = lax.map(spatial_head, (jnp.arange(head_count, dtype=jnp.int32), head_class))
    spatial = spatial.transpose(1, 0, 2).reshape(row_count, head_count * head_width)
    moved_query, moved_key, moved_value = (
        lax.all_to_all(query, "seq", split_axis=0, concat_axis=0, tiled=True),
        lax.all_to_all(key_proj, "seq", split_axis=0, concat_axis=0, tiled=True),
        lax.all_to_all(value, "seq", split_axis=0, concat_axis=0, tiled=True),
    )

    def to_tiles(x):
        shaped = x.reshape(split_count, frame_count, block_count, TILE, head_count, head_width)
        return shaped.transpose(4, 0, 2, 1, 3, 5).reshape(
            head_count * split_count * block_count, frame_count * TILE, head_width
        )

    temporal = attend_plain(to_tiles(moved_query), to_tiles(moved_key), to_tiles(moved_value))
    temporal = temporal.reshape(head_count, split_count, block_count, frame_count, TILE, head_width)
    temporal = temporal.transpose(1, 3, 2, 4, 0, 5).reshape(row_count, head_count * head_width)
    returned = lax.all_to_all(temporal, "seq", split_axis=0, concat_axis=0, tiled=True)
    column_class = jnp.repeat(head_class == 1, head_width)
    attended = jnp.where(column_class[None, :], returned, spatial)
    terms = jnp.dot(
        attended,
        lax.all_gather(out_weight, "seq", axis=1, tiled=True),
        preferred_element_type=jnp.float32,
    )
    return lax.psum_scatter(terms.astype(jnp.bfloat16), "head", scatter_dimension=1, tiled=True)


def solution(mesh):
    in_specs = (
        P("seq", "head"),
        P("seq", "head"),
        P("seq", "head"),
        P("head"),
        P(),
        P("head", "seq"),
    )
    out_specs = P("seq", "head")
    return jax.shard_map(
        per_device, mesh=mesh, in_specs=in_specs, out_specs=out_specs, check_vma=False
    )
```

profile of v0, /device:TPU:6, one launch (start us, length us, event | category | flops | bytes accessed | tf_op | source)
XLA Modules:
  0.0 817.6 jit_solution(857809969183749767)
XLA Ops:
  7.2 2.1 broadcast_select_fusion.1
  9.3 2.7 broadcast_select_fusion
  12.8 3.5 collective-permute-start
  17.0 12.6 %all-to-all-start.1 = ((bf16[64,4,384]{2,1,0:T(4,128)(2,1)}), bf16[64,4,384]{2,1,0:T(4,128)(2,1)S(1)}, u32[]{:S(2)}, u32[]{:S(2)}) async-start(bf16[64,4,384]{2,1,0:T(4,128)(2,1)} %all_to_all.28), calls=%async_computation.1 | async-start | bytes 393216 | tf_op jit(solution)/shard_map/all_to_all | solution.py:107
  29.7 3.5 collective-permute-start.1
  33.9 7.8 all-to-all-done.1
  41.7 5.4 all-to-all-start
  47.2 3.4 collective-permute-start.2
  50.5 1.7 all_to_all.30
  52.2 6.5 all-to-all-done
  58.7 5.4 all-to-all-start.2
  64.2 3.4 collective-permute-start.3
  67.5 1.0 copy.30
  69.3 1.8 copy.31
  71.1 0.9 copy.28
  72.8 1.8 copy.29
  74.6 1.2 all-to-all-done.2
  75.8 1.0 copy.32
  77.5 1.1 copy.33
  78.6 1.3 fusion.39
  80.6 2.6 collective-permute-start.4
  83.5 0.9 copy.45
  84.4 1.1 all_to_all.32
  86.3 9.7 %all-to-all-start.3 = ((bf16[64,4,384]{2,1,0:T(4,128)(2,1)}), bf16[64,4,384]{2,1,0:T(4,128)(2,1)S(1)}, u32[]{:S(2)}, u32[]{:S(2)}) async-start(bf16[64,4,384]{2,1,0:T(4,128)(2,1)} %copy.36), calls=%async_computation.3 | async-start | bytes 393216 | tf_op jit(solution)/shard_map/all_to_all | solution.py:120
  96.1 3.5 collective-permute-start.5
  99.7 1.1 constant_dynamic-update-slice_fusion.7
  100.8 6.8 all-to-all-done.3
  108.3 1.1 constant_dynamic-update-slice_fusion.6
  109.3 3.3 collective-permute-done.5
  112.7 2.1 collective-permute-start.6
  114.8 1.1 constant_dynamic-update-slice_fusion.5
  115.8 1.1 constant_dynamic-update-slice_fusion.4
  116.9 1.1 constant_dynamic-update-slice_fusion.3
  118.0 1.1 constant_dynamic-update-slice_fusion.2
  119.0 8.0 collective-permute-done.6
  127.1 445.2 %all-reduce.3.cloned.1.call-done = (bf16[2,256,384]{2,1,0:T(8,128)(2,1)}, bf16[2,256,384]{2,1,0:T(8,128)(2,1)}, bf16[2,256,384]{2,1,0:T(8,128)(2,1)}, bf16[2,256...) async-done(((bf16[2,256,384]{2,1,0:T(8,128)(2,1)}, ...) | async-done | bytes 3145744 | tf_op jit(solution)/shard_map/psum | solution.py:17
  572.3 1.2 constant_dynamic-update-slice_fusion.16
  573.4 1.1 constant_dynamic-update-slice_fusion.15
  574.5 1.1 constant_dynamic-update-slice_fusion.14
  575.6 1.1 constant_dynamic-update-slice_fusion.13
  577.0 1.7 copy-done
  578.6 6.0 while.11
  584.7 1.1 copy.38
  585.8 111.3 %all-gather.2.cloned.1.call-done = bf16[384,5120]{0,1:T(8,128)(2,1)} async-done(((bf16[384,80]{0,1:T(8,128)(2,1)}), bf16[384,5120]{0,1:T(8,128)(2,1)}) %all-gather.2.cloned.1.call-update) | async-done | bytes 3932176 | tf_op jit(solution)/shard_map/all_gather | solution.py:125
  697.1 3.8 convolution_convert_fusion
  700.9 2.6 copy.40
  703.5 105.7 %reduce-scatter.4.cloned.1.call-done = bf16[640,256]{1,0:T(8,128)(2,1)} async-done(((bf16[5120,256]{1,0:T(8,128)(2,1)}), bf16[640,256]{1,0:T(8,128)(2,1)}) %reduce-scatter.4.cloned.1.call-update) | async-done | bytes 327696
  809.2 1.9 copy.41
  (63 shorter events, 11.6 us)
Async XLA Ops:
  6.5 565.7 %all-reduce.3.cloned.1.call-start = ((), (), s32[]{:S(2)}) async-start(), calls=%async_computation.7 | async-start | bytes 6291456 | tf_op jit(solution)/shard_map/psum | solution.py:17
  9.3 7.0 copy-start.2
  9.3 23.8 %copy-start.1 = (bf16[256,384]{1,0:T(8,128)(2,1)S(1)}, bf16[256,384]{1,0:T(8,128)(2,1)}, u32[]{:S(2)}) copy-start(bf16[256,384]{1,0:T(8,128)(2,1)} %param.10) | copy-start | bytes 589828
  12.0 685.1 %all-gather.2.cloned.1.call-start = ((), (), s32[]{:S(2)}) async-start(), calls=%async_computation.5 | async-start | bytes 3993600 | tf_op jit(solution)/shard_map/all_gather | solution.py:125
  12.8 16.9 %collective-permute-start = (bf16[2,256,384]{2,1,0:T(8,128)(2,1)}, bf16[2,256,384]{2,1,0:T(8,128)(2,1)}, u32[]{:S(2)}, u32[]{:S(2)}) collective-permute-start(bf16[2,256,384]{2,1,0:T(8,128)(2,1)} %get-tuple-element.128), channel_id=1, source_target_pairs={{0,64},{8,72},{16,80},{24,88},{32,96},{40,104},{48,112},{56,120},{... | collective-permute-start | bytes 1179656 | tf_op jit(solution)/shard_map/ppermute | solution.py:12
  17.0 24.7 %all-to-all-start.1 = ((bf16[64,4,384]{2,1,0:T(4,128)(2,1)}), bf16[64,4,384]{2,1,0:T(4,128)(2,1)S(1)}, u32[]{:S(2)}, u32[]{:S(2)}) async-start(bf16[64,4,384]{2,1,0:T(4,128)(2,1)} %all_to_all.28), calls=%async_computation.1 | async-start | bytes 393216 | tf_op jit(solution)/shard_map/all_to_all | solution.py:107
  29.7 17.5 %collective-permute-start.1 = (bf16[2,256,384]{2,1,0:T(8,128)(2,1)}, bf16[2,256,384]{2,1,0:T(8,128)(2,1)}, u32[]{:S(2)}, u32[]{:S(2)}) collective-permute-start(bf16[2,256,384]{2,1,0:T(8,128)(2,1)} %collective-permute-done), channel_id=1, source_target_pairs={{0,64},{8,72},{16,80},{24,88},{32,96},{40,104},{48,112},{56,120},{... | collective-permute-start | bytes 1179656 | tf_op jit(solution)/shard_map/ppermute | solution.py:12
  41.7 22.4 %copy-start.3 = (bf16[64,4,384]{2,1,0:T(4,128)(2,1)}, bf16[64,4,384]{2,1,0:T(4,128)(2,1)S(1)}, u32[]{:S(2)}) copy-start(bf16[64,4,384]{2,1,0:T(4,128)(2,1)S(1)} %all-to-all-done.1) | copy-start | bytes 589828
  41.7 17.0 %all-to-all-start = ((bf16[64,4,384]{2,1,0:T(4,128)(2,1)}), bf16[64,4,384]{2,1,0:T(4,128)(2,1)}, u32[]{:S(2)}, u32[]{:S(2)}) async-start(bf16[64,4,384]{2,1,0:T(4,128)(2,1)} %all_to_all.26), calls=%async_computation | async-start | bytes 393216 | tf_op jit(solution)/shard_map/all_to_all | solution.py:106
  47.2 17.0 %collective-permute-start.2 = (bf16[2,256,384]{2,1,0:T(8,128)(2,1)}, bf16[2,256,384]{2,1,0:T(8,128)(2,1)}, u32[]{:S(2)}, u32[]{:S(2)}) collective-permute-start(bf16[2,256,384]{2,1,0:T(8,128)(2,1)} %collective-permute-done.1), channel_id=1, source_target_pairs={{0,64},{8,72},{16,80},{24,88},{32,96},{40,104},{48,112},{56,120},{... | collective-permute-start | bytes 1179656 | tf_op jit(solution)/shard_map/ppermute | solution.py:12
  58.7 17.1 %all-to-all-start.2 = ((bf16[64,4,384]{2,1,0:T(4,128)(2,1)}), bf16[64,4,384]{2,1,0:T(4,128)(2,1)}, u32[]{:S(2)}, u32[]{:S(2)}) async-start(bf16[64,4,384]{2,1,0:T(4,128)(2,1)} %all_to_all.30), calls=%async_computation.2 | async-start | bytes 393216 | tf_op jit(solution)/shard_map/all_to_all | solution.py:108
  64.2 16.4 %collective-permute-start.3 = (bf16[2,256,384]{2,1,0:T(8,128)(2,1)}, bf16[2,256,384]{2,1,0:T(8,128)(2,1)}, u32[]{:S(2)}, u32[]{:S(2)}) collective-permute-start(bf16[2,256,384]{2,1,0:T(8,128)(2,1)} %collective-permute-done.2), channel_id=1, source_target_pairs={{0,64},{8,72},{16,80},{24,88},{32,96},{40,104},{48,112},{56,120},{... | collective-permute-start | bytes 1179656 | tf_op jit(solution)/shard_map/ppermute | solution.py:12
  72.8 23.3 %copy-start.8 = (s32[3]{0:T(128)S(1)}, s32[3]{0:T(128)}, u32[]{:S(2)}) copy-start(s32[3]{0:T(128)} %param.13) | copy-start | bytes 40
  80.6 15.6 %collective-permute-start.4 = (bf16[2,256,384]{2,1,0:T(8,128)(2,1)}, bf16[2,256,384]{2,1,0:T(8,128)(2,1)}, u32[]{:S(2)}, u32[]{:S(2)}) collective-permute-start(bf16[2,256,384]{2,1,0:T(8,128)(2,1)} %collective-permute-done.3), channel_id=1, source_target_pairs={{0,64},{8,72},{16,80},{24,88},{32,96},{40,104},{48,112},{56,120},{... | collective-permute-start | bytes 1179656 | tf_op jit(solution)/shard_map/ppermute | solution.py:12
  86.3 21.2 %all-to-all-start.3 = ((bf16[64,4,384]{2,1,0:T(4,128)(2,1)}), bf16[64,4,384]{2,1,0:T(4,128)(2,1)S(1)}, u32[]{:S(2)}, u32[]{:S(2)}) async-start(bf16[64,4,384]{2,1,0:T(4,128)(2,1)} %copy.36), calls=%async_computation.3 | async-start | bytes 393216 | tf_op jit(solution)/shard_map/all_to_all | solution.py:120
  96.0 713.2 %reduce-scatter.4.cloned.1.call-start = ((), (), s32[]{:S(2)}) async-start(), calls=%async_computation.6 | async-start | bytes 2949120
  96.1 16.5 %collective-permute-start.5 = (bf16[2,256,384]{2,1,0:T(8,128)(2,1)}, bf16[2,256,384]{2,1,0:T(8,128)(2,1)}, u32[]{:S(2)}, u32[]{:S(2)}) collective-permute-start(bf16[2,256,384]{2,1,0:T(8,128)(2,1)} %collective-permute-done.4), channel_id=1, source_target_pairs={{0,64},{8,72},{16,80},{24,88},{32,96},{40,104},{48,112},{56,120},{... | collective-permute-start | bytes 1179656 | tf_op jit(solution)/shard_map/ppermute | solution.py:12
  112.7 14.3 %collective-permute-start.6 = (bf16[2,256,384]{2,1,0:T(8,128)(2,1)}, bf16[2,256,384]{2,1,0:T(8,128)(2,1)S(1)}, u32[]{:S(2)}, u32[]{:S(2)}) collective-permute-start(bf16[2,256,384]{2,1,0:T(8,128)(2,1)} %collective-permute-done.5), channel_id=1, source_target_pairs={{0,64},{8,72},{16,80},{24,88},{32,96},{40,104},{48,112},{56,120},{... | collective-permute-start | bytes 1179656 | tf_op jit(solution)/shard_map/ppermute | solution.py:12
  572.3 4.4 copy-start.7
  572.3 4.4 copy-start.6
  572.3 4.5 copy-start.5
  572.3 4.6 copy-start.4
  577.0 1.7 copy-start
Sparse Core Ops, SparseCore 0:
  12.2 560.0 all-reduce.2
  574.7 122.4 all-gather.1
  703.6 105.5 reduce-scatter.3
where the time goes:
time: 819 us; the launch traced here: 818 us
  waiting for transfers between devices  697 us (85%)
  starting transfers between devices  55.2 us (7%)
  local copies, waits for them, and re-layouts  38.9 us (5%)
  between operations  14.1 us (2%)
    psum x1, waiting for transfers between devices, spread(): return lax.psum(jnp.where(mine, x, jnp.zeros_like(x)), axis)  445 us
    all_gather x1, waiting for transfers between devices, per_device(): lax.all_gather(out_weight, 'seq', axis=1, tiled=True)  111 us
    unnamed x4, waiting for transfers between devices  106 us
    ppermute x7, starting transfers between devices, passed_along(): return lax.ppermute(x, axis, [(i, (i + by) % count) for i in range(count)])  21.9 us
    unnamed x33, local copies, waits for them, and re-layouts  17 us
  transfers between devices with their start and end apart: 14, of which 10 were waited for; matrix products, arithmetic and copies ran while one was open for 4% of the time, Pallas kernels for 0%

commit v1 on v0

v1 whole, which is shorter than its diff:
```python
import functools

import jax
import jax.numpy as jnp
from jax import lax
from jax.experimental import pallas as pl
from jax.experimental.pallas import tpu as pltpu
from jax.sharding import Mesh, PartitionSpec as P

HD = 128
NH = 3
TILE = 4
LOG2E = 1.4426950408889634
SCALE2 = HD**-0.5 * LOG2E
NT = (((1,), (1,)), ((), ()))
TN = (((0,), (0,)), ((), ()))
NN = (((1,), (0,)), ((), ()))


def dot(a, b, dims):
    return lax.dot_general(a, b, dims, preferred_element_type=jnp.float32)


def swap(x, axis):
    return lax.ppermute(x, axis, [(0, 1), (1, 0)])


def spatial_kernel(hc_ref, q_ref, k_ref, v_ref, ko_ref, vo_ref, sa_ref, sb_ref, core_ref, out_ref):
    parts = q_ref.shape[0]
    rows = q_ref.shape[1]
    core = core_ref[0]
    for h in range(NH):
        cols = slice(h * HD, (h + 1) * HD)

        @pl.when(hc_ref[h] == 0)
        def _():
            mine, other = sa_ref[:, cols], sb_ref[:, cols]
            first = core == 0
            sk = jnp.where(first, mine, other)
            sv = jnp.where(first, other, mine)
            keys = jnp.concatenate([k_ref[:, cols], ko_ref[:, cols], sk], axis=0)
            vals = jnp.concatenate([v_ref[:, cols], vo_ref[:, cols], sv], axis=0)
            for p in range(parts):
                q = q_ref[p, :, cols]
                s = dot(keys, q, NT) * SCALE2
                m = jnp.max(s, axis=0, keepdims=True)
                w = jnp.exp2(s - m)
                total = jnp.sum(w, axis=0, keepdims=True)
                o = dot(vals, w.astype(jnp.bfloat16), TN)
                out_ref[p, cols, :] = (o / total).astype(jnp.bfloat16)
                lse = m + jnp.log2(total)
                hi = lse.astype(jnp.bfloat16).astype(jnp.float32)
                mid = (lse - hi).astype(jnp.bfloat16).astype(jnp.float32)
                low = lse - hi - mid
                row = lax.broadcasted_iota(jnp.int32, (16, rows), 0)
                stats = jnp.where(row == 0, hi, jnp.where(row == 1, mid, low))
                out_ref[p, NH * HD + 16 * h : NH * HD + 16 * h + 16, :] = stats.astype(jnp.bfloat16)


def spatial(hc, q, k, v, ko, vo, sa, sb, core):
    parts, rows, width = q.shape
    smem = pl.BlockSpec(memory_space=pltpu.SMEM)
    vmem = pl.BlockSpec(memory_space=pltpu.VMEM)
    return pl.pallas_call(
        spatial_kernel,
        out_shape=jax.ShapeDtypeStruct((parts, width + 16 * NH, rows), jnp.bfloat16),
        in_specs=[smem] + [vmem] * 7 + [smem],
        out_specs=vmem,
        compiler_params=pltpu.CompilerParams(vmem_limit_bytes=24 * 1024 * 1024),
        name="spatial",
    )(hc, q, k, v, ko, vo, sa, sb, core)


def temporal_kernel(hc_ref, q_ref, k_ref, v_ref, out_ref):
    rows = q_ref.shape[0]
    span = rows // 8
    for h in range(NH):
        cols = slice(h * HD, (h + 1) * HD)

        @pl.when(hc_ref[h] == 1)
        def _():
            s = dot(q_ref[:, cols], k_ref[:, cols], NT) * SCALE2
            i = lax.broadcasted_iota(jnp.int32, (rows, rows), 0)
            j = lax.broadcasted_iota(jnp.int32, (rows, rows), 1)
            s = jnp.where((i % span) // TILE == (j % span) // TILE, s, -jnp.inf)
            w = jnp.exp2(s - jnp.max(s, axis=1, keepdims=True))
            total = jnp.sum(w, axis=1, keepdims=True)
            o = dot(w.astype(jnp.bfloat16), v_ref[:, cols], NN)
            out_ref[:, cols] = (o / total).astype(jnp.bfloat16)


def temporal(hc, q, k, v):
    smem = pl.BlockSpec(memory_space=pltpu.SMEM)
    vmem = pl.BlockSpec(memory_space=pltpu.VMEM)
    return pl.pallas_call(
        temporal_kernel,
        out_shape=jax.ShapeDtypeStruct(q.shape, jnp.bfloat16),
        in_specs=[smem] + [vmem] * 3,
        out_specs=vmem,
        compiler_params=pltpu.CompilerParams(vmem_limit_bytes=16 * 1024 * 1024),
        name="temporal",
    )(hc, q, k, v)


def combine_kernel(hc_ref, part_ref, back_ref, out_ref):
    parts = part_ref.shape[0]
    for h in range(NH):
        cols = slice(h * HD, (h + 1) * HD)

        @pl.when(hc_ref[h] == 0)
        def _():
            lses = []
            for p in range(parts):
                st = part_ref[p, NH * HD + 16 * h : NH * HD + 16 * h + 16, :].astype(jnp.float32)
                lses.append(st[0:1] + st[1:2] + st[2:3])
            m = functools.reduce(jnp.maximum, lses)
            es = [jnp.exp2(l - m) for l in lses]
            inv = 1.0 / sum(es)
            o = sum(part_ref[p, cols, :].astype(jnp.float32) * (es[p] * inv) for p in range(parts))
            out_ref[:, cols] = o.T.astype(jnp.bfloat16)

        @pl.when(hc_ref[h] != 0)
        def _():
            out_ref[:, cols] = back_ref[:, cols]


def combine(hc, part, back):
    smem = pl.BlockSpec(memory_space=pltpu.SMEM)
    vmem = pl.BlockSpec(memory_space=pltpu.VMEM)
    return pl.pallas_call(
        combine_kernel,
        out_shape=jax.ShapeDtypeStruct(back.shape, jnp.bfloat16),
        in_specs=[smem, vmem, vmem],
        out_specs=vmem,
        compiler_params=pltpu.CompilerParams(vmem_limit_bytes=16 * 1024 * 1024),
        name="combine",
    )(hc, part, back)


def project_kernel(w_ref, own_ref, other_ref, weight_ref, out_ref):
    here = w_ref[0] * 4
    there = 4 - here
    total = jnp.zeros(out_ref.shape, jnp.float32)
    for i in range(4):
        total += dot(own_ref[i], weight_ref[here + i], NT)
        total += dot(other_ref[i], weight_ref[there + i], NT)
    out_ref[...] = total.astype(jnp.bfloat16)


def project(w, own, other, weight):
    smem = pl.BlockSpec(memory_space=pltpu.SMEM)
    vmem = pl.BlockSpec(memory_space=pltpu.VMEM)
    return pl.pallas_call(
        project_kernel,
        out_shape=jax.ShapeDtypeStruct((own.shape[1], weight.shape[1]), jnp.bfloat16),
        in_specs=[smem, vmem, vmem, vmem],
        out_specs=vmem,
        compiler_params=pltpu.CompilerParams(vmem_limit_bytes=24 * 1024 * 1024),
        name="project",
    )(w, own, other, weight)


def to_all(x, axis):
    n = lax.axis_size(axis)
    return lax.all_to_all(jnp.broadcast_to(x[None], (n,) + x.shape), axis, 0, 0, tiled=True)


def per_device(query, key_proj, value, head_class, sink_frame, out_weight):
    rows, width = query.shape
    core = lax.axis_index("c")
    sink = sink_frame[0]
    is_temporal = jnp.repeat(head_class == 1, HD)

    turned = lax.ppermute(
        out_weight.T, ("a", "b", "w", "x"), [(y * 8 + h, h * 8 + y) for y in range(8) for h in range(8)]
    )
    weight = lax.all_gather(turned, ("z", "c"), axis=0, tiled=True)
    weight = lax.all_gather(weight, ("a", "b"), axis=0)

    key_value = jnp.concatenate([key_proj, value], axis=0)
    other_kv = swap(key_value, "b")
    group_query = to_all(query, "a")

    carried = jnp.where(core == 0, key_proj, value)
    given = swap(jnp.where(core == 0, value, key_proj), "c")
    candidate = jnp.where(sink % 2 == core, carried, given)
    pieces = [x.reshape(4, rows // 4, width) for x in (query, key_proj, value)]
    pieces = jnp.concatenate(pieces + [jnp.zeros_like(pieces[0])], axis=1)
    sent = jnp.where(is_temporal, pieces, candidate[None])
    got = lax.all_to_all(sent, "z", 0, 0, tiled=True)

    sink_part = lax.dynamic_index_in_dim(got, sink // 2, 0, keepdims=False)
    sink_pair = jnp.concatenate([sink_part, swap(sink_part, "b")], axis=0)
    sink_other = swap(sink_pair, "c")

    half = rows // 8
    tokens = got.reshape(4, 4, 2, half, width)[:, :3]
    keep = jnp.where(core == 0, tokens[:, :, 0], tokens[:, :, 1])
    give = jnp.where(core == 0, tokens[:, :, 1], tokens[:, :, 0])
    come = swap(give, "c")
    first = jnp.where(core == 0, keep, come)
    second = jnp.where(core == 0, come, keep)
    both = jnp.stack([first, second], axis=1)
    tq, tk, tv = (both[:, :, i].reshape(rows, width) for i in range(3))
    back = temporal(head_class, tq, tk, tv)
    back = lax.all_to_all(back.reshape(8, half, width), ("z", "c"), 0, 0, tiled=True).reshape(rows, width)

    part = spatial(
        head_class, group_query, key_proj, value, other_kv[:rows], other_kv[rows:], sink_pair, sink_other,
        core.reshape(1),
    )
    part = lax.all_to_all(part, "a", 0, 0, tiled=True)
    attended = combine(head_class, part, back)

    other = swap(attended, "w")
    own_all = to_all(attended, "x")
    other_all = to_all(other, "x")
    return project(lax.axis_index("w").reshape(1), own_all, other_all, weight)


def solution(mesh):
    fine = Mesh(mesh.devices.reshape(4, 2, 4, 2, 2, 4), ("a", "b", "z", "c", "w", "x"))
    seq, head = ("a", "b", "z", "c"), ("w", "x")
    in_specs = (P(seq, head), P(seq, head), P(seq, head), P(head), P(), P(head, seq))
    return jax.shard_map(per_device, mesh=fine, in_specs=in_specs, out_specs=P(seq, head), check_vma=False)
```

time: 819 us -> 216 us (0.26)
  the two profiles are of different devices: /device:TPU:6 before, /device:TPU:136 now
where the time goes in v1:
time: 216 us; the launch traced here: 215 us
  blocking collectives  69.8 us (32%)
  waiting for transfers between devices  56.3 us (26%)
  starting transfers between devices  55.9 us (26%)
  between operations  14.3 us (7%)
  Pallas kernels  11.2 us (5%)
  local copies, waits for them, and re-layouts  5.27 us (2%)
  other arithmetic  2.26 us (1%)
    ppermute x6, waiting for transfers between devices, swap(): return lax.ppermute(x, axis, [(0, 1), (1, 0)])  41.5 us
    all_to_all x3, starting transfers between devices, to_all(): lax.all_to_all(jnp.broadcast_to(x[None], (n,) + x.shape), axis, 0, 0, til...  31.1 us
    all_to_all x1, blocking collectives, per_device(): part = lax.all_to_all(part, 'a', 0, 0, tiled=True)  30.4 us
    all_to_all x1, blocking collectives, per_device(): got = lax.all_to_all(sent, 'z', 0, 0, tiled=True)  24.7 us
    ppermute x6, starting transfers between devices, swap(): return lax.ppermute(x, axis, [(0, 1), (1, 0)])  15.4 us
    all_gather x1, blocking collectives, per_device(): weight = lax.all_gather(turned, ('z', 'c'), axis=0, tiled=True)  14.8 us
    all_to_all x3, waiting for transfers between devices, to_all(): lax.all_to_all(jnp.broadcast_to(x[None], (n,) + x.shape), axis, 0, 0, til...  10.9 us
    pallas_call x1, Pallas kernels, spatial(): pl.pallas_call(spatial_kernel, out_shape=jax.ShapeDtypeStruct((parts, wid...  6.11 us
  transfers between devices with their start and end apart: 12, of which 6 were waited for; matrix products, arithmetic and copies ran while one was open for 3% of the time, Pallas kernels for 4%

profile of v1, /device:TPU:136, one launch (start us, length us, event | category | flops | bytes accessed | tf_op | source)
XLA Modules:
  0.0 215.1 jit_solution(16921676613664543926)
XLA Ops:
  6.5 0.0 copy-start
  6.5 0.0 copy-start.1
  6.5 0.0 all-gather.3.cloned.1.call-start
  6.6 3.4 %collective-permute-start.6 = (bf16[80,384]{1,0:T(8,128)(2,1)}, bf16[80,384]{1,0:T(8,128)(2,1)S(1)}, u32[]{:S(2)}, u32[]{:S(2)}) collective-permute-start(bf16[80,384]{1,0:T(8,128)(2,1)} %bitcast.64), channel_id=1, source_target_pairs={{0,0},{1,64},{2,128},{3,192},{4,256},{5,320},{6,384},{7,448},{64,1... | collective-permute-start | bytes 184328 | tf_op jit(solution)/shard_map/ppermute | solution.py:174
  10.0 3.9 %collective-permute-done.6 = bf16[80,384]{1,0:T(8,128)(2,1)S(1)} collective-permute-done((bf16[80,384]{1,0:T(8,128)(2,1)}, bf16[80,384]{1,0:T(8,128)(2,1)S(1)}, u32[]{:S(2)}, u32[]{:S(2)}) %collective-permute-start.6) | collective-permute-done | bytes 61472 | tf_op jit(solution)/shard_map/ppermute | solution.py:174
  13.9 14.8 %all_gather.9 = bf16[640,384]{1,0:T(8,128)(2,1)} all-gather(bf16[80,384]{1,0:T(8,128)(2,1)S(1)} %collective-permute-done.6), channel_id=1, replica_groups=mesh['a'=4,'b'=2,'z'=4,'c'=2,'w'=2,'x'=4] {'z','c'}, dimensions={0}, use_global_device_ids=true | all-gather | bytes 552960 | tf_op jit(solution)/shard_map/all_gather | solution.py:177
  28.7 0.0 all-gather.3.cloned.1.call-update
  28.8 1.0 broadcast_select_fusion
  29.7 2.3 %collective-permute-start.1 = (bf16[256,384]{1,0:T(8,128)(2,1)S(1)}, bf16[256,384]{1,0:T(8,128)(2,1)S(1)}, u32[]{:S(2)}, u32[]{:S(2)}) collective-permute-start(bf16[256,384]{1,0:T(8,128)(2,1)S(1)} %broadcast_select_fusion), channel_id=1, source_target_pairs={{0,8},{8,0},{1,9},{9,1},{2,10},{10,2},{3,11},{11,3},{4,12},{12,4},... | collective-permute-start | bytes 589832 | tf_op jit(solution)/shard_map/ppermute | solution.py:25
  32.7 0.1 pad.7.clone
  32.7 0.0 copy-done.3
  32.8 0.1 broadcast_bitcast_fusion
  32.8 0.2 collective-permute-done.1
  33.1 0.0 copy-done
  33.1 0.0 copy-done.1
  33.1 0.0 copy-done.4
  33.1 0.2 maximum_select_fusion
  33.4 24.7 %all_to_all.30 = bf16[4,256,384]{2,1,0:T(8,128)(2,1)S(1)} all-to-all(bf16[4,256,384]{2,1,0:T(8,128)(2,1)S(1)} %maximum_select_fusion), channel_id=1, replica_groups=mesh['a'=4,'b'=2,'z'=4,'c'=2,'w'=2,'x'=4] {'z'}, dimensions={0} | all-to-all | bytes 1572864 | tf_op jit(solution)/shard_map/all_to_all | solution.py:190
  58.0 1.0 broadcast_in_dim.22
  59.0 19.5 %all-to-all-start = ((bf16[4,256,384]{2,1,0:T(8,128)(2,1)}), bf16[4,256,384]{2,1,0:T(8,128)(2,1)S(1)}, u32[]{:S(2)}, u32[]{:S(2)}) async-start(bf16[4,256,384]{2,1,0:T(8,128)(2,1)} %broadcast_in_dim.22), calls=%async_computation | async-start | bytes 1572864 | tf_op jit(solution)/shard_map/all_to_all | solution.py:165
  78.5 1.9 collective-permute-start.2
  80.4 1.9 collective-permute-start.4
  82.4 0.8 pad_maximum_fusion
  83.2 3.9 %collective-permute-start = (bf16[512,384]{1,0:T(8,128)(2,1)}, bf16[512,384]{1,0:T(8,128)(2,1)S(1)}, u32[]{:S(2)}, u32[]{:S(2)}) collective-permute-start(bf16[512,384]{1,0:T(8,128)(2,1)} %pad_maximum_fusion), channel_id=1, source_target_pairs={{0,64},{64,0},{1,65},{65,1},{2,66},{66,2},{3,67},{67,3},{4,68},{68... | collective-permute-start | bytes 1179656 | tf_op jit(solution)/shard_map/ppermute | solution.py:25
  87.1 26.5 %collective-permute-done.2 = bf16[256,384]{1,0:T(8,128)(2,1)S(1)} collective-permute-done((bf16[256,384]{1,0:T(8,128)(2,1)S(1)}, bf16[256,384]{1,0:T(8,128)(2,1)S(1)}, u32[]{:S(2)}, u32[]{:S(2)}) %collective-permute-start.2) | collective-permute-done | bytes 196640 | tf_op jit(solution)/shard_map/ppermute | solution.py:25
  113.6 1.9 collective-permute-start.3
  115.6 0.0 collective-permute-done.4
  115.6 0.1 select_bitcast_fusion
  115.7 0.1 pad_maximum_fusion.2
  115.8 1.7 temporal.1
  117.5 0.0 all-to-all-done.q_ref
  117.5 6.0 %all-to-all-start.3 = ((bf16[8,32,384]{2,1,0:T(8,128)(2,1)}), bf16[8,32,384]{2,1,0:T(8,128)(2,1)S(1)}, u32[]{:S(2)}, u32[]{:S(2)}) async-start(bf16[8,32,384]{2,1,0:T(8,128)(2,1)} %bitcast.19), calls=%async_computation.3 | async-start | bytes 393216 | tf_op jit(solution)/shard_map/all_to_all | solution.py:206
  123.5 3.0 %collective-permute-done = bf16[512,384]{1,0:T(8,128)(2,1)S(1)} collective-permute-done((bf16[512,384]{1,0:T(8,128)(2,1)}, bf16[512,384]{1,0:T(8,128)(2,1)S(1)}, u32[]{:S(2)}, u32[]{:S(2)}) %collective-permute-start) | collective-permute-done | bytes 393248 | tf_op jit(solution)/shard_map/ppermute | solution.py:25
  126.6 0.0 collective-permute-done.3.sb_ref
  126.6 6.1 %spatial.1 = bf16[4,432,256]{2,1,0:T(8,128)(2,1)S(1)} custom-call(s32[3]{0:T(128)S(1)} %copy-done.3, bf16[4,256,384]{2,1,0:T(8,128)(2,1)S(1)} %all-to-all-done.q_ref, bf16[256,384]{1,0:T(8,128)(2,1)S(1)} %copy-done, bf16[256,384]{1,0:T(8,128)(2,1)S(1)} %copy-done.1, bf16[256,384]{1,0:T(8,128)(2,1)S(1)} %get-tuple-element.11.ko_ref, ...), custom_call_target="tpu_custom_call" | custom-call | tf_op jit(solution)/shard_map/spatial/pallas_call | solution.py:64
  132.7 0.0 all-to-all-done.3
  132.7 30.4 %all_to_all.31.part_ref = bf16[4,432,256]{2,1,0:T(8,128)(2,1)S(1)} all-to-all(bf16[4,432,256]{2,1,0:T(8,128)(2,1)S(1)} %spatial.1), channel_id=1, replica_groups=mesh['a'=4,'b'=2,'z'=4,'c'=2,'w'=2,'x'=4] {'a'}, dimensions={0} | all-to-all | bytes 1769472 | tf_op jit(solution)/shard_map/all_to_all | solution.py:212
  163.1 0.9 combine.1
  163.9 1.0 broadcast_in_dim.42
  164.9 7.1 %all-to-all-start.4 = ((bf16[4,256,384]{2,1,0:T(8,128)(2,1)}), bf16[4,256,384]{2,1,0:T(8,128)(2,1)S(1)}, u32[]{:S(2)}, u32[]{:S(2)}) async-start(bf16[4,256,384]{2,1,0:T(8,128)(2,1)} %broadcast_in_dim.42), calls=%async_computation.4 | async-start | bytes 1572864 | tf_op jit(solution)/shard_map/all_to_all | solution.py:165
  172.0 3.5 %collective-permute-start.5 = (bf16[256,384]{1,0:T(8,128)(2,1)S(1)}, bf16[256,384]{1,0:T(8,128)(2,1)S(1)}, u32[]{:S(2)}, u32[]{:S(2)}) collective-permute-start(bf16[256,384]{1,0:T(8,128)(2,1)S(1)} %combine.1), channel_id=1, source_target_pairs={{0,4},{4,0},{1,5},{5,1},{2,6},{6,2},{3,7},{7,3},{8,12},{12,8},{9,1... | collective-permute-start | bytes 589832 | tf_op jit(solution)/shard_map/ppermute | solution.py:25
  175.5 11.7 %collective-permute-done.5 = bf16[256,384]{1,0:T(8,128)(2,1)S(1)} collective-permute-done((bf16[256,384]{1,0:T(8,128)(2,1)S(1)}, bf16[256,384]{1,0:T(8,128)(2,1)S(1)}, u32[]{:S(2)}, u32[]{:S(2)}) %collective-permute-start.5) | collective-permute-done | bytes 196640 | tf_op jit(solution)/shard_map/ppermute | solution.py:25
  187.2 0.0 all-to-all-done.4.own_ref
  187.2 1.0 broadcast_in_dim.43
  188.2 4.5 %all-to-all-start.5 = ((bf16[4,256,384]{2,1,0:T(8,128)(2,1)}), bf16[4,256,384]{2,1,0:T(8,128)(2,1)S(1)}, u32[]{:S(2)}, u32[]{:S(2)}) async-start(bf16[4,256,384]{2,1,0:T(8,128)(2,1)} %broadcast_in_dim.43), calls=%async_computation.5 | async-start | bytes 1572864 | tf_op jit(solution)/shard_map/all_to_all | solution.py:165
  192.7 10.9 %all-to-all-done.5.other_ref = bf16[4,256,384]{2,1,0:T(8,128)(2,1)S(1)} async-done(((bf16[4,256,384]{2,1,0:T(8,128)(2,1)}), bf16[4,256,384]{2,1,0:T(8,128)(2,1)S(1)}, u32[]{:S(2)}, u32[]{:S(2)}) %all-to-all-start.5) | async-done | bytes 786464 | tf_op jit(solution)/shard_map/all_to_all | solution.py:165
  203.6 2.1 copy-done.2
  205.7 2.6 %project.1 = bf16[256,640]{1,0:T(8,128)(2,1)} custom-call(s32[1]{0:T(128)} %bitcast.w_ref, bf16[4,256,384]{2,1,0:T(8,128)(2,1)S(1)} %all-to-all-done.4.own_ref, bf16[4,256,384]{2,1,0:T(8,128)(2,1)S(1)} %all-to-all-done.5.other_ref, bf16[8,640,384]{2,1,0:T(8,128)(2,1)S(1)} %bitcast.56), custom_call_target="tpu_custom_call" | custom-call | tf_op jit(solution)/shard_map/project/pallas_call | solution.py:153
  (14 shorter events, 0.3 us)
Async XLA Ops:
  6.5 26.5 %copy-start = (bf16[256,384]{1,0:T(8,128)(2,1)S(1)}, bf16[256,384]{1,0:T(8,128)(2,1)}, u32[]{:S(2)}) copy-start(bf16[256,384]{1,0:T(8,128)(2,1)} %k_ref.1) | copy-start | bytes 589828
  6.5 26.5 %copy-start.1 = (bf16[256,384]{1,0:T(8,128)(2,1)S(1)}, bf16[256,384]{1,0:T(8,128)(2,1)}, u32[]{:S(2)}) copy-start(bf16[256,384]{1,0:T(8,128)(2,1)} %v_ref.1) | copy-start | bytes 589828
  6.5 26.2 %copy-start.3 = (s32[3]{0:T(128)S(1)}, s32[3]{0:T(128)}, u32[]{:S(2)}) copy-start(s32[3]{0:T(128)} %hc_ref.5) | copy-start | bytes 40
  6.5 26.6 %copy-start.4 = (bf16[256,384]{1,0:T(8,128)(2,1)S(1)}, bf16[256,384]{1,0:T(8,128)(2,1)}, u32[]{:S(2)}) copy-start(bf16[256,384]{1,0:T(8,128)(2,1)} %param.6) | copy-start | bytes 589828
  6.5 197.0 %all-gather.3.cloned.1.call-start = ((), (), s32[]{:S(2)}) async-start(), calls=%async_computation.6 | async-start | bytes 4423680 | tf_op jit(solution)/shard_map/all_gather | solution.py:178
  6.6 7.4 %collective-permute-start.6 = (bf16[80,384]{1,0:T(8,128)(2,1)}, bf16[80,384]{1,0:T(8,128)(2,1)S(1)}, u32[]{:S(2)}, u32[]{:S(2)}) collective-permute-start(bf16[80,384]{1,0:T(8,128)(2,1)} %bitcast.64), channel_id=1, source_target_pairs={{0,0},{1,64},{2,128},{3,192},{4,256},{5,320},{6,384},{7,448},{64,1... | collective-permute-start | bytes 184328 | tf_op jit(solution)/shard_map/ppermute | solution.py:174
  29.7 3.3 %collective-permute-start.1 = (bf16[256,384]{1,0:T(8,128)(2,1)S(1)}, bf16[256,384]{1,0:T(8,128)(2,1)S(1)}, u32[]{:S(2)}, u32[]{:S(2)}) collective-permute-start(bf16[256,384]{1,0:T(8,128)(2,1)S(1)} %broadcast_select_fusion), channel_id=1, source_target_pairs={{0,8},{8,0},{1,9},{9,1},{2,10},{10,2},{3,11},{11,3},{4,12},{12,4},... | collective-permute-start | bytes 589832 | tf_op jit(solution)/shard_map/ppermute | solution.py:25
  59.0 58.5 %all-to-all-start = ((bf16[4,256,384]{2,1,0:T(8,128)(2,1)}), bf16[4,256,384]{2,1,0:T(8,128)(2,1)S(1)}, u32[]{:S(2)}, u32[]{:S(2)}) async-start(bf16[4,256,384]{2,1,0:T(8,128)(2,1)} %broadcast_in_dim.22), calls=%async_computation | async-start | bytes 1572864 | tf_op jit(solution)/shard_map/all_to_all | solution.py:165
  78.5 35.1 %collective-permute-start.2 = (bf16[256,384]{1,0:T(8,128)(2,1)S(1)}, bf16[256,384]{1,0:T(8,128)(2,1)S(1)}, u32[]{:S(2)}, u32[]{:S(2)}) collective-permute-start(bf16[256,384]{1,0:T(8,128)(2,1)S(1)} %dynamic-slice_bitcast_fusion), channel_id=1, source_target_pairs={{0,64},{64,0},{1,65},{65,1},{2,66},{66,2},{3,67},{67,3},{4,68},{68... | collective-permute-start | bytes 589832 | tf_op jit(solution)/shard_map/ppermute | solution.py:25
  80.4 35.1 %collective-permute-start.4 = (bf16[4,3,32,384]{3,2,1,0:T(8,128)(2,1)S(1)}, bf16[4,3,32,384]{3,2,1,0:T(8,128)(2,1)S(1)}, u32[]{:S(2)}, u32[]{:S(2)}) collective-permute-start(bf16[4,3,32,384]{3,2,1,0:T(8,128)(2,1)S(1)} %fusion), channel_id=1, source_target_pairs={{0,8},{8,0},{1,9},{9,1},{2,10},{10,2},{3,11},{11,3},{4,12},{12,4},... | collective-permute-start | bytes 884744 | tf_op jit(solution)/shard_map/ppermute | solution.py:25
  83.2 43.3 %collective-permute-start = (bf16[512,384]{1,0:T(8,128)(2,1)}, bf16[512,384]{1,0:T(8,128)(2,1)S(1)}, u32[]{:S(2)}, u32[]{:S(2)}) collective-permute-start(bf16[512,384]{1,0:T(8,128)(2,1)} %pad_maximum_fusion), channel_id=1, source_target_pairs={{0,64},{64,0},{1,65},{65,1},{2,66},{66,2},{3,67},{67,3},{4,68},{68... | collective-permute-start | bytes 1179656 | tf_op jit(solution)/shard_map/ppermute | solution.py:25
  113.6 12.9 %collective-permute-start.3 = (bf16[512,384]{1,0:T(8,128)(2,1)S(1)}, bf16[512,384]{1,0:T(8,128)(2,1)S(1)}, u32[]{:S(2)}, u32[]{:S(2)}) collective-permute-start(bf16[512,384]{1,0:T(8,128)(2,1)S(1)} %pad_maximum_fusion.1.sa_ref), channel_id=1, source_target_pairs={{0,8},{8,0},{1,9},{9,1},{2,10},{10,2},{3,11},{11,3},{4,12},{12,4},... | collective-permute-start | bytes 1179656 | tf_op jit(solution)/shard_map/ppermute | solution.py:25
  117.5 15.2 %all-to-all-start.3 = ((bf16[8,32,384]{2,1,0:T(8,128)(2,1)}), bf16[8,32,384]{2,1,0:T(8,128)(2,1)S(1)}, u32[]{:S(2)}, u32[]{:S(2)}) async-start(bf16[8,32,384]{2,1,0:T(8,128)(2,1)} %bitcast.19), calls=%async_computation.3 | async-start | bytes 393216 | tf_op jit(solution)/shard_map/all_to_all | solution.py:206
  164.9 22.3 %all-to-all-start.4 = ((bf16[4,256,384]{2,1,0:T(8,128)(2,1)}), bf16[4,256,384]{2,1,0:T(8,128)(2,1)S(1)}, u32[]{:S(2)}, u32[]{:S(2)}) async-start(bf16[4,256,384]{2,1,0:T(8,128)(2,1)} %broadcast_in_dim.42), calls=%async_computation.4 | async-start | bytes 1572864 | tf_op jit(solution)/shard_map/all_to_all | solution.py:165
  172.0 15.2 %collective-permute-start.5 = (bf16[256,384]{1,0:T(8,128)(2,1)S(1)}, bf16[256,384]{1,0:T(8,128)(2,1)S(1)}, u32[]{:S(2)}, u32[]{:S(2)}) collective-permute-start(bf16[256,384]{1,0:T(8,128)(2,1)S(1)} %combine.1), channel_id=1, source_target_pairs={{0,4},{4,0},{1,5},{5,1},{2,6},{6,2},{3,7},{7,3},{8,12},{12,8},{9,1... | collective-permute-start | bytes 589832 | tf_op jit(solution)/shard_map/ppermute | solution.py:25
  188.2 15.4 %all-to-all-start.5 = ((bf16[4,256,384]{2,1,0:T(8,128)(2,1)}), bf16[4,256,384]{2,1,0:T(8,128)(2,1)S(1)}, u32[]{:S(2)}, u32[]{:S(2)}) async-start(bf16[4,256,384]{2,1,0:T(8,128)(2,1)} %broadcast_in_dim.43), calls=%async_computation.5 | async-start | bytes 1572864 | tf_op jit(solution)/shard_map/all_to_all | solution.py:165
  203.6 2.1 copy-start.2
Sparse Core Ops, SparseCore 0:
  28.9 96.0 all-gather.2

commit v2 on v1

v2 whole, which is shorter than its diff:
```python
import functools

import jax
import jax.numpy as jnp
from jax import lax
from jax.experimental import pallas as pl
from jax.experimental.pallas import tpu as pltpu
from jax.sharding import Mesh, PartitionSpec as P

HD = 128
NH = 3
TILE = 4
LOG2E = 1.4426950408889634
SCALE2 = HD**-0.5 * LOG2E
NT = (((1,), (1,)), ((), ()))
TN = (((0,), (0,)), ((), ()))
NN = (((1,), (0,)), ((), ()))


def dot(a, b, dims):
    return lax.dot_general(a, b, dims, preferred_element_type=jnp.float32)


def swap(x, axis):
    return lax.ppermute(x, axis, [(0, 1), (1, 0)])


def spatial_kernel(hc_ref, core_ref, at_ref, k_ref, v_ref, okv_ref, sa_ref, sb_ref, q_ref, *rest):
    count = len(rest) - 1
    out_refs, stats_ref = rest[:count], rest[-1]
    rows = k_ref.shape[0]
    first = core_ref[0] == 0
    for h in range(NH):
        cols = slice(h * HD, (h + 1) * HD)

        @pl.when(hc_ref[h] == 0)
        def _():
            mine, other = sa_ref[:, cols], sb_ref[:, cols]
            sk = jnp.where(first, mine, other)
            sv = jnp.where(first, other, mine)
            keys = jnp.concatenate([k_ref[:, cols], okv_ref[:rows, cols], sk], axis=0)
            vals = jnp.concatenate([v_ref[:, cols], okv_ref[rows:, cols], sv], axis=0)
            for i in range(count):
                at = at_ref[i] if q_ref.shape[0] > 1 else 0
                s = dot(keys, q_ref[at, :rows, cols], NT) * SCALE2
                m = jnp.max(s, axis=0, keepdims=True)
                w = jnp.exp2(s - m)
                total = jnp.sum(w, axis=0, keepdims=True)
                o = dot(vals, w.astype(jnp.bfloat16), TN)
                out_refs[i][cols, :] = (o / total).astype(jnp.bfloat16)
                lse = m + jnp.log2(total)
                hi = lse.astype(jnp.bfloat16).astype(jnp.float32)
                mid = (lse - hi).astype(jnp.bfloat16).astype(jnp.float32)
                stats_ref[i, 3 * h : 3 * h + 1, :] = hi
                stats_ref[i, 3 * h + 1 : 3 * h + 2, :] = mid
                stats_ref[i, 3 * h + 2 : 3 * h + 3, :] = lse - hi - mid

    for i in range(count):
        out_refs[i][NH * HD :, :] = stats_ref[i].astype(jnp.bfloat16)


def spatial(hc, core, at, k, v, okv, sa, sb, queries, after=()):
    rows, width = k.shape
    smem = pl.BlockSpec(memory_space=pltpu.SMEM)
    vmem = pl.BlockSpec(memory_space=pltpu.VMEM)
    count = at.shape[0]
    shape = jax.ShapeDtypeStruct((width + 16, rows), jnp.bfloat16)

    def body(*refs):
        spatial_kernel(*refs[:9], *refs[9 + len(after) :])

    return pl.pallas_call(
        body,
        out_shape=[shape] * count,
        in_specs=[smem] * 3 + [vmem] * 6 + [pl.BlockSpec(memory_space=pl.ANY)] * len(after),
        out_specs=[vmem] * count,
        scratch_shapes=[pltpu.VMEM((count, 16, rows), jnp.float32)],
        compiler_params=pltpu.CompilerParams(vmem_limit_bytes=16 * 1024 * 1024),
        name="spatial",
    )(hc, core, at, k, v, okv, sa, sb, queries, *after)


def temporal_kernel(hc_ref, q_ref, k_ref, v_ref, out_ref):
    rows = q_ref.shape[0]
    span = rows // 8
    for h in range(NH):
        cols = slice(h * HD, (h + 1) * HD)

        @pl.when(hc_ref[h] == 1)
        def _():
            s = dot(q_ref[:, cols], k_ref[:, cols], NT) * SCALE2
            i = lax.broadcasted_iota(jnp.int32, (rows, rows), 0)
            j = lax.broadcasted_iota(jnp.int32, (rows, rows), 1)
            s = jnp.where((i % span) // TILE == (j % span) // TILE, s, -jnp.inf)
            w = jnp.exp2(s - jnp.max(s, axis=1, keepdims=True))
            total = jnp.sum(w, axis=1, keepdims=True)
            o = dot(w.astype(jnp.bfloat16), v_ref[:, cols], NN)
            out_ref[:, cols] = (o / total).astype(jnp.bfloat16)


def temporal(hc, q, k, v):
    smem = pl.BlockSpec(memory_space=pltpu.SMEM)
    vmem = pl.BlockSpec(memory_space=pltpu.VMEM)
    return pl.pallas_call(
        temporal_kernel,
        out_shape=jax.ShapeDtypeStruct(q.shape, jnp.bfloat16),
        in_specs=[smem] + [vmem] * 3,
        out_specs=vmem,
        compiler_params=pltpu.CompilerParams(vmem_limit_bytes=16 * 1024 * 1024),
        name="temporal",
    )(hc, q, k, v)


def combine_kernel(hc_ref, p0_ref, p1_ref, p2_ref, p3_ref, back_ref, out_ref):
    parts = (p0_ref, p1_ref, p2_ref, p3_ref)
    stats = [p[NH * HD :, :].astype(jnp.float32) for p in parts]
    for h in range(NH):
        cols = slice(h * HD, (h + 1) * HD)

        @pl.when(hc_ref[h] == 0)
        def _():
            lses = [st[3 * h : 3 * h + 1] + st[3 * h + 1 : 3 * h + 2] + st[3 * h + 2 : 3 * h + 3] for st in stats]
            m = functools.reduce(jnp.maximum, lses)
            es = [jnp.exp2(l - m) for l in lses]
            inv = 1.0 / sum(es)
            o = sum(p[cols, :].astype(jnp.float32) * (e * inv) for p, e in zip(parts, es))
            out_ref[:, cols] = o.T.astype(jnp.bfloat16)

        @pl.when(hc_ref[h] != 0)
        def _():
            out_ref[:, cols] = back_ref[:, cols]


def combine(hc, parts, back):
    smem = pl.BlockSpec(memory_space=pltpu.SMEM)
    vmem = pl.BlockSpec(memory_space=pltpu.VMEM)
    return pl.pallas_call(
        combine_kernel,
        out_shape=jax.ShapeDtypeStruct(back.shape, jnp.bfloat16),
        in_specs=[smem] + [vmem] * 5,
        out_specs=vmem,
        compiler_params=pltpu.CompilerParams(vmem_limit_bytes=16 * 1024 * 1024),
        name="combine",
    )(hc, *parts, back)


def project_kernel(group_ref, a0_ref, a1_ref, a2_ref, a3_ref, weight_ref, *rest):
    total = rest[0][...] if len(rest) == 2 else None
    for i, ref in enumerate((a0_ref, a1_ref, a2_ref, a3_ref)):
        rows = jnp.concatenate([weight_ref[j, group_ref[i]] for j in range(weight_ref.shape[0])], axis=0)
        term = dot(ref[...], rows, NT)
        total = term if total is None else total + term
    rest[-1][...] = total.astype(rest[-1].dtype)


def project(groups, attended, weight, begin=None):
    rows, columns = attended[0].shape[0], weight.shape[0] * weight.shape[2]
    smem = pl.BlockSpec(memory_space=pltpu.SMEM)
    vmem = pl.BlockSpec(memory_space=pltpu.VMEM)
    inputs = [*attended, weight] + ([] if begin is None else [begin])
    return pl.pallas_call(
        project_kernel,
        out_shape=jax.ShapeDtypeStruct((rows, columns), jnp.float32 if begin is None else jnp.bfloat16),
        in_specs=[smem] + [vmem] * len(inputs),
        out_specs=vmem,
        compiler_params=pltpu.CompilerParams(vmem_limit_bytes=16 * 1024 * 1024),
        name="project",
    )(groups, *inputs)


def shifted(x, axis, by):
    n = lax.axis_size(axis)
    return lax.ppermute(x, axis, [(i, (i + by) % n) for i in range(n)])


def mirrored(x, by, back=False):
    pairs = [(y, (y + (by if y % 2 == 0 else -by)) % 8) for y in range(8)]
    return lax.ppermute(x, ("a", "b"), [(d, s) for s, d in pairs] if back else pairs)


def after(x, *others):
    return lax.optimization_barrier((x,) + others)[0]


def per_device(query, key_proj, value, head_class, sink_frame, out_weight):
    rows, width = query.shape
    core = lax.axis_index("c")
    sink = sink_frame[0]
    is_temporal = jnp.repeat(head_class == 1, HD)

    carried = jnp.where(core == 0, key_proj, value)
    given = swap(jnp.where(core == 0, value, key_proj), "c")
    candidate = jnp.where(sink % 2 == core, carried, given)
    pieces = [x.reshape(4, rows // 4, width) for x in (query, key_proj, value)]
    pieces = jnp.concatenate(pieces + [jnp.zeros_like(pieces[0])], axis=1)
    sent = jnp.where(is_temporal, pieces, candidate[None])
    got = lax.all_to_all(sent, "z", 0, 0, tiled=True)

    other_kv = swap(jnp.concatenate([key_proj, value], axis=0), "b")
    moves = (-3, 2, -1)
    y = 2 * lax.axis_index("a") + lax.axis_index("b")
    side = jnp.where(y % 2 == 0, -1, 1)
    chosen = jnp.stack([(y + side * abs(by)) % 8 for by in moves] + [y])

    turned = lax.ppermute(
        out_weight.T, ("a", "b", "w", "x"), [(y * 8 + h, h * 8 + y) for y in range(8) for h in range(8)]
    )
    early, other_kv = lax.optimization_barrier((query, other_kv))
    gathered = lax.all_gather(jnp.concatenate([early, turned], axis=0), ("a", "b"), axis=0)

    sink_part = lax.dynamic_index_in_dim(got, sink // 2, 0, keepdims=False)
    sink_pair = jnp.concatenate([sink_part, swap(sink_part, "b")], axis=0)
    sink_other = swap(sink_pair, "c")

    half = rows // 8
    tokens = got.reshape(4, 4, 2, half, width)[:, :3]
    keep = jnp.where(core == 0, tokens[:, :, 0], tokens[:, :, 1])
    give = jnp.where(core == 0, tokens[:, :, 1], tokens[:, :, 0])
    come = swap(give, "c")
    first = jnp.where(core == 0, keep, come)
    second = jnp.where(core == 0, come, keep)
    both = jnp.stack([first, second], axis=1)
    tq, tk, tv = (both[:, :, i].reshape(rows, width) for i in range(3))
    back = temporal(head_class, tq, tk, tv)
    gathered, back = lax.optimization_barrier((gathered, sink_other, back))[::2]
    weight = lax.all_gather(gathered[:, rows:], ("z", "c"), axis=0)
    back = lax.all_to_all(back.reshape(8, half, width), ("z", "c"), 0, 0, tiled=True).reshape(rows, width)

    keys = (key_proj, value, other_kv, sink_pair, sink_other)
    away = spatial(head_class, core.reshape(1), chosen[:3], *keys, gathered)
    (here,) = spatial(head_class, core.reshape(1), chosen[3:], *keys, query[None], after=away[:1])
    parts = [mirrored(x, by, back=True) for x, by in zip(away, moves)]
    attended = combine(head_class, [*parts, here], back)

    other = swap(attended, "w")
    x, w = lax.axis_index("x"), lax.axis_index("w")
    own_all = [attended] + [shifted(attended, "x", by) for by in (1, 2, 3)]
    other_all = [other] + [shifted(other, "x", by) for by in (1, 2, 3)]
    groups = (x - jnp.arange(4)) % 4
    begin = project(groups + 4 * w, own_all, weight)
    return project(groups + 4 * (1 - w), other_all, weight, begin)


def solution(mesh):
    fine = Mesh(mesh.devices.reshape(4, 2, 4, 2, 2, 4), ("a", "b", "z", "c", "w", "x"))
    seq, head = ("a", "b", "z", "c"), ("w", "x")
    in_specs = (P(seq, head), P(seq, head), P(seq, head), P(head), P(), P(head, seq))
    return jax.shard_map(per_device, mesh=fine, in_specs=in_specs, out_specs=P(seq, head), check_vma=False)
```

time: 216 us -> 168 us (0.78)
  the two profiles are of different devices: /device:TPU:136 before, /device:TPU:72 now
where the time goes in v2:
time: 168 us; the launch traced here: 167 us
  waiting for transfers between devices  66.4 us (40%)
  starting transfers between devices  65.8 us (39%)
  between operations  14.4 us (9%)
  Pallas kernels  10.6 us (6%)
  local copies, waits for them, and re-layouts  5.82 us (3%)
  other arithmetic  4.29 us (3%)
    ppermute x6, waiting for transfers between devices, swap(): return lax.ppermute(x, axis, [(0, 1), (1, 0)])  21 us
    ppermute x6, starting transfers between devices, shifted(): return lax.ppermute(x, axis, [(i, (i + by) % n) for i in range(n)])  18.8 us
    ppermute x6, starting transfers between devices, swap(): return lax.ppermute(x, axis, [(0, 1), (1, 0)])  18.3 us
    all_to_all x1, waiting for transfers between devices, per_device(): got = lax.all_to_all(sent, 'z', 0, 0, tiled=True)  17.1 us
    ppermute x3, waiting for transfers between devices, mirrored(): lax.ppermute(x, ('a', 'b'), [(d, s) for s, d in pairs] if back else pairs)  12 us
    ppermute x3, starting transfers between devices, mirrored(): lax.ppermute(x, ('a', 'b'), [(d, s) for s, d in pairs] if back else pairs)  11.9 us
    all_gather x1, waiting for transfers between devices, per_device(): lax.all_gather(jnp.concatenate([early, turned], axis=0), ('a', 'b'), axis=0)  9.76 us
    all_to_all x1, starting transfers between devices, per_device(): got = lax.all_to_all(sent, 'z', 0, 0, tiled=True)  6.91 us
  transfers between devices with their start and end apart: 20, of which 11 were waited for; matrix products, arithmetic and copies ran while one was open for 1% of the time, Pallas kernels for 5%

profile of v2, /device:TPU:72, one launch (start us, length us, event | category | flops | bytes accessed | tf_op | source)
XLA Modules:
  0.0 167.3 jit_solution(5387836258209958416)
XLA Ops:
  6.5 0.0 all-gather.5.cloned.1.call-start
  6.6 1.1 pad_maximum_fusion
  7.7 2.4 %collective-permute-start = (bf16[512,384]{1,0:T(8,128)(2,1)S(1)}, bf16[512,384]{1,0:T(8,128)(2,1)S(1)}, u32[]{:S(2)}, u32[]{:S(2)}) collective-permute-start(bf16[512,384]{1,0:T(8,128)(2,1)S(1)} %pad_maximum_fusion), channel_id=1, source_target_pairs={{0,64},{64,0},{1,65},{65,1},{2,66},{66,2},{3,67},{67,3},{4,68},{68... | collective-permute-start | bytes 1179656 | tf_op jit(solution)/shard_map/ppermute | solution.py:25
  10.1 4.4 %collective-permute-start.4 = (bf16[80,384]{1,0:T(8,128)(2,1)}, bf16[80,384]{1,0:T(8,128)(2,1)S(1)}, u32[]{:S(2)}, u32[]{:S(2)}) collective-permute-start(bf16[80,384]{1,0:T(8,128)(2,1)} %bitcast.55), channel_id=1, source_target_pairs={{0,0},{1,64},{2,128},{3,192},{4,256},{5,320},{6,384},{7,448},{64,1... | collective-permute-start | bytes 184328 | tf_op jit(solution)/shard_map/ppermute | solution.py:205
  14.5 6.6 %collective-permute-done.refs_5_ = bf16[512,384]{1,0:T(8,128)(2,1)S(1)} collective-permute-done((bf16[512,384]{1,0:T(8,128)(2,1)S(1)}, bf16[512,384]{1,0:T(8,128)(2,1)S(1)}, u32[]{:S(2)}, u32[]{:S(2)}) %collective-permute-start) | collective-permute-done | bytes 393248 | tf_op jit(solution)/shard_map/ppermute | solution.py:25
  21.1 1.9 %collective-permute-done.4 = bf16[80,384]{1,0:T(8,128)(2,1)S(1)} collective-permute-done((bf16[80,384]{1,0:T(8,128)(2,1)}, bf16[80,384]{1,0:T(8,128)(2,1)S(1)}, u32[]{:S(2)}, u32[]{:S(2)}) %collective-permute-start.4) | collective-permute-done | bytes 61472 | tf_op jit(solution)/shard_map/ppermute | solution.py:205
  23.0 1.6 pad_maximum_fusion.2
  24.7 1.9 %collective-permute-start.1 = (bf16[256,384]{1,0:T(8,128)(2,1)S(1)}, bf16[256,384]{1,0:T(8,128)(2,1)S(1)}, u32[]{:S(2)}, u32[]{:S(2)}) collective-permute-start(bf16[256,384]{1,0:T(8,128)(2,1)S(1)} %broadcast_select_fusion.1), channel_id=1, source_target_pairs={{0,8},{8,0},{1,9},{9,1},{2,10},{10,2},{3,11},{11,3},{4,12},{12,4},... | collective-permute-start | bytes 589832 | tf_op jit(solution)/shard_map/ppermute | solution.py:25
  27.3 0.1 pad.9.clone
  27.4 0.1 broadcast_bitcast_fusion
  27.5 0.6 collective-permute-done.1
  28.1 1.1 maximum_select_fusion
  29.2 6.9 %all-to-all-start = ((bf16[4,256,384]{2,1,0:T(8,128)(2,1)}), bf16[4,256,384]{2,1,0:T(8,128)(2,1)S(1)}, u32[]{:S(2)}, u32[]{:S(2)}) async-start(bf16[4,256,384]{2,1,0:T(8,128)(2,1)} %maximum_select_fusion), calls=%async_computation | async-start | bytes 1572864 | tf_op jit(solution)/shard_map/all_to_all | solution.py:197
  36.1 17.1 %all-to-all-done = bf16[4,256,384]{2,1,0:T(8,128)(2,1)S(1)} async-done(((bf16[4,256,384]{2,1,0:T(8,128)(2,1)}), bf16[4,256,384]{2,1,0:T(8,128)(2,1)S(1)}, u32[]{:S(2)}, u32[]{:S(2)}) %all-to-all-start) | async-done | bytes 786464 | tf_op jit(solution)/shard_map/all_to_all | solution.py:197
  53.3 2.5 %collective-permute-start.2 = (bf16[256,384]{1,0:T(8,128)(2,1)S(1)}, bf16[256,384]{1,0:T(8,128)(2,1)S(1)}, u32[]{:S(2)}, u32[]{:S(2)}) collective-permute-start(bf16[256,384]{1,0:T(8,128)(2,1)S(1)} %dynamic-slice_bitcast_fusion), channel_id=1, source_target_pairs={{0,64},{64,0},{1,65},{65,1},{2,66},{66,2},{3,67},{67,3},{4,68},{68... | collective-permute-start | bytes 589832 | tf_op jit(solution)/shard_map/ppermute | solution.py:25
  55.8 0.1 fusion.5
  55.9 1.9 %collective-permute-start.5 = (bf16[4,3,32,384]{3,2,0,1:T(8,128)(2,1)S(1)}, bf16[4,3,32,384]{3,2,0,1:T(8,128)(2,1)S(1)}, u32[]{:S(2)}, u32[]{:S(2)}) collective-permute-start(bf16[4,3,32,384]{3,2,0,1:T(8,128)(2,1)S(1)} %select_bitcast_fusion), channel_id=1, source_target_pairs={{0,8},{8,0},{1,9},{9,1},{2,10},{10,2},{3,11},{11,3},{4,12},{12,4},... | collective-permute-start | bytes 884744 | tf_op jit(solution)/shard_map/ppermute | solution.py:25
  57.8 8.5 %collective-permute-done.2 = bf16[256,384]{1,0:T(8,128)(2,1)S(1)} collective-permute-done((bf16[256,384]{1,0:T(8,128)(2,1)S(1)}, bf16[256,384]{1,0:T(8,128)(2,1)S(1)}, u32[]{:S(2)}, u32[]{:S(2)}) %collective-permute-start.2) | collective-permute-done | bytes 196640 | tf_op jit(solution)/shard_map/ppermute | solution.py:25
  66.4 1.9 %collective-permute-start.3 = (bf16[512,384]{1,0:T(8,128)(2,1)S(1)}, bf16[512,384]{1,0:T(8,128)(2,1)S(1)}, u32[]{:S(2)}, u32[]{:S(2)}) collective-permute-start(bf16[512,384]{1,0:T(8,128)(2,1)S(1)} %pad_maximum_fusion.1.refs_6_), channel_id=1, source_target_pairs={{0,8},{8,0},{1,9},{9,1},{2,10},{10,2},{3,11},{11,3},{4,12},{12,4},... | collective-permute-start | bytes 1179656 | tf_op jit(solution)/shard_map/ppermute | solution.py:25
  68.3 0.1 fusion.1
  68.4 0.1 pad_maximum_fusion.3
  68.5 2.1 %temporal.1 = bf16[256,384]{1,0:T(8,128)(2,1)} custom-call(s32[3]{0:T(128)S(1)} %copy-done.6, bf16[256,384]{1,0:T(8,128)(2,1)S(1)} %bitcast.51, bf16[256,384]{1,0:T(8,128)(2,1)S(1)} %bitcast.52, bf16[256,384]{1,0:T(8,128)(2,1)S(1)} %bitcast.50), custom_call_target="tpu_custom_call" | custom-call | tf_op jit(solution)/shard_map/temporal/pallas_call | solution.py:104
  70.6 9.8 %all-gather.5.cloned.1.call-done = bf16[2688,384]{1,0:T(8,128)(2,1)} async-done(((bf16[336,384]{1,0:T(8,128)(2,1)}), bf16[2688,384]{1,0:T(8,128)(2,1)}) %all-gather.5.cloned.1.call-update) | async-done | bytes 2064400 | tf_op jit(solution)/shard_map/all_gather | solution.py:209
  80.3 1.9 %slice.28 = bf16[8,80,384]{2,1,0:T(8,128)(2,1)} slice(bf16[8,336,384]{2,1,0:T(8,128)(2,1)} %bitcast.46), slice={[0:8], [256:336], [0:384]} | slice | bytes 983040 | tf_op jit(solution)/shard_map/slice | solution.py:226
  82.2 5.3 %all-to-all-start.1 = ((bf16[8,32,384]{2,1,0:T(8,128)(2,1)}), bf16[8,32,384]{2,1,0:T(8,128)(2,1)S(1)}, u32[]{:S(2)}, u32[]{:S(2)}) async-start(bf16[8,32,384]{2,1,0:T(8,128)(2,1)} %bitcast.23), calls=%async_computation.1 | async-start | bytes 393216 | tf_op jit(solution)/shard_map/all_to_all | solution.py:227
  87.6 0.1 pad_add_fusion.refs_2_
  87.7 1.6 copy-done.4
  89.2 2.6 %spatial.2 = (bf16[400,256]{1,0:T(8,128)(2,1)S(1)}, bf16[400,256]{1,0:T(8,128)(2,1)S(1)}, bf16[400,256]{1,0:T(8,128)(2,1)S(1)}) custom-call(s32[3]{0:T(128)S(1)} %copy-done.6, s32[1]{0:T(128)} %bitcast.refs_1_, s32[3]{0:T(128)S(1)} %pad_add_fusion.refs_2_, bf16[256,384]{1,0:T(8,128)(2,1)S(1)} %copy-done.2, bf16[256,384]{1,0:T(8,128)(2,1)S(1)} %copy-done.3, ...), custom_call_target="tpu_custom_call" | custom-call | tf_op jit(solution)/shard_map/spatial/pallas_call | solution.py:72
  91.9 4.1 %collective-permute-start.7 = (bf16[400,256]{1,0:T(8,128)(2,1)S(1)}, bf16[400,256]{1,0:T(8,128)(2,1)S(1)}, u32[]{:S(2)}, u32[]{:S(2)}) collective-permute-start(bf16[400,256]{1,0:T(8,128)(2,1)S(1)} %get-tuple-element.16), channel_id=1, source_target_pairs={{128,0},{448,64},{256,128},{64,192},{384,256},{192,320},{0,384},{3... | collective-permute-start | bytes 614408 | tf_op jit(solution)/shard_map/ppermute | solution.py:178
  96.0 2.1 %collective-permute-start.8 = (bf16[400,256]{1,0:T(8,128)(2,1)S(1)}, bf16[400,256]{1,0:T(8,128)(2,1)S(1)}, u32[]{:S(2)}, u32[]{:S(2)}) collective-permute-start(bf16[400,256]{1,0:T(8,128)(2,1)S(1)} %get-tuple-element.17), channel_id=1, source_target_pairs={{448,0},{128,64},{64,128},{256,192},{192,256},{384,320},{320,384},... | collective-permute-start | bytes 614408 | tf_op jit(solution)/shard_map/ppermute | solution.py:178
  98.1 5.7 %collective-permute-start.6 = (bf16[400,256]{1,0:T(8,128)(2,1)S(1)}, bf16[400,256]{1,0:T(8,128)(2,1)S(1)}, u32[]{:S(2)}, u32[]{:S(2)}) collective-permute-start(bf16[400,256]{1,0:T(8,128)(2,1)S(1)} %get-tuple-element.15.refs_9_), channel_id=1, source_target_pairs={{320,0},{256,64},{448,128},{384,192},{64,256},{0,320},{192,384},{1... | collective-permute-start | bytes 614408 | tf_op jit(solution)/shard_map/ppermute | solution.py:178
  103.9 1.3 spatial.3.p3_ref
  105.2 0.8 collective-permute-done.8.p2_ref
  106.0 11.1 %collective-permute-done.6.p0_ref = bf16[400,256]{1,0:T(8,128)(2,1)S(1)} collective-permute-done((bf16[400,256]{1,0:T(8,128)(2,1)S(1)}, bf16[400,256]{1,0:T(8,128)(2,1)S(1)}, u32[]{:S(2)}, u32[]{:S(2)}) %collective-permute-start.6) | collective-permute-done | bytes 204832 | tf_op jit(solution)/shard_map/ppermute | solution.py:178
  117.2 0.7 combine.1.a0_ref
  117.9 7.7 %collective-permute-start.9 = (bf16[256,384]{1,0:T(8,128)(2,1)S(1)}, bf16[256,384]{1,0:T(8,128)(2,1)S(1)}, u32[]{:S(2)}, u32[]{:S(2)}) collective-permute-start(bf16[256,384]{1,0:T(8,128)(2,1)S(1)} %combine.1.a0_ref), channel_id=1, source_target_pairs={{0,4},{4,0},{1,5},{5,1},{2,6},{6,2},{3,7},{7,3},{8,12},{12,8},{9,1... | collective-permute-start | bytes 589832 | tf_op jit(solution)/shard_map/ppermute | solution.py:25
  125.7 4.7 %collective-permute-start.15 = (bf16[256,384]{1,0:T(8,128)(2,1)S(1)}, bf16[256,384]{1,0:T(8,128)(2,1)S(1)}, u32[]{:S(2)}, u32[]{:S(2)}) collective-permute-start(bf16[256,384]{1,0:T(8,128)(2,1)S(1)} %combine.1.a0_ref), channel_id=1, source_target_pairs={{0,3},{1,0},{2,1},{3,2},{4,7},{5,4},{6,5},{7,6},{8,11},{9,8},{10,9... | collective-permute-start | bytes 589832 | tf_op jit(solution)/shard_map/ppermute | solution.py:173
  130.3 2.5 %collective-permute-start.14 = (bf16[256,384]{1,0:T(8,128)(2,1)S(1)}, bf16[256,384]{1,0:T(8,128)(2,1)S(1)}, u32[]{:S(2)}, u32[]{:S(2)}) collective-permute-start(bf16[256,384]{1,0:T(8,128)(2,1)S(1)} %combine.1.a0_ref), channel_id=1, source_target_pairs={{0,2},{1,3},{2,0},{3,1},{4,6},{5,7},{6,4},{7,5},{8,10},{9,11},{10,... | collective-permute-start | bytes 589832 | tf_op jit(solution)/shard_map/ppermute | solution.py:173
  132.9 2.2 %collective-permute-start.13 = (bf16[256,384]{1,0:T(8,128)(2,1)S(1)}, bf16[256,384]{1,0:T(8,128)(2,1)S(1)}, u32[]{:S(2)}, u32[]{:S(2)}) collective-permute-start(bf16[256,384]{1,0:T(8,128)(2,1)S(1)} %combine.1.a0_ref), channel_id=1, source_target_pairs={{0,1},{1,2},{2,3},{3,0},{4,5},{5,6},{6,7},{7,4},{8,9},{9,10},{10,1... | collective-permute-start | bytes 589832 | tf_op jit(solution)/shard_map/ppermute | solution.py:173
  135.0 5.3 %collective-permute-done.9.a0_ref = bf16[256,384]{1,0:T(8,128)(2,1)S(1)} collective-permute-done((bf16[256,384]{1,0:T(8,128)(2,1)S(1)}, bf16[256,384]{1,0:T(8,128)(2,1)S(1)}, u32[]{:S(2)}, u32[]{:S(2)}) %collective-permute-start.9) | collective-permute-done | bytes 196640 | tf_op jit(solution)/shard_map/ppermute | solution.py:25
  140.4 4.6 %collective-permute-start.12 = (bf16[256,384]{1,0:T(8,128)(2,1)S(1)}, bf16[256,384]{1,0:T(8,128)(2,1)S(1)}, u32[]{:S(2)}, u32[]{:S(2)}) collective-permute-start(bf16[256,384]{1,0:T(8,128)(2,1)S(1)} %collective-permute-done.9.a0_ref), channel_id=1, source_target_pairs={{0,3},{1,0},{2,1},{3,2},{4,7},{5,4},{6,5},{7,6},{8,11},{9,8},{10,9... | collective-permute-start | bytes 589832 | tf_op jit(solution)/shard_map/ppermute | solution.py:173
  145.0 2.6 %collective-permute-start.11 = (bf16[256,384]{1,0:T(8,128)(2,1)S(1)}, bf16[256,384]{1,0:T(8,128)(2,1)S(1)}, u32[]{:S(2)}, u32[]{:S(2)}) collective-permute-start(bf16[256,384]{1,0:T(8,128)(2,1)S(1)} %collective-permute-done.9.a0_ref), channel_id=1, source_target_pairs={{0,2},{1,3},{2,0},{3,1},{4,6},{5,7},{6,4},{7,5},{8,10},{9,11},{10,... | collective-permute-start | bytes 589832 | tf_op jit(solution)/shard_map/ppermute | solution.py:173
  147.6 2.2 %collective-permute-start.10 = (bf16[256,384]{1,0:T(8,128)(2,1)S(1)}, bf16[256,384]{1,0:T(8,128)(2,1)S(1)}, u32[]{:S(2)}, u32[]{:S(2)}) collective-permute-start(bf16[256,384]{1,0:T(8,128)(2,1)S(1)} %collective-permute-done.9.a0_ref), channel_id=1, source_target_pairs={{0,1},{1,2},{2,3},{3,0},{4,5},{5,6},{6,7},{7,4},{8,9},{9,10},{10,1... | collective-permute-start | bytes 589832 | tf_op jit(solution)/shard_map/ppermute | solution.py:173
  149.9 2.1 %copy-done = bf16[64,80,384]{2,1,0:T(8,128)(2,1)S(1)} copy-done((bf16[64,80,384]{2,1,0:T(8,128)(2,1)S(1)}, bf16[64,80,384]{2,1,0:T(8,128)(2,1)}, u32[]{:S(2)}) %copy-start) | copy-done | bytes 3932184
  152.0 1.6 project.2.rest_0_
  153.6 2.5 %collective-permute-done.11.a2_ref = bf16[256,384]{1,0:T(8,128)(2,1)S(1)} collective-permute-done((bf16[256,384]{1,0:T(8,128)(2,1)S(1)}, bf16[256,384]{1,0:T(8,128)(2,1)S(1)}, u32[]{:S(2)}, u32[]{:S(2)}) %collective-permute-start.11) | collective-permute-done | bytes 196640 | tf_op jit(solution)/shard_map/ppermute | solution.py:173
  156.1 2.1 %collective-permute-done.10.a1_ref = bf16[256,384]{1,0:T(8,128)(2,1)S(1)} collective-permute-done((bf16[256,384]{1,0:T(8,128)(2,1)S(1)}, bf16[256,384]{1,0:T(8,128)(2,1)S(1)}, u32[]{:S(2)}, u32[]{:S(2)}) %collective-permute-start.10) | collective-permute-done | bytes 196640 | tf_op jit(solution)/shard_map/ppermute | solution.py:173
  158.2 2.3 %project.3 = bf16[256,640]{1,0:T(8,128)(2,1)} custom-call(s32[4]{0:T(128)S(1)} %get-tuple-element.27.group_ref, bf16[256,384]{1,0:T(8,128)(2,1)S(1)} %collective-permute-done.9.a0_ref, bf16[256,384]{1,0:T(8,128)(2,1)S(1)} %collective-permute-done.10.a1_ref, bf16[256,384]{1,0:T(8,128)(2,1)S(1)} %collective-permute-done.11.a2_ref, ...), custom_call_target="tpu_custom_call" | custom-call | tf_op jit(solution)/shard_map/project/pallas_call | solution.py:161
  (32 shorter events, 0.3 us)
Async XLA Ops:
  6.5 18.1 %copy-start.3 = (bf16[256,384]{1,0:T(8,128)(2,1)S(1)}, bf16[256,384]{1,0:T(8,128)(2,1)}, u32[]{:S(2)}) copy-start(bf16[256,384]{1,0:T(8,128)(2,1)} %refs_4_.3) | copy-start | bytes 589828
  6.5 18.1 %copy-start.2 = (bf16[256,384]{1,0:T(8,128)(2,1)S(1)}, bf16[256,384]{1,0:T(8,128)(2,1)}, u32[]{:S(2)}) copy-start(bf16[256,384]{1,0:T(8,128)(2,1)} %refs_3_.3) | copy-start | bytes 589828
  6.5 21.6 %copy-start.5 = (bf16[256,384]{1,0:T(8,128)(2,1)S(1)}, bf16[256,384]{1,0:T(8,128)(2,1)}, u32[]{:S(2)}) copy-start(bf16[256,384]{1,0:T(8,128)(2,1)} %param.6) | copy-start | bytes 589828
  6.5 20.9 %copy-start.6 = (s32[3]{0:T(128)S(1)}, s32[3]{0:T(128)}, u32[]{:S(2)}) copy-start(s32[3]{0:T(128)} %hc_ref.3) | copy-start | bytes 40
  6.5 73.8 %all-gather.5.cloned.1.call-start = ((), (), s32[]{:S(2)}) async-start(), calls=%async_computation.2 | async-start | bytes 2322432 | tf_op jit(solution)/shard_map/all_gather | solution.py:209
  7.7 13.4 %collective-permute-start = (bf16[512,384]{1,0:T(8,128)(2,1)S(1)}, bf16[512,384]{1,0:T(8,128)(2,1)S(1)}, u32[]{:S(2)}, u32[]{:S(2)}) collective-permute-start(bf16[512,384]{1,0:T(8,128)(2,1)S(1)} %pad_maximum_fusion), channel_id=1, source_target_pairs={{0,64},{64,0},{1,65},{65,1},{2,66},{66,2},{3,67},{67,3},{4,68},{68... | collective-permute-start | bytes 1179656 | tf_op jit(solution)/shard_map/ppermute | solution.py:25
  10.1 12.9 %collective-permute-start.4 = (bf16[80,384]{1,0:T(8,128)(2,1)}, bf16[80,384]{1,0:T(8,128)(2,1)S(1)}, u32[]{:S(2)}, u32[]{:S(2)}) collective-permute-start(bf16[80,384]{1,0:T(8,128)(2,1)} %bitcast.55), channel_id=1, source_target_pairs={{0,0},{1,64},{2,128},{3,192},{4,256},{5,320},{6,384},{7,448},{64,1... | collective-permute-start | bytes 184328 | tf_op jit(solution)/shard_map/ppermute | solution.py:205
  24.7 3.3 %collective-permute-start.1 = (bf16[256,384]{1,0:T(8,128)(2,1)S(1)}, bf16[256,384]{1,0:T(8,128)(2,1)S(1)}, u32[]{:S(2)}, u32[]{:S(2)}) collective-permute-start(bf16[256,384]{1,0:T(8,128)(2,1)S(1)} %broadcast_select_fusion.1), channel_id=1, source_target_pairs={{0,8},{8,0},{1,9},{9,1},{2,10},{10,2},{3,11},{11,3},{4,12},{12,4},... | collective-permute-start | bytes 589832 | tf_op jit(solution)/shard_map/ppermute | solution.py:25
  29.2 24.0 %all-to-all-start = ((bf16[4,256,384]{2,1,0:T(8,128)(2,1)}), bf16[4,256,384]{2,1,0:T(8,128)(2,1)S(1)}, u32[]{:S(2)}, u32[]{:S(2)}) async-start(bf16[4,256,384]{2,1,0:T(8,128)(2,1)} %maximum_select_fusion), calls=%async_computation | async-start | bytes 1572864 | tf_op jit(solution)/shard_map/all_to_all | solution.py:197
  36.1 113.8 %all-gather.7.cloned.1.call-start = ((), (), s32[]{:S(2)}) async-start(), calls=%async_computation.3 | async-start | bytes 4423680 | tf_op jit(solution)/shard_map/all_gather | solution.py:226
  53.3 13.1 %collective-permute-start.2 = (bf16[256,384]{1,0:T(8,128)(2,1)S(1)}, bf16[256,384]{1,0:T(8,128)(2,1)S(1)}, u32[]{:S(2)}, u32[]{:S(2)}) collective-permute-start(bf16[256,384]{1,0:T(8,128)(2,1)S(1)} %dynamic-slice_bitcast_fusion), channel_id=1, source_target_pairs={{0,64},{64,0},{1,65},{65,1},{2,66},{66,2},{3,67},{67,3},{4,68},{68... | collective-permute-start | bytes 589832 | tf_op jit(solution)/shard_map/ppermute | solution.py:25
  55.9 12.4 %collective-permute-start.5 = (bf16[4,3,32,384]{3,2,0,1:T(8,128)(2,1)S(1)}, bf16[4,3,32,384]{3,2,0,1:T(8,128)(2,1)S(1)}, u32[]{:S(2)}, u32[]{:S(2)}) collective-permute-start(bf16[4,3,32,384]{3,2,0,1:T(8,128)(2,1)S(1)} %select_bitcast_fusion), channel_id=1, source_target_pairs={{0,8},{8,0},{1,9},{9,1},{2,10},{10,2},{3,11},{11,3},{4,12},{12,4},... | collective-permute-start | bytes 884744 | tf_op jit(solution)/shard_map/ppermute | solution.py:25
  66.4 4.2 %collective-permute-start.3 = (bf16[512,384]{1,0:T(8,128)(2,1)S(1)}, bf16[512,384]{1,0:T(8,128)(2,1)S(1)}, u32[]{:S(2)}, u32[]{:S(2)}) collective-permute-start(bf16[512,384]{1,0:T(8,128)(2,1)S(1)} %pad_maximum_fusion.1.refs_6_), channel_id=1, source_target_pairs={{0,8},{8,0},{1,9},{9,1},{2,10},{10,2},{3,11},{11,3},{4,12},{12,4},... | collective-permute-start | bytes 1179656 | tf_op jit(solution)/shard_map/ppermute | solution.py:25
  82.2 34.9 %all-to-all-start.1 = ((bf16[8,32,384]{2,1,0:T(8,128)(2,1)}), bf16[8,32,384]{2,1,0:T(8,128)(2,1)S(1)}, u32[]{:S(2)}, u32[]{:S(2)}) async-start(bf16[8,32,384]{2,1,0:T(8,128)(2,1)} %bitcast.23), calls=%async_computation.1 | async-start | bytes 393216 | tf_op jit(solution)/shard_map/all_to_all | solution.py:227
  87.7 1.6 copy-start.4
  91.9 13.3 %collective-permute-start.7 = (bf16[400,256]{1,0:T(8,128)(2,1)S(1)}, bf16[400,256]{1,0:T(8,128)(2,1)S(1)}, u32[]{:S(2)}, u32[]{:S(2)}) collective-permute-start(bf16[400,256]{1,0:T(8,128)(2,1)S(1)} %get-tuple-element.16), channel_id=1, source_target_pairs={{128,0},{448,64},{256,128},{64,192},{384,256},{192,320},{0,384},{3... | collective-permute-start | bytes 614408 | tf_op jit(solution)/shard_map/ppermute | solution.py:178
  96.0 10.1 %collective-permute-start.8 = (bf16[400,256]{1,0:T(8,128)(2,1)S(1)}, bf16[400,256]{1,0:T(8,128)(2,1)S(1)}, u32[]{:S(2)}, u32[]{:S(2)}) collective-permute-start(bf16[400,256]{1,0:T(8,128)(2,1)S(1)} %get-tuple-element.17), channel_id=1, source_target_pairs={{448,0},{128,64},{64,128},{256,192},{192,256},{384,320},{320,384},... | collective-permute-start | bytes 614408 | tf_op jit(solution)/shard_map/ppermute | solution.py:178
  98.1 19.1 %collective-permute-start.6 = (bf16[400,256]{1,0:T(8,128)(2,1)S(1)}, bf16[400,256]{1,0:T(8,128)(2,1)S(1)}, u32[]{:S(2)}, u32[]{:S(2)}) collective-permute-start(bf16[400,256]{1,0:T(8,128)(2,1)S(1)} %get-tuple-element.15.refs_9_), channel_id=1, source_target_pairs={{320,0},{256,64},{448,128},{384,192},{64,256},{0,320},{192,384},{1... | collective-permute-start | bytes 614408 | tf_op jit(solution)/shard_map/ppermute | solution.py:178
  117.9 22.5 %collective-permute-start.9 = (bf16[256,384]{1,0:T(8,128)(2,1)S(1)}, bf16[256,384]{1,0:T(8,128)(2,1)S(1)}, u32[]{:S(2)}, u32[]{:S(2)}) collective-permute-start(bf16[256,384]{1,0:T(8,128)(2,1)S(1)} %combine.1.a0_ref), channel_id=1, source_target_pairs={{0,4},{4,0},{1,5},{5,1},{2,6},{6,2},{3,7},{7,3},{8,12},{12,8},{9,1... | collective-permute-start | bytes 589832 | tf_op jit(solution)/shard_map/ppermute | solution.py:25
  125.7 21.9 %collective-permute-start.15 = (bf16[256,384]{1,0:T(8,128)(2,1)S(1)}, bf16[256,384]{1,0:T(8,128)(2,1)S(1)}, u32[]{:S(2)}, u32[]{:S(2)}) collective-permute-start(bf16[256,384]{1,0:T(8,128)(2,1)S(1)} %combine.1.a0_ref), channel_id=1, source_target_pairs={{0,3},{1,0},{2,1},{3,2},{4,7},{5,4},{6,5},{7,6},{8,11},{9,8},{10,9... | collective-permute-start | bytes 589832 | tf_op jit(solution)/shard_map/ppermute | solution.py:173
  130.3 19.5 %collective-permute-start.14 = (bf16[256,384]{1,0:T(8,128)(2,1)S(1)}, bf16[256,384]{1,0:T(8,128)(2,1)S(1)}, u32[]{:S(2)}, u32[]{:S(2)}) collective-permute-start(bf16[256,384]{1,0:T(8,128)(2,1)S(1)} %combine.1.a0_ref), channel_id=1, source_target_pairs={{0,2},{1,3},{2,0},{3,1},{4,6},{5,7},{6,4},{7,5},{8,10},{9,11},{10,... | collective-permute-start | bytes 589832 | tf_op jit(solution)/shard_map/ppermute | solution.py:173
  132.9 17.0 %collective-permute-start.13 = (bf16[256,384]{1,0:T(8,128)(2,1)S(1)}, bf16[256,384]{1,0:T(8,128)(2,1)S(1)}, u32[]{:S(2)}, u32[]{:S(2)}) collective-permute-start(bf16[256,384]{1,0:T(8,128)(2,1)S(1)} %combine.1.a0_ref), channel_id=1, source_target_pairs={{0,1},{1,2},{2,3},{3,0},{4,5},{5,6},{6,7},{7,4},{8,9},{9,10},{10,1... | collective-permute-start | bytes 589832 | tf_op jit(solution)/shard_map/ppermute | solution.py:173
  140.4 13.2 %collective-permute-start.12 = (bf16[256,384]{1,0:T(8,128)(2,1)S(1)}, bf16[256,384]{1,0:T(8,128)(2,1)S(1)}, u32[]{:S(2)}, u32[]{:S(2)}) collective-permute-start(bf16[256,384]{1,0:T(8,128)(2,1)S(1)} %collective-permute-done.9.a0_ref), channel_id=1, source_target_pairs={{0,3},{1,0},{2,1},{3,2},{4,7},{5,4},{6,5},{7,6},{8,11},{9,8},{10,9... | collective-permute-start | bytes 589832 | tf_op jit(solution)/shard_map/ppermute | solution.py:173
  145.0 11.1 %collective-permute-start.11 = (bf16[256,384]{1,0:T(8,128)(2,1)S(1)}, bf16[256,384]{1,0:T(8,128)(2,1)S(1)}, u32[]{:S(2)}, u32[]{:S(2)}) collective-permute-start(bf16[256,384]{1,0:T(8,128)(2,1)S(1)} %collective-permute-done.9.a0_ref), channel_id=1, source_target_pairs={{0,2},{1,3},{2,0},{3,1},{4,6},{5,7},{6,4},{7,5},{8,10},{9,11},{10,... | collective-permute-start | bytes 589832 | tf_op jit(solution)/shard_map/ppermute | solution.py:173
  147.6 10.5 %collective-permute-start.10 = (bf16[256,384]{1,0:T(8,128)(2,1)S(1)}, bf16[256,384]{1,0:T(8,128)(2,1)S(1)}, u32[]{:S(2)}, u32[]{:S(2)}) collective-permute-start(bf16[256,384]{1,0:T(8,128)(2,1)S(1)} %collective-permute-done.9.a0_ref), channel_id=1, source_target_pairs={{0,1},{1,2},{2,3},{3,0},{4,5},{5,6},{6,7},{7,4},{8,9},{9,10},{10,1... | collective-permute-start | bytes 589832 | tf_op jit(solution)/shard_map/ppermute | solution.py:173
  149.9 2.1 %copy-start = (bf16[64,80,384]{2,1,0:T(8,128)(2,1)S(1)}, bf16[64,80,384]{2,1,0:T(8,128)(2,1)}, u32[]{:S(2)}) copy-start(bf16[64,80,384]{2,1,0:T(8,128)(2,1)} %all-gather.7.cloned.1.call-done) | copy-start | bytes 11796484
  152.0 6.1 %copy-start.1 = (bf16[64,80,384]{2,1,0:T(8,128)(2,1)S(1)}, bf16[64,80,384]{2,1,0:T(8,128)(2,1)}, u32[]{:S(2)}) copy-start(bf16[64,80,384]{2,1,0:T(8,128)(2,1)} %all-gather.7.cloned.1.call-done) | copy-start | bytes 11796484
Sparse Core Ops, SparseCore 0:
  24.8 55.5 all-gather.4
  82.4 59.2 all-gather.6

commit v3 on v2

--- a/solution.py
+++ b/solution.py
@@ -25,9 +25,9 @@
     return lax.ppermute(x, axis, [(0, 1), (1, 0)])
 
 
-def spatial_kernel(hc_ref, core_ref, at_ref, k_ref, v_ref, okv_ref, sa_ref, sb_ref, q_ref, *rest):
-    count = len(rest) - 1
-    out_refs, stats_ref = rest[:count], rest[-1]
+def spatial_kernel(hc_ref, core_ref, k_ref, v_ref, okv_ref, sa_ref, sb_ref, *rest):
+    count = len(rest) // 2
+    q_refs, out_refs, stats_ref = rest[:count], rest[count:-1], rest[-1]
     rows = k_ref.shape[0]
     first = core_ref[0] == 0
     for h in range(NH):
@@ -41,8 +41,7 @@
             keys = jnp.concatenate([k_ref[:, cols], okv_ref[:rows, cols], sk], axis=0)
             vals = jnp.concatenate([v_ref[:, cols], okv_ref[rows:, cols], sv], axis=0)
             for i in range(count):
-                at = at_ref[i] if q_ref.shape[0] > 1 else 0
-                s = dot(keys, q_ref[at, :rows, cols], NT) * SCALE2
+                s = dot(keys, q_refs[i][:, cols], NT) * SCALE2
                 m = jnp.max(s, axis=0, keepdims=True)
                 w = jnp.exp2(s - m)
                 total = jnp.sum(w, axis=0, keepdims=True)
@@ -59,25 +58,25 @@
         out_refs[i][NH * HD :, :] = stats_ref[i].astype(jnp.bfloat16)
 
 
-def spatial(hc, core, at, k, v, okv, sa, sb, queries, after=()):
+def spatial(hc, core, k, v, okv, sa, sb, queries, after=()):
     rows, width = k.shape
     smem = pl.BlockSpec(memory_space=pltpu.SMEM)
     vmem = pl.BlockSpec(memory_space=pltpu.VMEM)
-    count = at.shape[0]
+    count = len(queries)
     shape = jax.ShapeDtypeStruct((width + 16, rows), jnp.bfloat16)
 
     def body(*refs):
-        spatial_kernel(*refs[:9], *refs[9 + len(after) :])
+        spatial_kernel(*refs[: 7 + count], *refs[7 + count + len(after) :])
 
     return pl.pallas_call(
         body,
         out_shape=[shape] * count,
-        in_specs=[smem] * 3 + [vmem] * 6 + [pl.BlockSpec(memory_space=pl.ANY)] * len(after),
+        in_specs=[smem] * 2 + [vmem] * (5 + count) + [pl.BlockSpec(memory_space=pl.ANY)] * len(after),
         out_specs=[vmem] * count,
         scratch_shapes=[pltpu.VMEM((count, 16, rows), jnp.float32)],
         compiler_params=pltpu.CompilerParams(vmem_limit_bytes=16 * 1024 * 1024),
         name="spatial",
-    )(hc, core, at, k, v, okv, sa, sb, queries, *after)
+    )(hc, core, k, v, okv, sa, sb, *queries, *after)
 
 
 def temporal_kernel(hc_ref, q_ref, k_ref, v_ref, out_ref):
@@ -144,28 +143,36 @@
     )(hc, *parts, back)
 
 
-def project_kernel(group_ref, a0_ref, a1_ref, a2_ref, a3_ref, weight_ref, *rest):
-    total = rest[0][...] if len(rest) == 2 else None
-    for i, ref in enumerate((a0_ref, a1_ref, a2_ref, a3_ref)):
-        rows = jnp.concatenate([weight_ref[j, group_ref[i]] for j in range(weight_ref.shape[0])], axis=0)
-        term = dot(ref[...], rows, NT)
+def project_kernel(at_ref, all_ref, low_ref, high_ref, *rest):
+    total = None
+    for i, (ref, j) in enumerate(((low_ref, 0), (low_ref, 1), (high_ref, 0), (high_ref, 1))):
+        rows = jnp.concatenate([ref[k, j] for k in range(ref.shape[0])], axis=0)
+        term = dot(all_ref[i], rows, NT)
         total = term if total is None else total + term
     rest[-1][...] = total.astype(rest[-1].dtype)
 
 
-def project(groups, attended, weight, begin=None):
-    rows, columns = attended[0].shape[0], weight.shape[0] * weight.shape[2]
-    smem = pl.BlockSpec(memory_space=pltpu.SMEM)
-    vmem = pl.BlockSpec(memory_space=pltpu.VMEM)
-    inputs = [*attended, weight] + ([] if begin is None else [begin])
+def project(at, attended, weight, dtype, after=()):
+    count, rows, width = attended.shape
+    columns = weight.shape[0] * weight.shape[2]
+    block = (weight.shape[0], 2) + weight.shape[2:]
     return pl.pallas_call(
         project_kernel,
-        out_shape=jax.ShapeDtypeStruct((rows, columns), jnp.float32 if begin is None else jnp.bfloat16),
-        in_specs=[smem] + [vmem] * len(inputs),
-        out_specs=vmem,
-        compiler_params=pltpu.CompilerParams(vmem_limit_bytes=16 * 1024 * 1024),
+        out_shape=jax.ShapeDtypeStruct((rows, columns), dtype),
+        grid_spec=pltpu.PrefetchScalarGridSpec(
+            num_scalar_prefetch=1,
+            grid=(1,),
+            in_specs=[
+                pl.BlockSpec((count, rows, width), lambda i, at: (0, 0, 0)),
+                pl.BlockSpec(block, lambda i, at: (0, at[0], 0, 0)),
+                pl.BlockSpec(block, lambda i, at: (0, at[1], 0, 0)),
+            ]
+            + [pl.BlockSpec(memory_space=pl.ANY)] * len(after),
+            out_specs=pl.BlockSpec((rows, columns), lambda i, at: (0, 0)),
+        ),
+        compiler_params=pltpu.CompilerParams(vmem_limit_bytes=50 * 1024 * 1024),
         name="project",
-    )(groups, *inputs)
+    )(at, attended, weight, weight, *after)
 
 
 def shifted(x, axis, by):
@@ -173,9 +180,8 @@
     return lax.ppermute(x, axis, [(i, (i + by) % n) for i in range(n)])
 
 
-def mirrored(x, by, back=False):
-    pairs = [(y, (y + (by if y % 2 == 0 else -by)) % 8) for y in range(8)]
-    return lax.ppermute(x, ("a", "b"), [(d, s) for s, d in pairs] if back else pairs)
+def mirrored(x, by):
+    return lax.ppermute(x, ("a", "b"), [(y, (y + (by if y % 2 == 0 else -by)) % 8) for y in range(8)])
 
 
 def after(x, *others):
@@ -188,29 +194,34 @@
     sink = sink_frame[0]
     is_temporal = jnp.repeat(head_class == 1, HD)
 
+    turned = lax.ppermute(
+        out_weight.T,
+        ("a", "b", "x"),
+        [((4 * u + v) * 4 + x, (4 * u + x) * 4 + v) for u in range(2) for v in range(4) for x in range(4)],
+    )
+    given = swap(jnp.where(core == 0, value, key_proj), "c")
     carried = jnp.where(core == 0, key_proj, value)
-    given = swap(jnp.where(core == 0, value, key_proj), "c")
     candidate = jnp.where(sink % 2 == core, carried, given)
     pieces = [x.reshape(4, rows // 4, width) for x in (query, key_proj, value)]
     pieces = jnp.concatenate(pieces + [jnp.zeros_like(pieces[0])], axis=1)
     sent = jnp.where(is_temporal, pieces, candidate[None])
+
+    sent, turned = lax.optimization_barrier((sent, turned))
     got = lax.all_to_all(sent, "z", 0, 0, tiled=True)
-
-    other_kv = swap(jnp.concatenate([key_proj, value], axis=0), "b")
-    moves = (-3, 2, -1)
-    y = 2 * lax.axis_index("a") + lax.axis_index("b")
-    side = jnp.where(y % 2 == 0, -1, 1)
-    chosen = jnp.stack([(y + side * abs(by)) % 8 for by in moves] + [y])
-
-    turned = lax.ppermute(
-        out_weight.T, ("a", "b", "w", "x"), [(y * 8 + h, h * 8 + y) for y in range(8) for h in range(8)]
-    )
-    early, other_kv = lax.optimization_barrier((query, other_kv))
-    gathered = lax.all_gather(jnp.concatenate([early, turned], axis=0), ("a", "b"), axis=0)
-
+    beside = swap(jnp.concatenate([key_proj, value, turned], axis=0), "b")
+    other_kv, beside = beside[: 2 * rows], beside[2 * rows :]
+    even = lax.axis_index("b") == 0
+    pair = [jnp.where(even, turned, beside), jnp.where(even, beside, turned)]
+    moves = (-3, 3, -1)
+    moving = jnp.concatenate([query] + pair, axis=0)
+    moved = [mirrored(moving, by) for by in moves]
+
+    got, moved = lax.optimization_barrier((got, moved))
+    queries = [x[:rows] for x in moved]
+    weight = jnp.concatenate(pair + [x[rows:] for x in moved], axis=0).reshape(8, *turned.shape)
+    weight = lax.all_gather(weight, ("z", "c"), axis=0)
     sink_part = lax.dynamic_index_in_dim(got, sink // 2, 0, keepdims=False)
     sink_pair = jnp.concatenate([sink_part, swap(sink_part, "b")], axis=0)
-    sink_other = swap(sink_pair, "c")
 
     half = rows // 8
     tokens = got.reshape(4, 4, 2, half, width)[:, :3]
@@ -222,23 +233,23 @@
     both = jnp.stack([first, second], axis=1)
     tq, tk, tv = (both[:, :, i].reshape(rows, width) for i in range(3))
     back = temporal(head_class, tq, tk, tv)
-    gathered, back = lax.optimization_barrier((gathered, sink_other, back))[::2]
-    weight = lax.all_gather(gathered[:, rows:], ("z", "c"), axis=0)
+    sink_pair, back = lax.optimization_barrier((sink_pair, back))
+    sink_other = swap(sink_pair, "c")
     back = lax.all_to_all(back.reshape(8, half, width), ("z", "c"), 0, 0, tiled=True).reshape(rows, width)
 
     keys = (key_proj, value, other_kv, sink_pair, sink_other)
-    away = spatial(head_class, core.reshape(1), chosen[:3], *keys, gathered)
-    (here,) = spatial(head_class, core.reshape(1), chosen[3:], *keys, query[None], after=away[:1])
-    parts = [mirrored(x, by, back=True) for x, by in zip(away, moves)]
+    away = spatial(head_class, core.reshape(1), *keys, queries)
+    (here,) = spatial(head_class, core.reshape(1), *keys, [query], after=away[:1])
+    parts = [mirrored(x, by) for x, by in zip(away, moves)]
     attended = combine(head_class, [*parts, here], back)
 
-    other = swap(attended, "w")
-    x, w = lax.axis_index("x"), lax.axis_index("w")
-    own_all = [attended] + [shifted(attended, "x", by) for by in (1, 2, 3)]
-    other_all = [other] + [shifted(other, "x", by) for by in (1, 2, 3)]
-    groups = (x - jnp.arange(4)) % 4
-    begin = project(groups + 4 * w, own_all, weight)
-    return project(groups + 4 * (1 - w), other_all, weight, begin)
+    everyone = lax.all_gather(attended, "x", axis=0)
+    w = lax.axis_index("w")
+    ahead = (2 * jnp.stack([1 - w, w])[:, None] + jnp.arange(2) - lax.axis_index("a")) % 4
+    places = jnp.where(ahead == 1, jnp.where(even, 2, 3), jnp.where(ahead == 3, jnp.where(even, 3, 2), ahead // 2))
+    theirs = project(places[0], everyone, weight, jnp.bfloat16)
+    mine = project(places[1], everyone, weight, jnp.float32, (theirs,))
+    return (mine + swap(theirs, "w").astype(jnp.float32)).astype(jnp.bfloat16)
 
 
 def solution(mesh):

time: 168 us -> 165 us (0.982); the launches traced: 167 us -> 162 us
  waiting for transfers between devices: 66.4 us -> 50.2 us
  blocking collectives: 0 us -> 14.1 us
  local copies, waits for them, and re-layouts: 5.82 us -> 1.28 us
  starting transfers between devices: 65.8 us -> 62.7 us
  Pallas kernels: 10.6 us -> 12.9 us
  other arithmetic: 4.29 us -> 6.18 us
    all_to_all x1, waiting for transfers between devices: 17.1 us -> 0.01 us  [per_device(): got = lax.all_to_all(sent, 'z', 0, 0, tiled=True)]
    ppermute x10 -> x7, waiting for transfers between devices: 18.4 us -> 32.8 us  [the longest x6 32.8 us: mirrored(): lax.ppermute(x, ('a', 'b'), [(y, (y + (by if y % 2 == 0 else -by)) % 8) f...]
    all_gather x0 -> x1, blocking collectives: none -> 14.1 us  [per_device(): everyone = lax.all_gather(attended, 'x', axis=0)]
    all_gather x2 -> x1, waiting for transfers between devices: 9.78 us -> 0.01 us  [per_device(): weight = lax.all_gather(weight, ('z', 'c'), axis=0)]
    ppermute x10 -> x7, starting transfers between devices: 35.1 us -> 30.1 us  [the longest x6 26.8 us: mirrored(): lax.ppermute(x, ('a', 'b'), [(y, (y + (by if y % 2 == 0 else -by)) % 8) f...]
    ppermute x6, waiting for transfers between devices: 21 us -> 17.3 us  [swap(): return lax.ppermute(x, axis, [(0, 1), (1, 0)])]
    unnamed x14 -> x28, local copies, waits for them, and re-layouts: 3.71 us -> 0.9 us
    concatenate x2, other arithmetic: 2.8 us -> 0.08 us  [the longest x1 0.05 us: per_device(): beside = swap(jnp.concatenate([key_proj, value, turned], axis=0), 'b')]
  transfers between devices with their start and end apart: 20 -> 16, of which waited for: 11 -> 8; matrix products, arithmetic and copies ran while one was open for 1% -> 3% of each run, Pallas kernels for 5% -> 6%
where the time goes in v3:
time: 165 us; the launch traced here: 162 us
  starting transfers between devices  62.7 us (38%)
  waiting for transfers between devices  50.2 us (30%)
  between operations  14.5 us (9%)
  blocking collectives  14.1 us (9%)
  Pallas kernels  12.9 us (8%)
  other arithmetic  6.18 us (4%)
    ppermute x6, waiting for transfers between devices, mirrored(): lax.ppermute(x, ('a', 'b'), [(y, (y + (by if y % 2 == 0 else -by)) % 8) f...  32.8 us
    ppermute x6, starting transfers between devices, mirrored(): lax.ppermute(x, ('a', 'b'), [(y, (y + (by if y % 2 == 0 else -by)) % 8) f...  26.8 us
    ppermute x6, starting transfers between devices, swap(): return lax.ppermute(x, axis, [(0, 1), (1, 0)])  18.5 us
    ppermute x6, waiting for transfers between devices, swap(): return lax.ppermute(x, axis, [(0, 1), (1, 0)])  17.3 us
    all_gather x1, blocking collectives, per_device(): everyone = lax.all_gather(attended, 'x', axis=0)  14.1 us
    all_to_all x1, starting transfers between devices, per_device(): got = lax.all_to_all(sent, 'z', 0, 0, tiled=True)  7.13 us
    all_to_all x1, starting transfers between devices, per_device(): lax.all_to_all(back.reshape(8, half, width), ('z', 'c'), 0, 0, tiled=True)  7.02 us
    pallas_call x2, Pallas kernels, project(): pl.pallas_call(project_kernel, out_shape=jax.ShapeDtypeStruct((rows, colu...  6.11 us
  transfers between devices with their start and end apart: 16, of which 8 were waited for; matrix products, arithmetic and copies ran while one was open for 3% of the time, Pallas kernels for 6%

profile of v3, /device:TPU:72, one launch (start us, length us, event | category | flops | bytes accessed | tf_op | source)
XLA Modules:
  0.0 161.8 jit_solution(17400210210887848019)
XLA Ops:
  6.5 1.0 broadcast_select_fusion.1
  7.6 1.9 %collective-permute-start = (bf16[256,384]{1,0:T(8,128)(2,1)S(1)}, bf16[256,384]{1,0:T(8,128)(2,1)S(1)}, u32[]{:S(2)}, u32[]{:S(2)}) collective-permute-start(bf16[256,384]{1,0:T(8,128)(2,1)S(1)} %broadcast_select_fusion.1), channel_id=1, source_target_pairs={{0,8},{8,0},{1,9},{9,1},{2,10},{10,2},{3,11},{11,3},{4,12},{12,4},... | collective-permute-start | bytes 589832 | tf_op jit(solution)/shard_map/ppermute | solution.py:25
  9.5 3.3 %collective-permute-start.1 = (bf16[80,384]{1,0:T(8,128)(2,1)}, bf16[80,384]{1,0:T(8,128)(2,1)S(1)}, u32[]{:S(2)}, u32[]{:S(2)}) collective-permute-start(bf16[80,384]{1,0:T(8,128)(2,1)} %bitcast.54), channel_id=1, source_target_pairs={{0,0},{1,64},{2,128},{3,192},{64,1},{65,65},{66,129},{67,193},{128... | collective-permute-start | bytes 184328 | tf_op jit(solution)/shard_map/ppermute | solution.py:197
  13.5 0.7 broadcast_compare_fusion
  14.1 0.1 pad.13.clone
  14.2 0.1 broadcast_bitcast_fusion
  14.3 0.0 collective-permute-done
  14.3 1.0 select_select_fusion
  15.2 2.2 %maximum_select_fusion = bf16[4,256,384]{2,1,0:T(8,128)(2,1)} fusion(bf16[4,64,384]{2,1,0:T(8,128)(2,1)} %bitcast.46, bf16[4,64,384]{2,1,0:T(8,128)(2,1)} %bitcast.45, bf16[4,64,384]{2,1,0:T(8,128)(2,1)} %bitcast.47, pred[384]{0:T(512)(128)(4,1)S(1)} %broadcast_bitcast_fusion, bf16[256]{0:T(256)(128)(2,1)S(1)} %pad.13.clone, ...), kind=kLoop, calls=%fused_computation | loop fusion | flops 3538944 | bytes 1573760 | tf_op jit(solution)/shard_map/jit(_where)/select_n | solution.py:207
  17.6 2.1 %collective-permute-start.2 = (bf16[592,384]{1,0:T(8,128)(2,1)S(1)}, bf16[592,384]{1,0:T(8,128)(2,1)S(1)}, u32[]{:S(2)}, u32[]{:S(2)}) collective-permute-start(bf16[592,384]{1,0:T(8,128)(2,1)S(1)} %pad_maximum_fusion), channel_id=1, source_target_pairs={{0,64},{64,0},{1,65},{65,1},{2,66},{66,2},{3,67},{67,3},{4,68},{68... | collective-permute-start | bytes 1363976 | tf_op jit(solution)/shard_map/ppermute | solution.py:25
  19.6 7.1 %all-to-all-start = ((bf16[4,256,384]{2,1,0:T(8,128)(2,1)}), bf16[4,256,384]{2,1,0:T(8,128)(2,1)S(1)}, u32[]{:S(2)}, u32[]{:S(2)}) async-start(bf16[4,256,384]{2,1,0:T(8,128)(2,1)} %maximum_select_fusion), calls=%async_computation | async-start | bytes 1572864 | tf_op jit(solution)/shard_map/all_to_all | solution.py:210
  26.8 5.4 %collective-permute-done.2 = bf16[592,384]{1,0:T(8,128)(2,1)S(1)} collective-permute-done((bf16[592,384]{1,0:T(8,128)(2,1)S(1)}, bf16[592,384]{1,0:T(8,128)(2,1)S(1)}, u32[]{:S(2)}, u32[]{:S(2)}) %collective-permute-start.2) | collective-permute-done | bytes 454688 | tf_op jit(solution)/shard_map/ppermute | solution.py:25
  32.2 6.6 %collective-permute-start.3 = (bf16[416,384]{1,0:T(8,128)(2,1)S(1)}, bf16[416,384]{1,0:T(8,128)(2,1)S(1)}, u32[]{:S(2)}, u32[]{:S(2)}) collective-permute-start(bf16[416,384]{1,0:T(8,128)(2,1)S(1)} %pad_maximum_fusion.2), channel_id=1, source_target_pairs={{0,320},{64,256},{128,448},{192,384},{256,64},{320,0},{384,192},{4... | collective-permute-start | bytes 958472 | tf_op jit(solution)/shard_map/ppermute | solution.py:184
  38.8 5.2 %collective-permute-start.4 = (bf16[416,384]{1,0:T(8,128)(2,1)S(1)}, bf16[416,384]{1,0:T(8,128)(2,1)S(1)}, u32[]{:S(2)}, u32[]{:S(2)}) collective-permute-start(bf16[416,384]{1,0:T(8,128)(2,1)S(1)} %pad_maximum_fusion.2), channel_id=1, source_target_pairs={{0,192},{64,384},{128,320},{192,0},{256,448},{320,128},{384,64},{4... | collective-permute-start | bytes 958472 | tf_op jit(solution)/shard_map/ppermute | solution.py:184
  44.0 2.5 %collective-permute-start.5 = (bf16[416,384]{1,0:T(8,128)(2,1)S(1)}, bf16[416,384]{1,0:T(8,128)(2,1)S(1)}, u32[]{:S(2)}, u32[]{:S(2)}) collective-permute-start(bf16[416,384]{1,0:T(8,128)(2,1)S(1)} %pad_maximum_fusion.2), channel_id=1, source_target_pairs={{0,448},{64,128},{128,64},{192,256},{256,192},{320,384},{384,320},... | collective-permute-start | bytes 958472 | tf_op jit(solution)/shard_map/ppermute | solution.py:184
  46.6 4.5 %collective-permute-done.3 = bf16[416,384]{1,0:T(8,128)(2,1)S(1)} collective-permute-done((bf16[416,384]{1,0:T(8,128)(2,1)S(1)}, bf16[416,384]{1,0:T(8,128)(2,1)S(1)}, u32[]{:S(2)}, u32[]{:S(2)}) %collective-permute-start.3) | collective-permute-done | bytes 319520 | tf_op jit(solution)/shard_map/ppermute | solution.py:184
  51.0 11.2 %collective-permute-done.4 = bf16[416,384]{1,0:T(8,128)(2,1)S(1)} collective-permute-done((bf16[416,384]{1,0:T(8,128)(2,1)S(1)}, bf16[416,384]{1,0:T(8,128)(2,1)S(1)}, u32[]{:S(2)}, u32[]{:S(2)}) %collective-permute-start.4) | collective-permute-done | bytes 319520 | tf_op jit(solution)/shard_map/ppermute | solution.py:184
  62.3 4.5 %collective-permute-done.5 = bf16[416,384]{1,0:T(8,128)(2,1)S(1)} collective-permute-done((bf16[416,384]{1,0:T(8,128)(2,1)S(1)}, bf16[416,384]{1,0:T(8,128)(2,1)S(1)}, u32[]{:S(2)}, u32[]{:S(2)}) %collective-permute-start.5) | collective-permute-done | bytes 319520 | tf_op jit(solution)/shard_map/ppermute | solution.py:184
  66.9 0.8 copy-done.4
  67.7 0.0 all-gather.3.cloned.1.call-update
  67.8 3.3 %collective-permute-start.6 = (bf16[256,384]{1,0:T(8,128)(2,1)S(1)}, bf16[256,384]{1,0:T(8,128)(2,1)S(1)}, u32[]{:S(2)}, u32[]{:S(2)}) collective-permute-start(bf16[256,384]{1,0:T(8,128)(2,1)S(1)} %dynamic-slice_bitcast_fusion), channel_id=1, source_target_pairs={{0,64},{64,0},{1,65},{65,1},{2,66},{66,2},{3,67},{67,3},{4,68},{68... | collective-permute-start | bytes 589832 | tf_op jit(solution)/shard_map/ppermute | solution.py:25
  71.2 0.1 fusion.5
  71.3 0.0 copy-start.3
  71.3 1.9 %collective-permute-start.7 = (bf16[4,3,32,384]{3,2,0,1:T(8,128)(2,1)S(1)}, bf16[4,3,32,384]{3,2,0,1:T(8,128)(2,1)S(1)}, u32[]{:S(2)}, u32[]{:S(2)}) collective-permute-start(bf16[4,3,32,384]{3,2,0,1:T(8,128)(2,1)S(1)} %select_bitcast_fusion), channel_id=1, source_target_pairs={{0,8},{8,0},{1,9},{9,1},{2,10},{10,2},{3,11},{11,3},{4,12},{12,4},... | collective-permute-start | bytes 884744 | tf_op jit(solution)/shard_map/ppermute | solution.py:25
  73.2 3.0 %collective-permute-done.6 = bf16[256,384]{1,0:T(8,128)(2,1)S(1)} collective-permute-done((bf16[256,384]{1,0:T(8,128)(2,1)S(1)}, bf16[256,384]{1,0:T(8,128)(2,1)S(1)}, u32[]{:S(2)}, u32[]{:S(2)}) %collective-permute-start.6) | collective-permute-done | bytes 196640 | tf_op jit(solution)/shard_map/ppermute | solution.py:25
  76.3 0.1 fusion.1
  76.4 0.0 copy-start.8
  76.4 0.1 pad_maximum_fusion.3
  76.5 2.1 %temporal.1 = bf16[256,384]{1,0:T(8,128)(2,1)} custom-call(s32[3]{0:T(128)S(1)} %copy-done.3, bf16[256,384]{1,0:T(8,128)(2,1)S(1)} %bitcast.49, bf16[256,384]{1,0:T(8,128)(2,1)S(1)} %bitcast.50, bf16[256,384]{1,0:T(8,128)(2,1)S(1)} %bitcast.48), custom_call_target="tpu_custom_call" | custom-call | tf_op jit(solution)/shard_map/temporal/pallas_call | solution.py:103
  78.5 1.9 %collective-permute-start.8 = (bf16[512,384]{1,0:T(8,128)(2,1)S(1)}, bf16[512,384]{1,0:T(8,128)(2,1)S(1)}, u32[]{:S(2)}, u32[]{:S(2)}) collective-permute-start(bf16[512,384]{1,0:T(8,128)(2,1)S(1)} %pad_maximum_fusion.1.refs_5_), channel_id=1, source_target_pairs={{0,8},{8,0},{1,9},{9,1},{2,10},{10,2},{3,11},{11,3},{4,12},{12,4},... | collective-permute-start | bytes 1179656 | tf_op jit(solution)/shard_map/ppermute | solution.py:25
  80.5 0.1 add_multiply_fusion
  80.5 7.0 %all-to-all-start.1 = ((bf16[8,32,384]{2,1,0:T(8,128)(2,1)}), bf16[8,32,384]{2,1,0:T(8,128)(2,1)S(1)}, u32[]{:S(2)}, u32[]{:S(2)}) async-start(bf16[8,32,384]{2,1,0:T(8,128)(2,1)} %bitcast.20), calls=%async_computation.1 | async-start | bytes 393216 | tf_op jit(solution)/shard_map/all_to_all | solution.py:238
  87.6 0.1 compare_select_fusion.3
  87.8 0.0 collective-permute-done.8.refs_6_
  87.8 2.6 %spatial.2 = (bf16[400,256]{1,0:T(8,128)(2,1)S(1)}, bf16[400,256]{1,0:T(8,128)(2,1)S(1)}, bf16[400,256]{1,0:T(8,128)(2,1)S(1)}) custom-call(s32[3]{0:T(128)S(1)} %copy-done.3, s32[1]{0:T(128)} %bitcast.3.refs_1_, bf16[256,384]{1,0:T(8,128)(2,1)S(1)} %copy-done, bf16[256,384]{1,0:T(8,128)(2,1)S(1)} %copy-done.1, bf16[512,384]{1,0:T(8,128)(2,1)S(1)} %slice.65.refs_4_, ...), custom_call_target="tpu_custom_call" | custom-call | tf_op jit(solution)/shard_map/spatial/pallas_call | solution.py:71
  90.5 7.0 %collective-permute-start.9 = (bf16[400,256]{1,0:T(8,128)(2,1)S(1)}, bf16[400,256]{1,0:T(8,128)(2,1)S(1)}, u32[]{:S(2)}, u32[]{:S(2)}) collective-permute-start(bf16[400,256]{1,0:T(8,128)(2,1)S(1)} %get-tuple-element.23.refs_8_), channel_id=1, source_target_pairs={{0,320},{64,256},{128,448},{192,384},{256,64},{320,0},{384,192},{4... | collective-permute-start | bytes 614408 | tf_op jit(solution)/shard_map/ppermute | solution.py:184
  97.5 2.4 %collective-permute-start.10 = (bf16[400,256]{1,0:T(8,128)(2,1)S(1)}, bf16[400,256]{1,0:T(8,128)(2,1)S(1)}, u32[]{:S(2)}, u32[]{:S(2)}) collective-permute-start(bf16[400,256]{1,0:T(8,128)(2,1)S(1)} %get-tuple-element.24), channel_id=1, source_target_pairs={{0,192},{64,384},{128,320},{192,0},{256,448},{320,128},{384,64},{4... | collective-permute-start | bytes 614408 | tf_op jit(solution)/shard_map/ppermute | solution.py:184
  99.9 3.1 %collective-permute-start.11 = (bf16[400,256]{1,0:T(8,128)(2,1)S(1)}, bf16[400,256]{1,0:T(8,128)(2,1)S(1)}, u32[]{:S(2)}, u32[]{:S(2)}) collective-permute-start(bf16[400,256]{1,0:T(8,128)(2,1)S(1)} %get-tuple-element.25), channel_id=1, source_target_pairs={{0,448},{64,128},{128,64},{192,256},{256,192},{320,384},{384,320},... | collective-permute-start | bytes 614408 | tf_op jit(solution)/shard_map/ppermute | solution.py:184
  103.0 1.3 spatial.3.p3_ref
  104.3 7.9 %collective-permute-done.9.p0_ref = bf16[400,256]{1,0:T(8,128)(2,1)S(1)} collective-permute-done((bf16[400,256]{1,0:T(8,128)(2,1)S(1)}, bf16[400,256]{1,0:T(8,128)(2,1)S(1)}, u32[]{:S(2)}, u32[]{:S(2)}) %collective-permute-start.9) | collective-permute-done | bytes 204832 | tf_op jit(solution)/shard_map/ppermute | solution.py:184
  112.3 4.6 %collective-permute-done.10.p1_ref = bf16[400,256]{1,0:T(8,128)(2,1)S(1)} collective-permute-done((bf16[400,256]{1,0:T(8,128)(2,1)S(1)}, bf16[400,256]{1,0:T(8,128)(2,1)S(1)}, u32[]{:S(2)}, u32[]{:S(2)}) %collective-permute-start.10) | collective-permute-done | bytes 204832 | tf_op jit(solution)/shard_map/ppermute | solution.py:184
  116.9 0.7 combine.1
  117.7 14.1 %all-gather = bf16[1024,384]{1,0:T(8,128)(2,1)S(1)} all-gather(bf16[256,384]{1,0:T(8,128)(2,1)S(1)} %combine.1), channel_id=2, replica_groups=mesh['a'=4,'b'=2,'z'=4,'c'=2,'w'=2,'x'=4] {'x'}, dimensions={0}, use_global_device_ids=true | all-gather | bytes 983040 | tf_op jit(solution)/shard_map/all_gather | solution.py:246
  131.8 3.1 %project.2.rest_0_ = bf16[256,640]{1,0:T(8,128)(2,1)S(1)} custom-call(s32[2]{0:T(128)S(1)} %get-tuple-element.38.at_ref, bf16[4,256,384]{2,1,0:T(8,128)(2,1)S(1)} %bitcast.43, bf16[8,8,80,384]{3,2,1,0:T(8,128)(2,1)} %all-gather.3.cloned.1.call-done.low_ref.high_ref, bf16[8,8,80,384]{3,2,1,0:T(8,128)(2,1)} %all-gather.3.cloned.1.call-done.low_ref.high_ref), custom_call_target="tpu_custom_call" | custom-call | tf_op jit(solution)/shard_map/project/pallas_call | solution.py:159
  134.8 7.3 %collective-permute-start.12 = (bf16[256,640]{1,0:T(8,128)(2,1)S(1)}, bf16[256,640]{1,0:T(8,128)(2,1)S(1)}, u32[]{:S(2)}, u32[]{:S(2)}) collective-permute-start(bf16[256,640]{1,0:T(8,128)(2,1)S(1)} %project.2.rest_0_), channel_id=1, source_target_pairs={{0,4},{4,0},{1,5},{5,1},{2,6},{6,2},{3,7},{7,3},{8,12},{12,8},{9,1... | collective-permute-start | bytes 983048 | tf_op jit(solution)/shard_map/ppermute | solution.py:25
  142.2 3.1 %project.3 = f32[256,640]{1,0:T(8,128)S(1)} custom-call(s32[2]{0:T(128)S(1)} %get-tuple-element.39.at_ref, bf16[4,256,384]{2,1,0:T(8,128)(2,1)S(1)} %bitcast.44, bf16[8,8,80,384]{3,2,1,0:T(8,128)(2,1)} %all-gather.3.cloned.1.call-done.low_ref.high_ref, bf16[8,8,80,384]{3,2,1,0:T(8,128)(2,1)} %all-gather.3.cloned.1.call-done.low_ref.high_ref, ...), custom_call_target="tpu_custom_call" | custom-call | tf_op jit(solution)/shard_map/project/pallas_call | solution.py:159
  145.2 8.9 %collective-permute-done.12 = bf16[256,640]{1,0:T(8,128)(2,1)S(1)} collective-permute-done((bf16[256,640]{1,0:T(8,128)(2,1)S(1)}, bf16[256,640]{1,0:T(8,128)(2,1)S(1)}, u32[]{:S(2)}, u32[]{:S(2)}) %collective-permute-start.12) | collective-permute-done | bytes 327712 | tf_op jit(solution)/shard_map/ppermute | solution.py:25
  154.2 0.8 add_convert_fusion
  (46 shorter events, 0.5 us)
Async XLA Ops:
  6.5 11.0 %copy-start = (bf16[256,384]{1,0:T(8,128)(2,1)S(1)}, bf16[256,384]{1,0:T(8,128)(2,1)}, u32[]{:S(2)}) copy-start(bf16[256,384]{1,0:T(8,128)(2,1)} %refs_2_.3) | copy-start | bytes 589828
  6.5 11.0 %copy-start.1 = (bf16[256,384]{1,0:T(8,128)(2,1)S(1)}, bf16[256,384]{1,0:T(8,128)(2,1)}, u32[]{:S(2)}) copy-start(bf16[256,384]{1,0:T(8,128)(2,1)} %refs_3_.3) | copy-start | bytes 589828
  7.6 6.7 %collective-permute-start = (bf16[256,384]{1,0:T(8,128)(2,1)S(1)}, bf16[256,384]{1,0:T(8,128)(2,1)S(1)}, u32[]{:S(2)}, u32[]{:S(2)}) collective-permute-start(bf16[256,384]{1,0:T(8,128)(2,1)S(1)} %broadcast_select_fusion.1), channel_id=1, source_target_pairs={{0,8},{8,0},{1,9},{9,1},{2,10},{10,2},{3,11},{11,3},{4,12},{12,4},... | collective-permute-start | bytes 589832 | tf_op jit(solution)/shard_map/ppermute | solution.py:25
  9.5 8.0 %collective-permute-start.1 = (bf16[80,384]{1,0:T(8,128)(2,1)}, bf16[80,384]{1,0:T(8,128)(2,1)S(1)}, u32[]{:S(2)}, u32[]{:S(2)}) collective-permute-start(bf16[80,384]{1,0:T(8,128)(2,1)} %bitcast.54), channel_id=1, source_target_pairs={{0,0},{1,64},{2,128},{3,192},{64,1},{65,65},{66,129},{67,193},{128... | collective-permute-start | bytes 184328 | tf_op jit(solution)/shard_map/ppermute | solution.py:197
  17.5 14.7 %copy-start.2 = (bf16[256,384]{1,0:T(8,128)(2,1)S(1)}, bf16[256,384]{1,0:T(8,128)(2,1)}, u32[]{:S(2)}) copy-start(bf16[256,384]{1,0:T(8,128)(2,1)} %refs_7_.1) | copy-start | bytes 589828
  17.6 14.6 %collective-permute-start.2 = (bf16[592,384]{1,0:T(8,128)(2,1)S(1)}, bf16[592,384]{1,0:T(8,128)(2,1)S(1)}, u32[]{:S(2)}, u32[]{:S(2)}) collective-permute-start(bf16[592,384]{1,0:T(8,128)(2,1)S(1)} %pad_maximum_fusion), channel_id=1, source_target_pairs={{0,64},{64,0},{1,65},{65,1},{2,66},{66,2},{3,67},{67,3},{4,68},{68... | collective-permute-start | bytes 1363976 | tf_op jit(solution)/shard_map/ppermute | solution.py:25
  19.6 47.2 %all-to-all-start = ((bf16[4,256,384]{2,1,0:T(8,128)(2,1)}), bf16[4,256,384]{2,1,0:T(8,128)(2,1)S(1)}, u32[]{:S(2)}, u32[]{:S(2)}) async-start(bf16[4,256,384]{2,1,0:T(8,128)(2,1)} %maximum_select_fusion), calls=%async_computation | async-start | bytes 1572864 | tf_op jit(solution)/shard_map/all_to_all | solution.py:210
  26.8 105.0 %all-gather.3.cloned.1.call-start = ((), (), s32[]{:S(2)}) async-start(), calls=%async_computation.2 | async-start | bytes 4423680 | tf_op jit(solution)/shard_map/all_gather | solution.py:222
  32.1 39.0 %copy-start.5 = (bf16[592,384]{1,0:T(8,128)(2,1)}, bf16[592,384]{1,0:T(8,128)(2,1)S(1)}, u32[]{:S(2)}) copy-start(bf16[592,384]{1,0:T(8,128)(2,1)S(1)} %collective-permute-done.2) | copy-start | bytes 1363972
  32.2 18.8 %collective-permute-start.3 = (bf16[416,384]{1,0:T(8,128)(2,1)S(1)}, bf16[416,384]{1,0:T(8,128)(2,1)S(1)}, u32[]{:S(2)}, u32[]{:S(2)}) collective-permute-start(bf16[416,384]{1,0:T(8,128)(2,1)S(1)} %pad_maximum_fusion.2), channel_id=1, source_target_pairs={{0,320},{64,256},{128,448},{192,384},{256,64},{320,0},{384,192},{4... | collective-permute-start | bytes 958472 | tf_op jit(solution)/shard_map/ppermute | solution.py:184
  38.8 23.5 %collective-permute-start.4 = (bf16[416,384]{1,0:T(8,128)(2,1)S(1)}, bf16[416,384]{1,0:T(8,128)(2,1)S(1)}, u32[]{:S(2)}, u32[]{:S(2)}) collective-permute-start(bf16[416,384]{1,0:T(8,128)(2,1)S(1)} %pad_maximum_fusion.2), channel_id=1, source_target_pairs={{0,192},{64,384},{128,320},{192,0},{256,448},{320,128},{384,64},{4... | collective-permute-start | bytes 958472 | tf_op jit(solution)/shard_map/ppermute | solution.py:184
  44.0 22.8 %collective-permute-start.5 = (bf16[416,384]{1,0:T(8,128)(2,1)S(1)}, bf16[416,384]{1,0:T(8,128)(2,1)S(1)}, u32[]{:S(2)}, u32[]{:S(2)}) collective-permute-start(bf16[416,384]{1,0:T(8,128)(2,1)S(1)} %pad_maximum_fusion.2), channel_id=1, source_target_pairs={{0,448},{64,128},{128,64},{192,256},{256,192},{320,384},{384,320},... | collective-permute-start | bytes 958472 | tf_op jit(solution)/shard_map/ppermute | solution.py:184
  51.0 20.2 %copy-start.7 = (bf16[416,384]{1,0:T(8,128)(2,1)}, bf16[416,384]{1,0:T(8,128)(2,1)S(1)}, u32[]{:S(2)}) copy-start(bf16[416,384]{1,0:T(8,128)(2,1)S(1)} %collective-permute-done.3) | copy-start | bytes 958468
  62.3 5.5 %copy-start.9 = (bf16[416,384]{1,0:T(8,128)(2,1)}, bf16[416,384]{1,0:T(8,128)(2,1)S(1)}, u32[]{:S(2)}) copy-start(bf16[416,384]{1,0:T(8,128)(2,1)S(1)} %collective-permute-done.4) | copy-start | bytes 958468
  66.8 1.0 copy-start.11
  66.9 0.8 copy-start.4
  67.8 8.4 %collective-permute-start.6 = (bf16[256,384]{1,0:T(8,128)(2,1)S(1)}, bf16[256,384]{1,0:T(8,128)(2,1)S(1)}, u32[]{:S(2)}, u32[]{:S(2)}) collective-permute-start(bf16[256,384]{1,0:T(8,128)(2,1)S(1)} %dynamic-slice_bitcast_fusion), channel_id=1, source_target_pairs={{0,64},{64,0},{1,65},{65,1},{2,66},{66,2},{3,67},{67,3},{4,68},{68... | collective-permute-start | bytes 589832 | tf_op jit(solution)/shard_map/ppermute | solution.py:25
  71.3 5.2 %copy-start.3 = (s32[3]{0:T(128)S(1)}, s32[3]{0:T(128)}, u32[]{:S(2)}) copy-start(s32[3]{0:T(128)} %hc_ref.3) | copy-start | bytes 40
  71.3 5.0 %collective-permute-start.7 = (bf16[4,3,32,384]{3,2,0,1:T(8,128)(2,1)S(1)}, bf16[4,3,32,384]{3,2,0,1:T(8,128)(2,1)S(1)}, u32[]{:S(2)}, u32[]{:S(2)}) collective-permute-start(bf16[4,3,32,384]{3,2,0,1:T(8,128)(2,1)S(1)} %select_bitcast_fusion), channel_id=1, source_target_pairs={{0,8},{8,0},{1,9},{9,1},{2,10},{10,2},{3,11},{11,3},{4,12},{12,4},... | collective-permute-start | bytes 884744 | tf_op jit(solution)/shard_map/ppermute | solution.py:25
  76.3 11.4 %copy-start.6 = (bf16[592,384]{1,0:T(8,128)(2,1)S(1)}, bf16[592,384]{1,0:T(8,128)(2,1)}, u32[]{:S(2)}) copy-start(bf16[592,384]{1,0:T(8,128)(2,1)} %copy-done.5) | copy-start | bytes 1363972
  76.4 11.4 %copy-start.8 = (bf16[416,384]{1,0:T(8,128)(2,1)S(1)}, bf16[416,384]{1,0:T(8,128)(2,1)}, u32[]{:S(2)}) copy-start(bf16[416,384]{1,0:T(8,128)(2,1)} %copy-done.7) | copy-start | bytes 958468
  76.4 11.4 %copy-start.10 = (bf16[416,384]{1,0:T(8,128)(2,1)S(1)}, bf16[416,384]{1,0:T(8,128)(2,1)}, u32[]{:S(2)}) copy-start(bf16[416,384]{1,0:T(8,128)(2,1)} %copy-done.9) | copy-start | bytes 958468
  76.5 11.3 %copy-start.12 = (bf16[416,384]{1,0:T(8,128)(2,1)S(1)}, bf16[416,384]{1,0:T(8,128)(2,1)}, u32[]{:S(2)}) copy-start(bf16[416,384]{1,0:T(8,128)(2,1)} %copy-done.11) | copy-start | bytes 958468
  78.5 9.3 %collective-permute-start.8 = (bf16[512,384]{1,0:T(8,128)(2,1)S(1)}, bf16[512,384]{1,0:T(8,128)(2,1)S(1)}, u32[]{:S(2)}, u32[]{:S(2)}) collective-permute-start(bf16[512,384]{1,0:T(8,128)(2,1)S(1)} %pad_maximum_fusion.1.refs_5_), channel_id=1, source_target_pairs={{0,8},{8,0},{1,9},{9,1},{2,10},{10,2},{3,11},{11,3},{4,12},{12,4},... | collective-permute-start | bytes 1179656 | tf_op jit(solution)/shard_map/ppermute | solution.py:25
  80.5 23.8 %all-to-all-start.1 = ((bf16[8,32,384]{2,1,0:T(8,128)(2,1)}), bf16[8,32,384]{2,1,0:T(8,128)(2,1)S(1)}, u32[]{:S(2)}, u32[]{:S(2)}) async-start(bf16[8,32,384]{2,1,0:T(8,128)(2,1)} %bitcast.20), calls=%async_computation.1 | async-start | bytes 393216 | tf_op jit(solution)/shard_map/all_to_all | solution.py:238
  90.5 21.8 %collective-permute-start.9 = (bf16[400,256]{1,0:T(8,128)(2,1)S(1)}, bf16[400,256]{1,0:T(8,128)(2,1)S(1)}, u32[]{:S(2)}, u32[]{:S(2)}) collective-permute-start(bf16[400,256]{1,0:T(8,128)(2,1)S(1)} %get-tuple-element.23.refs_8_), channel_id=1, source_target_pairs={{0,320},{64,256},{128,448},{192,384},{256,64},{320,0},{384,192},{4... | collective-permute-start | bytes 614408 | tf_op jit(solution)/shard_map/ppermute | solution.py:184
  97.5 19.4 %collective-permute-start.10 = (bf16[400,256]{1,0:T(8,128)(2,1)S(1)}, bf16[400,256]{1,0:T(8,128)(2,1)S(1)}, u32[]{:S(2)}, u32[]{:S(2)}) collective-permute-start(bf16[400,256]{1,0:T(8,128)(2,1)S(1)} %get-tuple-element.24), channel_id=1, source_target_pairs={{0,192},{64,384},{128,320},{192,0},{256,448},{320,128},{384,64},{4... | collective-permute-start | bytes 614408 | tf_op jit(solution)/shard_map/ppermute | solution.py:184
  99.9 17.1 %collective-permute-start.11 = (bf16[400,256]{1,0:T(8,128)(2,1)S(1)}, bf16[400,256]{1,0:T(8,128)(2,1)S(1)}, u32[]{:S(2)}, u32[]{:S(2)}) collective-permute-start(bf16[400,256]{1,0:T(8,128)(2,1)S(1)} %get-tuple-element.25), channel_id=1, source_target_pairs={{0,448},{64,128},{128,64},{192,256},{256,192},{320,384},{384,320},... | collective-permute-start | bytes 614408 | tf_op jit(solution)/shard_map/ppermute | solution.py:184
  134.8 19.4 %collective-permute-start.12 = (bf16[256,640]{1,0:T(8,128)(2,1)S(1)}, bf16[256,640]{1,0:T(8,128)(2,1)S(1)}, u32[]{:S(2)}, u32[]{:S(2)}) collective-permute-start(bf16[256,640]{1,0:T(8,128)(2,1)S(1)} %project.2.rest_0_), channel_id=1, source_target_pairs={{0,4},{4,0},{1,5},{5,1},{2,6},{6,2},{3,7},{7,3},{8,12},{12,8},{9,1... | collective-permute-start | bytes 983048 | tf_op jit(solution)/shard_map/ppermute | solution.py:25
Sparse Core Ops, SparseCore 0:
  67.9 56.3 all-gather.2

commit v4 on v3

--- a/solution.py
+++ b/solution.py
@@ -143,13 +143,22 @@
     )(hc, *parts, back)
 
 
-def project_kernel(at_ref, all_ref, low_ref, high_ref, *rest):
+def project_kernel(at_ref, all_ref, weight_ref, *rest):
+    out_ref, total_ref = rest[-2:]
+    step = pl.program_id(0)
     total = None
-    for i, (ref, j) in enumerate(((low_ref, 0), (low_ref, 1), (high_ref, 0), (high_ref, 1))):
-        rows = jnp.concatenate([ref[k, j] for k in range(ref.shape[0])], axis=0)
+    for i in range(all_ref.shape[0]):
+        rows = jnp.concatenate([weight_ref[k, i] for k in range(weight_ref.shape[0])], axis=0)
         term = dot(all_ref[i], rows, NT)
         total = term if total is None else total + term
-    rest[-1][...] = total.astype(rest[-1].dtype)
+
+    @pl.when(step == 0)
+    def _():
+        total_ref[...] = total
+
+    @pl.when(step == 1)
+    def _():
+        out_ref[...] = (total_ref[...] + total).astype(out_ref.dtype)
 
 
 def project(at, attended, weight, dtype, after=()):
@@ -161,18 +170,18 @@
         out_shape=jax.ShapeDtypeStruct((rows, columns), dtype),
         grid_spec=pltpu.PrefetchScalarGridSpec(
             num_scalar_prefetch=1,
-            grid=(1,),
+            grid=(2,),
             in_specs=[
-                pl.BlockSpec((count, rows, width), lambda i, at: (0, 0, 0)),
-                pl.BlockSpec(block, lambda i, at: (0, at[0], 0, 0)),
-                pl.BlockSpec(block, lambda i, at: (0, at[1], 0, 0)),
+                pl.BlockSpec((count // 2, rows, width), lambda i, at: (i, 0, 0)),
+                pl.BlockSpec(block, lambda i, at: (0, at[i], 0, 0)),
             ]
             + [pl.BlockSpec(memory_space=pl.ANY)] * len(after),
             out_specs=pl.BlockSpec((rows, columns), lambda i, at: (0, 0)),
+            scratch_shapes=[pltpu.VMEM((rows, columns), jnp.float32)],
         ),
         compiler_params=pltpu.CompilerParams(vmem_limit_bytes=50 * 1024 * 1024),
         name="project",
-    )(at, attended, weight, weight, *after)
+    )(at, attended, weight, *after)
 
 
 def shifted(x, axis, by):

time: 165 us -> 162 us (0.982)
  the two profiles are of different devices: /device:TPU:72 before, /device:TPU:6 now
where the time goes in v4:
time: 162 us; the launch traced here: 160 us
  starting transfers between devices  63.4 us (39%)
  waiting for transfers between devices  50.9 us (31%)
  between operations  14.5 us (9%)
  blocking collectives  13.3 us (8%)
  Pallas kernels  10.4 us (6%)
  other arithmetic  6.18 us (4%)
    ppermute x6, waiting for transfers between devices, mirrored(): lax.ppermute(x, ('a', 'b'), [(y, (y + (by if y % 2 == 0 else -by)) % 8) f...  34.4 us
    ppermute x6, starting transfers between devices, mirrored(): lax.ppermute(x, ('a', 'b'), [(y, (y + (by if y % 2 == 0 else -by)) % 8) f...  23.3 us
    ppermute x6, starting transfers between devices, swap(): return lax.ppermute(x, axis, [(0, 1), (1, 0)])  20 us
    ppermute x6, waiting for transfers between devices, swap(): return lax.ppermute(x, axis, [(0, 1), (1, 0)])  16.1 us
    all_gather x1, blocking collectives, per_device(): everyone = lax.all_gather(attended, 'x', axis=0)  13.3 us
    all_to_all x1, starting transfers between devices, per_device(): lax.all_to_all(back.reshape(8, half, width), ('z', 'c'), 0, 0, tiled=True)  7.37 us
    all_to_all x1, starting transfers between devices, per_device(): got = lax.all_to_all(sent, 'z', 0, 0, tiled=True)  7.27 us
    pallas_call x2, Pallas kernels, project(): pl.pallas_call(project_kernel, out_shape=jax.ShapeDtypeStruct((rows, colu...  6.17 us
  transfers between devices with their start and end apart: 16, of which 11 were waited for; matrix products, arithmetic and copies ran while one was open for 3% of the time, Pallas kernels for 5%

profile of v4, /device:TPU:6, one launch (start us, length us, event | category | flops | bytes accessed | tf_op | source)
XLA Modules:
  0.0 160.1 jit_solution(3296995774084445728)
XLA Ops:
  6.5 1.0 broadcast_select_fusion.1
  7.6 1.9 %collective-permute-start = (bf16[256,384]{1,0:T(8,128)(2,1)S(1)}, bf16[256,384]{1,0:T(8,128)(2,1)S(1)}, u32[]{:S(2)}, u32[]{:S(2)}) collective-permute-start(bf16[256,384]{1,0:T(8,128)(2,1)S(1)} %broadcast_select_fusion.1), channel_id=1, source_target_pairs={{0,8},{8,0},{1,9},{9,1},{2,10},{10,2},{3,11},{11,3},{4,12},{12,4},... | collective-permute-start | bytes 589832 | tf_op jit(solution)/shard_map/ppermute | solution.py:25
  9.5 5.4 %collective-permute-start.1 = (bf16[80,384]{1,0:T(8,128)(2,1)}, bf16[80,384]{1,0:T(8,128)(2,1)S(1)}, u32[]{:S(2)}, u32[]{:S(2)}) collective-permute-start(bf16[80,384]{1,0:T(8,128)(2,1)} %bitcast.54), channel_id=1, source_target_pairs={{0,0},{1,64},{2,128},{3,192},{64,1},{65,65},{66,129},{67,193},{128... | collective-permute-start | bytes 184328 | tf_op jit(solution)/shard_map/ppermute | solution.py:206
  15.6 0.7 broadcast_compare_fusion
  16.3 0.1 pad.13.clone
  16.3 0.1 broadcast_bitcast_fusion
  16.4 1.0 select_select_fusion
  17.4 2.2 %maximum_select_fusion = bf16[4,256,384]{2,1,0:T(8,128)(2,1)} fusion(bf16[4,64,384]{2,1,0:T(8,128)(2,1)} %bitcast.46, bf16[4,64,384]{2,1,0:T(8,128)(2,1)} %bitcast.45, bf16[4,64,384]{2,1,0:T(8,128)(2,1)} %bitcast.47, pred[384]{0:T(512)(128)(4,1)S(1)} %broadcast_bitcast_fusion, bf16[256]{0:T(256)(128)(2,1)S(1)} %pad.13.clone, ...), kind=kLoop, calls=%fused_computation | loop fusion | flops 3538944 | bytes 1573760 | tf_op jit(solution)/shard_map/jit(_where)/select_n | solution.py:216
  19.6 0.4 collective-permute-done.1
  20.1 3.1 %collective-permute-start.2 = (bf16[592,384]{1,0:T(8,128)(2,1)S(1)}, bf16[592,384]{1,0:T(8,128)(2,1)S(1)}, u32[]{:S(2)}, u32[]{:S(2)}) collective-permute-start(bf16[592,384]{1,0:T(8,128)(2,1)S(1)} %pad_maximum_fusion), channel_id=1, source_target_pairs={{0,64},{64,0},{1,65},{65,1},{2,66},{66,2},{3,67},{67,3},{4,68},{68... | collective-permute-start | bytes 1363976 | tf_op jit(solution)/shard_map/ppermute | solution.py:25
  23.2 7.3 %all-to-all-start = ((bf16[4,256,384]{2,1,0:T(8,128)(2,1)}), bf16[4,256,384]{2,1,0:T(8,128)(2,1)S(1)}, u32[]{:S(2)}, u32[]{:S(2)}) async-start(bf16[4,256,384]{2,1,0:T(8,128)(2,1)} %maximum_select_fusion), calls=%async_computation | async-start | bytes 1572864 | tf_op jit(solution)/shard_map/all_to_all | solution.py:219
  30.5 3.8 %collective-permute-done.2 = bf16[592,384]{1,0:T(8,128)(2,1)S(1)} collective-permute-done((bf16[592,384]{1,0:T(8,128)(2,1)S(1)}, bf16[592,384]{1,0:T(8,128)(2,1)S(1)}, u32[]{:S(2)}, u32[]{:S(2)}) %collective-permute-start.2) | collective-permute-done | bytes 454688 | tf_op jit(solution)/shard_map/ppermute | solution.py:25
  34.4 6.2 %collective-permute-start.3 = (bf16[416,384]{1,0:T(8,128)(2,1)S(1)}, bf16[416,384]{1,0:T(8,128)(2,1)S(1)}, u32[]{:S(2)}, u32[]{:S(2)}) collective-permute-start(bf16[416,384]{1,0:T(8,128)(2,1)S(1)} %pad_maximum_fusion.2), channel_id=1, source_target_pairs={{0,320},{64,256},{128,448},{192,384},{256,64},{320,0},{384,192},{4... | collective-permute-start | bytes 958472 | tf_op jit(solution)/shard_map/ppermute | solution.py:193
  40.6 1.9 %collective-permute-start.4 = (bf16[416,384]{1,0:T(8,128)(2,1)S(1)}, bf16[416,384]{1,0:T(8,128)(2,1)S(1)}, u32[]{:S(2)}, u32[]{:S(2)}) collective-permute-start(bf16[416,384]{1,0:T(8,128)(2,1)S(1)} %pad_maximum_fusion.2), channel_id=1, source_target_pairs={{0,192},{64,384},{128,320},{192,0},{256,448},{320,128},{384,64},{4... | collective-permute-start | bytes 958472 | tf_op jit(solution)/shard_map/ppermute | solution.py:193
  42.5 4.1 %collective-permute-start.5 = (bf16[416,384]{1,0:T(8,128)(2,1)S(1)}, bf16[416,384]{1,0:T(8,128)(2,1)S(1)}, u32[]{:S(2)}, u32[]{:S(2)}) collective-permute-start(bf16[416,384]{1,0:T(8,128)(2,1)S(1)} %pad_maximum_fusion.2), channel_id=1, source_target_pairs={{0,448},{64,128},{128,64},{192,256},{256,192},{320,384},{384,320},... | collective-permute-start | bytes 958472 | tf_op jit(solution)/shard_map/ppermute | solution.py:193
  46.7 15.6 %collective-permute-done.3 = bf16[416,384]{1,0:T(8,128)(2,1)S(1)} collective-permute-done((bf16[416,384]{1,0:T(8,128)(2,1)S(1)}, bf16[416,384]{1,0:T(8,128)(2,1)S(1)}, u32[]{:S(2)}, u32[]{:S(2)}) %collective-permute-start.3) | collective-permute-done | bytes 319520 | tf_op jit(solution)/shard_map/ppermute | solution.py:193
  62.3 3.8 %collective-permute-done.4 = bf16[416,384]{1,0:T(8,128)(2,1)S(1)} collective-permute-done((bf16[416,384]{1,0:T(8,128)(2,1)S(1)}, bf16[416,384]{1,0:T(8,128)(2,1)S(1)}, u32[]{:S(2)}, u32[]{:S(2)}) %collective-permute-start.4) | collective-permute-done | bytes 319520 | tf_op jit(solution)/shard_map/ppermute | solution.py:193
  66.1 1.3 collective-permute-done.5
  67.5 0.8 copy-done.4
  68.3 0.0 all-gather.3.cloned.1.call-update
  68.4 2.3 %collective-permute-start.6 = (bf16[256,384]{1,0:T(8,128)(2,1)S(1)}, bf16[256,384]{1,0:T(8,128)(2,1)S(1)}, u32[]{:S(2)}, u32[]{:S(2)}) collective-permute-start(bf16[256,384]{1,0:T(8,128)(2,1)S(1)} %dynamic-slice_bitcast_fusion), channel_id=1, source_target_pairs={{0,64},{64,0},{1,65},{65,1},{2,66},{66,2},{3,67},{67,3},{4,68},{68... | collective-permute-start | bytes 589832 | tf_op jit(solution)/shard_map/ppermute | solution.py:25
  70.8 0.1 fusion.5
  70.9 0.0 copy-start.3
  70.9 1.9 %collective-permute-start.7 = (bf16[4,3,32,384]{3,2,0,1:T(8,128)(2,1)S(1)}, bf16[4,3,32,384]{3,2,0,1:T(8,128)(2,1)S(1)}, u32[]{:S(2)}, u32[]{:S(2)}) collective-permute-start(bf16[4,3,32,384]{3,2,0,1:T(8,128)(2,1)S(1)} %select_bitcast_fusion), channel_id=1, source_target_pairs={{0,8},{8,0},{1,9},{9,1},{2,10},{10,2},{3,11},{11,3},{4,12},{12,4},... | collective-permute-start | bytes 884744 | tf_op jit(solution)/shard_map/ppermute | solution.py:25
  72.8 3.9 %collective-permute-done.6 = bf16[256,384]{1,0:T(8,128)(2,1)S(1)} collective-permute-done((bf16[256,384]{1,0:T(8,128)(2,1)S(1)}, bf16[256,384]{1,0:T(8,128)(2,1)S(1)}, u32[]{:S(2)}, u32[]{:S(2)}) %collective-permute-start.6) | collective-permute-done | bytes 196640 | tf_op jit(solution)/shard_map/ppermute | solution.py:25
  76.8 0.1 fusion.1
  76.9 0.1 pad_maximum_fusion.3
  77.0 2.5 %temporal.1 = bf16[256,384]{1,0:T(8,128)(2,1)} custom-call(s32[3]{0:T(128)S(1)} %copy-done.3, bf16[256,384]{1,0:T(8,128)(2,1)S(1)} %bitcast.49, bf16[256,384]{1,0:T(8,128)(2,1)S(1)} %bitcast.50, bf16[256,384]{1,0:T(8,128)(2,1)S(1)} %bitcast.48), custom_call_target="tpu_custom_call" | custom-call | tf_op jit(solution)/shard_map/temporal/pallas_call | solution.py:103
  79.5 1.9 %collective-permute-start.8 = (bf16[512,384]{1,0:T(8,128)(2,1)S(1)}, bf16[512,384]{1,0:T(8,128)(2,1)S(1)}, u32[]{:S(2)}, u32[]{:S(2)}) collective-permute-start(bf16[512,384]{1,0:T(8,128)(2,1)S(1)} %pad_maximum_fusion.1.refs_5_), channel_id=1, source_target_pairs={{0,8},{8,0},{1,9},{9,1},{2,10},{10,2},{3,11},{11,3},{4,12},{12,4},... | collective-permute-start | bytes 1179656 | tf_op jit(solution)/shard_map/ppermute | solution.py:25
  81.4 0.1 add_multiply_fusion
  81.5 7.4 %all-to-all-start.1 = ((bf16[8,32,384]{2,1,0:T(8,128)(2,1)}), bf16[8,32,384]{2,1,0:T(8,128)(2,1)S(1)}, u32[]{:S(2)}, u32[]{:S(2)}) async-start(bf16[8,32,384]{2,1,0:T(8,128)(2,1)} %bitcast.20), calls=%async_computation.1 | async-start | bytes 393216 | tf_op jit(solution)/shard_map/all_to_all | solution.py:247
  88.8 0.1 compare_select_fusion.3
  89.1 0.6 spatial.2
  89.7 2.7 %collective-permute-start.9 = (bf16[400,256]{1,0:T(8,128)(2,1)S(1)}, bf16[400,256]{1,0:T(8,128)(2,1)S(1)}, u32[]{:S(2)}, u32[]{:S(2)}) collective-permute-start(bf16[400,256]{1,0:T(8,128)(2,1)S(1)} %get-tuple-element.23.refs_8_), channel_id=1, source_target_pairs={{0,320},{64,256},{128,448},{192,384},{256,64},{320,0},{384,192},{4... | collective-permute-start | bytes 614408 | tf_op jit(solution)/shard_map/ppermute | solution.py:193
  92.4 4.9 %collective-permute-start.10 = (bf16[400,256]{1,0:T(8,128)(2,1)S(1)}, bf16[400,256]{1,0:T(8,128)(2,1)S(1)}, u32[]{:S(2)}, u32[]{:S(2)}) collective-permute-start(bf16[400,256]{1,0:T(8,128)(2,1)S(1)} %get-tuple-element.24), channel_id=1, source_target_pairs={{0,192},{64,384},{128,320},{192,0},{256,448},{320,128},{384,64},{4... | collective-permute-start | bytes 614408 | tf_op jit(solution)/shard_map/ppermute | solution.py:193
  97.3 3.5 %collective-permute-start.11 = (bf16[400,256]{1,0:T(8,128)(2,1)S(1)}, bf16[400,256]{1,0:T(8,128)(2,1)S(1)}, u32[]{:S(2)}, u32[]{:S(2)}) collective-permute-start(bf16[400,256]{1,0:T(8,128)(2,1)S(1)} %get-tuple-element.25), channel_id=1, source_target_pairs={{0,448},{64,128},{128,64},{192,256},{256,192},{320,384},{384,320},... | collective-permute-start | bytes 614408 | tf_op jit(solution)/shard_map/ppermute | solution.py:193
  100.8 0.6 spatial.3.p3_ref
  101.4 2.8 %collective-permute-done.9.p0_ref = bf16[400,256]{1,0:T(8,128)(2,1)S(1)} collective-permute-done((bf16[400,256]{1,0:T(8,128)(2,1)S(1)}, bf16[400,256]{1,0:T(8,128)(2,1)S(1)}, u32[]{:S(2)}, u32[]{:S(2)}) %collective-permute-start.9) | collective-permute-done | bytes 204832 | tf_op jit(solution)/shard_map/ppermute | solution.py:193
  104.2 6.3 %collective-permute-done.10.p1_ref = bf16[400,256]{1,0:T(8,128)(2,1)S(1)} collective-permute-done((bf16[400,256]{1,0:T(8,128)(2,1)S(1)}, bf16[400,256]{1,0:T(8,128)(2,1)S(1)}, u32[]{:S(2)}, u32[]{:S(2)}) %collective-permute-start.10) | collective-permute-done | bytes 204832 | tf_op jit(solution)/shard_map/ppermute | solution.py:193
  110.5 4.5 %collective-permute-done.11.p2_ref = bf16[400,256]{1,0:T(8,128)(2,1)S(1)} collective-permute-done((bf16[400,256]{1,0:T(8,128)(2,1)S(1)}, bf16[400,256]{1,0:T(8,128)(2,1)S(1)}, u32[]{:S(2)}, u32[]{:S(2)}) %collective-permute-start.11) | collective-permute-done | bytes 204832 | tf_op jit(solution)/shard_map/ppermute | solution.py:193
  115.0 0.6 combine.1
  115.6 13.3 %all-gather = bf16[1024,384]{1,0:T(8,128)(2,1)S(1)} all-gather(bf16[256,384]{1,0:T(8,128)(2,1)S(1)} %combine.1), channel_id=2, replica_groups=mesh['a'=4,'b'=2,'z'=4,'c'=2,'w'=2,'x'=4] {'x'}, dimensions={0}, use_global_device_ids=true | all-gather | bytes 983040 | tf_op jit(solution)/shard_map/all_gather | solution.py:255
  128.9 0.1 all-gather.3.cloned.1.call-done.weight_ref
  129.0 3.1 %project.2.rest_0_ = bf16[256,640]{1,0:T(8,128)(2,1)S(1)} custom-call(s32[2]{0:T(128)S(1)} %get-tuple-element.38.at_ref, bf16[4,256,384]{2,1,0:T(8,128)(2,1)S(1)} %bitcast.43, bf16[8,8,80,384]{3,2,1,0:T(8,128)(2,1)} %all-gather.3.cloned.1.call-done.weight_ref), custom_call_target="tpu_custom_call" | custom-call | tf_op jit(solution)/shard_map/project/pallas_call | solution.py:168
  132.1 8.8 %collective-permute-start.12 = (bf16[256,640]{1,0:T(8,128)(2,1)S(1)}, bf16[256,640]{1,0:T(8,128)(2,1)S(1)}, u32[]{:S(2)}, u32[]{:S(2)}) collective-permute-start(bf16[256,640]{1,0:T(8,128)(2,1)S(1)} %project.2.rest_0_), channel_id=1, source_target_pairs={{0,4},{4,0},{1,5},{5,1},{2,6},{6,2},{3,7},{7,3},{8,12},{12,8},{9,1... | collective-permute-start | bytes 983048 | tf_op jit(solution)/shard_map/ppermute | solution.py:25
  140.9 3.1 %project.3 = f32[256,640]{1,0:T(8,128)S(1)} custom-call(s32[2]{0:T(128)S(1)} %get-tuple-element.39.at_ref, bf16[4,256,384]{2,1,0:T(8,128)(2,1)S(1)} %bitcast.44, bf16[8,8,80,384]{3,2,1,0:T(8,128)(2,1)} %all-gather.3.cloned.1.call-done.weight_ref, bf16[256,640]{1,0:T(8,128)(2,1)S(1)} %project.2.rest_0_), custom_call_target="tpu_custom_call" | custom-call | tf_op jit(solution)/shard_map/project/pallas_call | solution.py:168
  144.0 8.4 %collective-permute-done.12 = bf16[256,640]{1,0:T(8,128)(2,1)S(1)} collective-permute-done((bf16[256,640]{1,0:T(8,128)(2,1)S(1)}, bf16[256,640]{1,0:T(8,128)(2,1)S(1)}, u32[]{:S(2)}, u32[]{:S(2)}) %collective-permute-start.12) | collective-permute-done | bytes 327712 | tf_op jit(solution)/shard_map/ppermute | solution.py:25
  152.4 0.8 add_convert_fusion
  (46 shorter events, 0.5 us)
Async XLA Ops:
  6.5 13.5 %copy-start = (bf16[256,384]{1,0:T(8,128)(2,1)S(1)}, bf16[256,384]{1,0:T(8,128)(2,1)}, u32[]{:S(2)}) copy-start(bf16[256,384]{1,0:T(8,128)(2,1)} %refs_2_.3) | copy-start | bytes 589828
  6.5 13.5 %copy-start.1 = (bf16[256,384]{1,0:T(8,128)(2,1)S(1)}, bf16[256,384]{1,0:T(8,128)(2,1)}, u32[]{:S(2)}) copy-start(bf16[256,384]{1,0:T(8,128)(2,1)} %refs_3_.3) | copy-start | bytes 589828
  7.6 8.8 %collective-permute-start = (bf16[256,384]{1,0:T(8,128)(2,1)S(1)}, bf16[256,384]{1,0:T(8,128)(2,1)S(1)}, u32[]{:S(2)}, u32[]{:S(2)}) collective-permute-start(bf16[256,384]{1,0:T(8,128)(2,1)S(1)} %broadcast_select_fusion.1), channel_id=1, source_target_pairs={{0,8},{8,0},{1,9},{9,1},{2,10},{10,2},{3,11},{11,3},{4,12},{12,4},... | collective-permute-start | bytes 589832 | tf_op jit(solution)/shard_map/ppermute | solution.py:25
  9.5 10.5 %collective-permute-start.1 = (bf16[80,384]{1,0:T(8,128)(2,1)}, bf16[80,384]{1,0:T(8,128)(2,1)S(1)}, u32[]{:S(2)}, u32[]{:S(2)}) collective-permute-start(bf16[80,384]{1,0:T(8,128)(2,1)} %bitcast.54), channel_id=1, source_target_pairs={{0,0},{1,64},{2,128},{3,192},{64,1},{65,65},{66,129},{67,193},{128... | collective-permute-start | bytes 184328 | tf_op jit(solution)/shard_map/ppermute | solution.py:206
  19.6 14.7 %copy-start.2 = (bf16[256,384]{1,0:T(8,128)(2,1)S(1)}, bf16[256,384]{1,0:T(8,128)(2,1)}, u32[]{:S(2)}) copy-start(bf16[256,384]{1,0:T(8,128)(2,1)} %refs_7_.1) | copy-start | bytes 589828
  20.1 14.2 %collective-permute-start.2 = (bf16[592,384]{1,0:T(8,128)(2,1)S(1)}, bf16[592,384]{1,0:T(8,128)(2,1)S(1)}, u32[]{:S(2)}, u32[]{:S(2)}) collective-permute-start(bf16[592,384]{1,0:T(8,128)(2,1)S(1)} %pad_maximum_fusion), channel_id=1, source_target_pairs={{0,64},{64,0},{1,65},{65,1},{2,66},{66,2},{3,67},{67,3},{4,68},{68... | collective-permute-start | bytes 1363976 | tf_op jit(solution)/shard_map/ppermute | solution.py:25
  23.2 44.2 %all-to-all-start = ((bf16[4,256,384]{2,1,0:T(8,128)(2,1)}), bf16[4,256,384]{2,1,0:T(8,128)(2,1)S(1)}, u32[]{:S(2)}, u32[]{:S(2)}) async-start(bf16[4,256,384]{2,1,0:T(8,128)(2,1)} %maximum_select_fusion), calls=%async_computation | async-start | bytes 1572864 | tf_op jit(solution)/shard_map/all_to_all | solution.py:219
  30.5 98.5 %all-gather.3.cloned.1.call-start = ((), (), s32[]{:S(2)}) async-start(), calls=%async_computation.2 | async-start | bytes 4423680 | tf_op jit(solution)/shard_map/all_gather | solution.py:231
  34.3 36.5 %copy-start.5 = (bf16[592,384]{1,0:T(8,128)(2,1)}, bf16[592,384]{1,0:T(8,128)(2,1)S(1)}, u32[]{:S(2)}) copy-start(bf16[592,384]{1,0:T(8,128)(2,1)S(1)} %collective-permute-done.2) | copy-start | bytes 1363972
  34.4 27.9 %collective-permute-start.3 = (bf16[416,384]{1,0:T(8,128)(2,1)S(1)}, bf16[416,384]{1,0:T(8,128)(2,1)S(1)}, u32[]{:S(2)}, u32[]{:S(2)}) collective-permute-start(bf16[416,384]{1,0:T(8,128)(2,1)S(1)} %pad_maximum_fusion.2), channel_id=1, source_target_pairs={{0,320},{64,256},{128,448},{192,384},{256,64},{320,0},{384,192},{4... | collective-permute-start | bytes 958472 | tf_op jit(solution)/shard_map/ppermute | solution.py:193
  40.6 25.5 %collective-permute-start.4 = (bf16[416,384]{1,0:T(8,128)(2,1)S(1)}, bf16[416,384]{1,0:T(8,128)(2,1)S(1)}, u32[]{:S(2)}, u32[]{:S(2)}) collective-permute-start(bf16[416,384]{1,0:T(8,128)(2,1)S(1)} %pad_maximum_fusion.2), channel_id=1, source_target_pairs={{0,192},{64,384},{128,320},{192,0},{256,448},{320,128},{384,64},{4... | collective-permute-start | bytes 958472 | tf_op jit(solution)/shard_map/ppermute | solution.py:193
  42.5 24.9 %collective-permute-start.5 = (bf16[416,384]{1,0:T(8,128)(2,1)S(1)}, bf16[416,384]{1,0:T(8,128)(2,1)S(1)}, u32[]{:S(2)}, u32[]{:S(2)}) collective-permute-start(bf16[416,384]{1,0:T(8,128)(2,1)S(1)} %pad_maximum_fusion.2), channel_id=1, source_target_pairs={{0,448},{64,128},{128,64},{192,256},{256,192},{320,384},{384,320},... | collective-permute-start | bytes 958472 | tf_op jit(solution)/shard_map/ppermute | solution.py:193
  62.3 8.6 %copy-start.7 = (bf16[416,384]{1,0:T(8,128)(2,1)}, bf16[416,384]{1,0:T(8,128)(2,1)S(1)}, u32[]{:S(2)}) copy-start(bf16[416,384]{1,0:T(8,128)(2,1)S(1)} %collective-permute-done.3) | copy-start | bytes 958468
  66.1 2.3 %copy-start.9 = (bf16[416,384]{1,0:T(8,128)(2,1)}, bf16[416,384]{1,0:T(8,128)(2,1)S(1)}, u32[]{:S(2)}) copy-start(bf16[416,384]{1,0:T(8,128)(2,1)S(1)} %collective-permute-done.4) | copy-start | bytes 958468
  67.4 1.0 copy-start.11
  67.5 0.8 copy-start.4
  68.4 8.3 %collective-permute-start.6 = (bf16[256,384]{1,0:T(8,128)(2,1)S(1)}, bf16[256,384]{1,0:T(8,128)(2,1)S(1)}, u32[]{:S(2)}, u32[]{:S(2)}) collective-permute-start(bf16[256,384]{1,0:T(8,128)(2,1)S(1)} %dynamic-slice_bitcast_fusion), channel_id=1, source_target_pairs={{0,64},{64,0},{1,65},{65,1},{2,66},{66,2},{3,67},{67,3},{4,68},{68... | collective-permute-start | bytes 589832 | tf_op jit(solution)/shard_map/ppermute | solution.py:25
  70.9 6.1 %copy-start.3 = (s32[3]{0:T(128)S(1)}, s32[3]{0:T(128)}, u32[]{:S(2)}) copy-start(s32[3]{0:T(128)} %hc_ref.3) | copy-start | bytes 40
  70.9 5.9 %collective-permute-start.7 = (bf16[4,3,32,384]{3,2,0,1:T(8,128)(2,1)S(1)}, bf16[4,3,32,384]{3,2,0,1:T(8,128)(2,1)S(1)}, u32[]{:S(2)}, u32[]{:S(2)}) collective-permute-start(bf16[4,3,32,384]{3,2,0,1:T(8,128)(2,1)S(1)} %select_bitcast_fusion), channel_id=1, source_target_pairs={{0,8},{8,0},{1,9},{9,1},{2,10},{10,2},{3,11},{11,3},{4,12},{12,4},... | collective-permute-start | bytes 884744 | tf_op jit(solution)/shard_map/ppermute | solution.py:25
  76.8 12.2 %copy-start.6 = (bf16[592,384]{1,0:T(8,128)(2,1)S(1)}, bf16[592,384]{1,0:T(8,128)(2,1)}, u32[]{:S(2)}) copy-start(bf16[592,384]{1,0:T(8,128)(2,1)} %copy-done.5) | copy-start | bytes 1363972
  76.9 12.1 %copy-start.8 = (bf16[416,384]{1,0:T(8,128)(2,1)S(1)}, bf16[416,384]{1,0:T(8,128)(2,1)}, u32[]{:S(2)}) copy-start(bf16[416,384]{1,0:T(8,128)(2,1)} %copy-done.7) | copy-start | bytes 958468
  76.9 12.2 %copy-start.10 = (bf16[416,384]{1,0:T(8,128)(2,1)S(1)}, bf16[416,384]{1,0:T(8,128)(2,1)}, u32[]{:S(2)}) copy-start(bf16[416,384]{1,0:T(8,128)(2,1)} %copy-done.9) | copy-start | bytes 958468
  77.0 12.1 %copy-start.12 = (bf16[416,384]{1,0:T(8,128)(2,1)S(1)}, bf16[416,384]{1,0:T(8,128)(2,1)}, u32[]{:S(2)}) copy-start(bf16[416,384]{1,0:T(8,128)(2,1)} %copy-done.11) | copy-start | bytes 958468
  79.5 9.6 %collective-permute-start.8 = (bf16[512,384]{1,0:T(8,128)(2,1)S(1)}, bf16[512,384]{1,0:T(8,128)(2,1)S(1)}, u32[]{:S(2)}, u32[]{:S(2)}) collective-permute-start(bf16[512,384]{1,0:T(8,128)(2,1)S(1)} %pad_maximum_fusion.1.refs_5_), channel_id=1, source_target_pairs={{0,8},{8,0},{1,9},{9,1},{2,10},{10,2},{3,11},{11,3},{4,12},{12,4},... | collective-permute-start | bytes 1179656 | tf_op jit(solution)/shard_map/ppermute | solution.py:25
  81.5 19.9 %all-to-all-start.1 = ((bf16[8,32,384]{2,1,0:T(8,128)(2,1)}), bf16[8,32,384]{2,1,0:T(8,128)(2,1)S(1)}, u32[]{:S(2)}, u32[]{:S(2)}) async-start(bf16[8,32,384]{2,1,0:T(8,128)(2,1)} %bitcast.20), calls=%async_computation.1 | async-start | bytes 393216 | tf_op jit(solution)/shard_map/all_to_all | solution.py:247
  89.7 14.5 %collective-permute-start.9 = (bf16[400,256]{1,0:T(8,128)(2,1)S(1)}, bf16[400,256]{1,0:T(8,128)(2,1)S(1)}, u32[]{:S(2)}, u32[]{:S(2)}) collective-permute-start(bf16[400,256]{1,0:T(8,128)(2,1)S(1)} %get-tuple-element.23.refs_8_), channel_id=1, source_target_pairs={{0,320},{64,256},{128,448},{192,384},{256,64},{320,0},{384,192},{4... | collective-permute-start | bytes 614408 | tf_op jit(solution)/shard_map/ppermute | solution.py:193
  92.4 18.0 %collective-permute-start.10 = (bf16[400,256]{1,0:T(8,128)(2,1)S(1)}, bf16[400,256]{1,0:T(8,128)(2,1)S(1)}, u32[]{:S(2)}, u32[]{:S(2)}) collective-permute-start(bf16[400,256]{1,0:T(8,128)(2,1)S(1)} %get-tuple-element.24), channel_id=1, source_target_pairs={{0,192},{64,384},{128,320},{192,0},{256,448},{320,128},{384,64},{4... | collective-permute-start | bytes 614408 | tf_op jit(solution)/shard_map/ppermute | solution.py:193
  97.3 17.7 %collective-permute-start.11 = (bf16[400,256]{1,0:T(8,128)(2,1)S(1)}, bf16[400,256]{1,0:T(8,128)(2,1)S(1)}, u32[]{:S(2)}, u32[]{:S(2)}) collective-permute-start(bf16[400,256]{1,0:T(8,128)(2,1)S(1)} %get-tuple-element.25), channel_id=1, source_target_pairs={{0,448},{64,128},{128,64},{192,256},{256,192},{320,384},{384,320},... | collective-permute-start | bytes 614408 | tf_op jit(solution)/shard_map/ppermute | solution.py:193
  132.1 20.4 %collective-permute-start.12 = (bf16[256,640]{1,0:T(8,128)(2,1)S(1)}, bf16[256,640]{1,0:T(8,128)(2,1)S(1)}, u32[]{:S(2)}, u32[]{:S(2)}) collective-permute-start(bf16[256,640]{1,0:T(8,128)(2,1)S(1)} %project.2.rest_0_), channel_id=1, source_target_pairs={{0,4},{4,0},{1,5},{5,1},{2,6},{6,2},{3,7},{7,3},{8,12},{12,8},{9,1... | collective-permute-start | bytes 983048 | tf_op jit(solution)/shard_map/ppermute | solution.py:25
Sparse Core Ops, SparseCore 0:
  68.5 60.4 all-gather.2

commit v5 on v3

--- a/solution.py
+++ b/solution.py
@@ -233,7 +233,6 @@
     both = jnp.stack([first, second], axis=1)
     tq, tk, tv = (both[:, :, i].reshape(rows, width) for i in range(3))
     back = temporal(head_class, tq, tk, tv)
-    sink_pair, back = lax.optimization_barrier((sink_pair, back))
     sink_other = swap(sink_pair, "c")
     back = lax.all_to_all(back.reshape(8, half, width), ("z", "c"), 0, 0, tiled=True).reshape(rows, width)
 

time: 165 us -> 166 us (level)
  the two profiles are of different devices: /device:TPU:72 before, /device:TPU:6 now
where the time goes in v5:
time: 166 us; the launch traced here: 165 us
  starting transfers between devices  62.8 us (38%)
  waiting for transfers between devices  48.5 us (29%)
  Pallas kernels  18 us (11%)
  between operations  14.5 us (9%)
  blocking collectives  14 us (8%)
  other arithmetic  6.19 us (4%)
    ppermute x6, waiting for transfers between devices, mirrored(): lax.ppermute(x, ('a', 'b'), [(y, (y + (by if y % 2 == 0 else -by)) % 8) f...  32.1 us
    ppermute x6, starting transfers between devices, mirrored(): lax.ppermute(x, ('a', 'b'), [(y, (y + (by if y % 2 == 0 else -by)) % 8) f...  23.3 us
    ppermute x6, starting transfers between devices, swap(): return lax.ppermute(x, axis, [(0, 1), (1, 0)])  19.5 us
    ppermute x6, waiting for transfers between devices, swap(): return lax.ppermute(x, axis, [(0, 1), (1, 0)])  15.9 us
    all_gather x1, blocking collectives, per_device(): everyone = lax.all_gather(attended, 'x', axis=0)  14 us
    pallas_call x2, Pallas kernels, spatial(): pl.pallas_call(body, out_shape=[shape] * count, in_specs=[smem] * 2 + [vm...  9.63 us
    all_to_all x1, starting transfers between devices, per_device(): lax.all_to_all(back.reshape(8, half, width), ('z', 'c'), 0, 0, tiled=True)  7.37 us
    all_to_all x1, starting transfers between devices, per_device(): got = lax.all_to_all(sent, 'z', 0, 0, tiled=True)  7.27 us
  transfers between devices with their start and end apart: 16, of which 10 were waited for; matrix products, arithmetic and copies ran while one was open for 3% of the time, Pallas kernels for 9%

profile of v5, /device:TPU:6, one launch (start us, length us, event | category | flops | bytes accessed | tf_op | source)
XLA Modules:
  0.0 165.3 jit_solution(11912203132385432244)
XLA Ops:
  6.5 1.0 broadcast_select_fusion
  7.6 1.9 %collective-permute-start = (bf16[256,384]{1,0:T(8,128)(2,1)S(1)}, bf16[256,384]{1,0:T(8,128)(2,1)S(1)}, u32[]{:S(2)}, u32[]{:S(2)}) collective-permute-start(bf16[256,384]{1,0:T(8,128)(2,1)S(1)} %broadcast_select_fusion), channel_id=1, source_target_pairs={{0,8},{8,0},{1,9},{9,1},{2,10},{10,2},{3,11},{11,3},{4,12},{12,4},... | collective-permute-start | bytes 589832 | tf_op jit(solution)/shard_map/ppermute | solution.py:25
  9.5 5.4 %collective-permute-start.1 = (bf16[80,384]{1,0:T(8,128)(2,1)}, bf16[80,384]{1,0:T(8,128)(2,1)S(1)}, u32[]{:S(2)}, u32[]{:S(2)}) collective-permute-start(bf16[80,384]{1,0:T(8,128)(2,1)} %bitcast.72), channel_id=1, source_target_pairs={{0,0},{1,64},{2,128},{3,192},{64,1},{65,65},{66,129},{67,193},{128... | collective-permute-start | bytes 184328 | tf_op jit(solution)/shard_map/ppermute | solution.py:197
  15.6 0.7 broadcast_compare_fusion
  16.3 0.1 pad.13.clone
  16.3 0.1 broadcast_bitcast_fusion
  16.4 0.0 collective-permute-done
  16.4 1.0 select_select_fusion
  17.4 2.2 %maximum_select_fusion = bf16[4,256,384]{2,1,0:T(8,128)(2,1)} fusion(bf16[4,64,384]{2,1,0:T(8,128)(2,1)} %bitcast.63, bf16[4,64,384]{2,1,0:T(8,128)(2,1)} %bitcast.62, bf16[4,64,384]{2,1,0:T(8,128)(2,1)} %bitcast.64, pred[384]{0:T(512)(128)(4,1)S(1)} %broadcast_bitcast_fusion, bf16[256]{0:T(256)(128)(2,1)S(1)} %pad.13.clone, ...), kind=kLoop, calls=%fused_computation | loop fusion | flops 3538944 | bytes 1573760 | tf_op jit(solution)/shard_map/jit(_where)/select_n | solution.py:207
  19.6 0.4 collective-permute-done.1
  20.1 3.2 %collective-permute-start.2 = (bf16[592,384]{1,0:T(8,128)(2,1)S(1)}, bf16[592,384]{1,0:T(8,128)(2,1)S(1)}, u32[]{:S(2)}, u32[]{:S(2)}) collective-permute-start(bf16[592,384]{1,0:T(8,128)(2,1)S(1)} %pad_maximum_fusion), channel_id=1, source_target_pairs={{0,64},{64,0},{1,65},{65,1},{2,66},{66,2},{3,67},{67,3},{4,68},{68... | collective-permute-start | bytes 1363976 | tf_op jit(solution)/shard_map/ppermute | solution.py:25
  23.2 7.3 %all-to-all-start = ((bf16[4,256,384]{2,1,0:T(8,128)(2,1)}), bf16[4,256,384]{2,1,0:T(8,128)(2,1)S(1)}, u32[]{:S(2)}, u32[]{:S(2)}) async-start(bf16[4,256,384]{2,1,0:T(8,128)(2,1)} %maximum_select_fusion), calls=%async_computation | async-start | bytes 1572864 | tf_op jit(solution)/shard_map/all_to_all | solution.py:210
  30.5 3.8 %collective-permute-done.2 = bf16[592,384]{1,0:T(8,128)(2,1)S(1)} collective-permute-done((bf16[592,384]{1,0:T(8,128)(2,1)S(1)}, bf16[592,384]{1,0:T(8,128)(2,1)S(1)}, u32[]{:S(2)}, u32[]{:S(2)}) %collective-permute-start.2) | collective-permute-done | bytes 454688 | tf_op jit(solution)/shard_map/ppermute | solution.py:25
  34.4 6.2 %collective-permute-start.3 = (bf16[416,384]{1,0:T(8,128)(2,1)S(1)}, bf16[416,384]{1,0:T(8,128)(2,1)S(1)}, u32[]{:S(2)}, u32[]{:S(2)}) collective-permute-start(bf16[416,384]{1,0:T(8,128)(2,1)S(1)} %pad_maximum_fusion.2), channel_id=1, source_target_pairs={{0,320},{64,256},{128,448},{192,384},{256,64},{320,0},{384,192},{4... | collective-permute-start | bytes 958472 | tf_op jit(solution)/shard_map/ppermute | solution.py:184
  40.6 1.9 %collective-permute-start.4 = (bf16[416,384]{1,0:T(8,128)(2,1)S(1)}, bf16[416,384]{1,0:T(8,128)(2,1)S(1)}, u32[]{:S(2)}, u32[]{:S(2)}) collective-permute-start(bf16[416,384]{1,0:T(8,128)(2,1)S(1)} %pad_maximum_fusion.2), channel_id=1, source_target_pairs={{0,192},{64,384},{128,320},{192,0},{256,448},{320,128},{384,64},{4... | collective-permute-start | bytes 958472 | tf_op jit(solution)/shard_map/ppermute | solution.py:184
  42.5 4.1 %collective-permute-start.5 = (bf16[416,384]{1,0:T(8,128)(2,1)S(1)}, bf16[416,384]{1,0:T(8,128)(2,1)S(1)}, u32[]{:S(2)}, u32[]{:S(2)}) collective-permute-start(bf16[416,384]{1,0:T(8,128)(2,1)S(1)} %pad_maximum_fusion.2), channel_id=1, source_target_pairs={{0,448},{64,128},{128,64},{192,256},{256,192},{320,384},{384,320},... | collective-permute-start | bytes 958472 | tf_op jit(solution)/shard_map/ppermute | solution.py:184
  46.7 15.6 %collective-permute-done.3 = bf16[416,384]{1,0:T(8,128)(2,1)S(1)} collective-permute-done((bf16[416,384]{1,0:T(8,128)(2,1)S(1)}, bf16[416,384]{1,0:T(8,128)(2,1)S(1)}, u32[]{:S(2)}, u32[]{:S(2)}) %collective-permute-start.3) | collective-permute-done | bytes 319520 | tf_op jit(solution)/shard_map/ppermute | solution.py:184
  62.3 3.8 %collective-permute-done.4 = bf16[416,384]{1,0:T(8,128)(2,1)S(1)} collective-permute-done((bf16[416,384]{1,0:T(8,128)(2,1)S(1)}, bf16[416,384]{1,0:T(8,128)(2,1)S(1)}, u32[]{:S(2)}, u32[]{:S(2)}) %collective-permute-start.4) | collective-permute-done | bytes 319520 | tf_op jit(solution)/shard_map/ppermute | solution.py:184
  66.1 1.4 collective-permute-done.5
  67.5 0.8 copy-done.4
  68.3 0.0 all-gather.3.cloned.1.call-update
  68.4 2.3 %collective-permute-start.6 = (bf16[256,384]{1,0:T(8,128)(2,1)S(1)}, bf16[256,384]{1,0:T(8,128)(2,1)S(1)}, u32[]{:S(2)}, u32[]{:S(2)}) collective-permute-start(bf16[256,384]{1,0:T(8,128)(2,1)S(1)} %dynamic-slice_bitcast_fusion), channel_id=1, source_target_pairs={{0,64},{64,0},{1,65},{65,1},{2,66},{66,2},{3,67},{67,3},{4,68},{68... | collective-permute-start | bytes 589832 | tf_op jit(solution)/shard_map/ppermute | solution.py:25
  70.8 1.9 %collective-permute-start.11 = (bf16[4,3,32,384]{3,2,1,0:T(8,128)(2,1)S(1)}, bf16[4,3,32,384]{3,2,1,0:T(8,128)(2,1)S(1)}, u32[]{:S(2)}, u32[]{:S(2)}) collective-permute-start(bf16[4,3,32,384]{3,2,1,0:T(8,128)(2,1)S(1)} %fusion), channel_id=1, source_target_pairs={{0,8},{8,0},{1,9},{9,1},{2,10},{10,2},{3,11},{11,3},{4,12},{12,4},... | collective-permute-start | bytes 884744 | tf_op jit(solution)/shard_map/ppermute | solution.py:25
  72.7 0.1 add_multiply_fusion
  72.8 3.9 %collective-permute-done.6 = bf16[256,384]{1,0:T(8,128)(2,1)S(1)} collective-permute-done((bf16[256,384]{1,0:T(8,128)(2,1)S(1)}, bf16[256,384]{1,0:T(8,128)(2,1)S(1)}, u32[]{:S(2)}, u32[]{:S(2)}) %collective-permute-start.6) | collective-permute-done | bytes 196640 | tf_op jit(solution)/shard_map/ppermute | solution.py:25
  76.7 0.0 copy-start.3
  76.7 1.9 %collective-permute-start.7 = (bf16[512,384]{1,0:T(8,128)(2,1)S(1)}, bf16[512,384]{1,0:T(8,128)(2,1)S(1)}, u32[]{:S(2)}, u32[]{:S(2)}) collective-permute-start(bf16[512,384]{1,0:T(8,128)(2,1)S(1)} %pad_maximum_fusion.1.refs_5_), channel_id=1, source_target_pairs={{0,8},{8,0},{1,9},{9,1},{2,10},{10,2},{3,11},{11,3},{4,12},{12,4},... | collective-permute-start | bytes 1179656 | tf_op jit(solution)/shard_map/ppermute | solution.py:25
  78.7 0.1 select_bitcast_fusion
  78.8 0.1 pad_maximum_fusion.3
  78.8 0.0 copy-start.8
  79.0 1.3 temporal.1
  80.2 7.4 %all-to-all-start.1 = ((bf16[8,32,384]{2,1,0:T(8,128)(2,1)}), bf16[8,32,384]{2,1,0:T(8,128)(2,1)S(1)}, u32[]{:S(2)}, u32[]{:S(2)}) async-start(bf16[8,32,384]{2,1,0:T(8,128)(2,1)} %bitcast.22), calls=%async_computation.1 | async-start | bytes 393216 | tf_op jit(solution)/shard_map/all_to_all | solution.py:237
  87.6 0.1 compare_select_fusion.3
  87.9 6.8 %spatial.2 = (bf16[400,256]{1,0:T(8,128)(2,1)S(1)}, bf16[400,256]{1,0:T(8,128)(2,1)S(1)}, bf16[400,256]{1,0:T(8,128)(2,1)S(1)}) custom-call(s32[3]{0:T(128)S(1)} %copy-done.3, s32[1]{0:T(128)} %bitcast.3.refs_1_, bf16[256,384]{1,0:T(8,128)(2,1)S(1)} %copy-done, bf16[256,384]{1,0:T(8,128)(2,1)S(1)} %copy-done.1, bf16[512,384]{1,0:T(8,128)(2,1)S(1)} %slice.65.refs_4_, ...), custom_call_target="tpu_custom_call" | custom-call | tf_op jit(solution)/shard_map/spatial/pallas_call | solution.py:71
  94.7 2.8 %collective-permute-start.8 = (bf16[400,256]{1,0:T(8,128)(2,1)S(1)}, bf16[400,256]{1,0:T(8,128)(2,1)S(1)}, u32[]{:S(2)}, u32[]{:S(2)}) collective-permute-start(bf16[400,256]{1,0:T(8,128)(2,1)S(1)} %get-tuple-element.20.refs_8_), channel_id=1, source_target_pairs={{0,320},{64,256},{128,448},{192,384},{256,64},{320,0},{384,192},{4... | collective-permute-start | bytes 614408 | tf_op jit(solution)/shard_map/ppermute | solution.py:184
  97.4 4.9 %collective-permute-start.9 = (bf16[400,256]{1,0:T(8,128)(2,1)S(1)}, bf16[400,256]{1,0:T(8,128)(2,1)S(1)}, u32[]{:S(2)}, u32[]{:S(2)}) collective-permute-start(bf16[400,256]{1,0:T(8,128)(2,1)S(1)} %get-tuple-element.21), channel_id=1, source_target_pairs={{0,192},{64,384},{128,320},{192,0},{256,448},{320,128},{384,64},{4... | collective-permute-start | bytes 614408 | tf_op jit(solution)/shard_map/ppermute | solution.py:184
  102.3 3.4 %collective-permute-start.10 = (bf16[400,256]{1,0:T(8,128)(2,1)S(1)}, bf16[400,256]{1,0:T(8,128)(2,1)S(1)}, u32[]{:S(2)}, u32[]{:S(2)}) collective-permute-start(bf16[400,256]{1,0:T(8,128)(2,1)S(1)} %get-tuple-element.22), channel_id=1, source_target_pairs={{0,448},{64,128},{128,64},{192,256},{256,192},{320,384},{384,320},... | collective-permute-start | bytes 614408 | tf_op jit(solution)/shard_map/ppermute | solution.py:184
  105.8 2.8 %spatial.3.p3_ref = bf16[400,256]{1,0:T(8,128)(2,1)S(1)} custom-call(s32[3]{0:T(128)S(1)} %copy-done.3, s32[1]{0:T(128)} %bitcast.3.refs_1_, bf16[256,384]{1,0:T(8,128)(2,1)S(1)} %copy-done, bf16[256,384]{1,0:T(8,128)(2,1)S(1)} %copy-done.1, bf16[512,384]{1,0:T(8,128)(2,1)S(1)} %slice.65.refs_4_, bf16[512,384]{1,0:T(8,128)(2,1)S(1)} %pad_maximum_fusion.1.refs_5_, ...), custom_call_target="tpu_custom_call" | custom-call | tf_op jit(solution)/shard_map/spatial/pallas_call | solution.py:71
  108.6 0.5 collective-permute-done.8.p0_ref
  109.1 6.3 %collective-permute-done.9.p1_ref = bf16[400,256]{1,0:T(8,128)(2,1)S(1)} collective-permute-done((bf16[400,256]{1,0:T(8,128)(2,1)S(1)}, bf16[400,256]{1,0:T(8,128)(2,1)S(1)}, u32[]{:S(2)}, u32[]{:S(2)}) %collective-permute-start.9) | collective-permute-done | bytes 204832 | tf_op jit(solution)/shard_map/ppermute | solution.py:184
  115.4 4.5 %collective-permute-done.10.p2_ref = bf16[400,256]{1,0:T(8,128)(2,1)S(1)} collective-permute-done((bf16[400,256]{1,0:T(8,128)(2,1)S(1)}, bf16[400,256]{1,0:T(8,128)(2,1)S(1)}, u32[]{:S(2)}, u32[]{:S(2)}) %collective-permute-start.10) | collective-permute-done | bytes 204832 | tf_op jit(solution)/shard_map/ppermute | solution.py:184
  119.9 1.0 combine.1
  121.0 14.0 %all-gather = bf16[1024,384]{1,0:T(8,128)(2,1)S(1)} all-gather(bf16[256,384]{1,0:T(8,128)(2,1)S(1)} %combine.1), channel_id=2, replica_groups=mesh['a'=4,'b'=2,'z'=4,'c'=2,'w'=2,'x'=4] {'x'}, dimensions={0}, use_global_device_ids=true | all-gather | bytes 983040 | tf_op jit(solution)/shard_map/all_gather | solution.py:245
  135.0 3.1 %project.2.rest_0_ = bf16[256,640]{1,0:T(8,128)(2,1)S(1)} custom-call(s32[2]{0:T(128)S(1)} %get-tuple-element.32.at_ref, bf16[4,256,384]{2,1,0:T(8,128)(2,1)S(1)} %bitcast.60, bf16[8,8,80,384]{3,2,1,0:T(8,128)(2,1)} %all-gather.3.cloned.1.call-done.low_ref.high_ref, bf16[8,8,80,384]{3,2,1,0:T(8,128)(2,1)} %all-gather.3.cloned.1.call-done.low_ref.high_ref), custom_call_target="tpu_custom_call" | custom-call | tf_op jit(solution)/shard_map/project/pallas_call | solution.py:159
  138.0 8.2 %collective-permute-start.12 = (bf16[256,640]{1,0:T(8,128)(2,1)S(1)}, bf16[256,640]{1,0:T(8,128)(2,1)S(1)}, u32[]{:S(2)}, u32[]{:S(2)}) collective-permute-start(bf16[256,640]{1,0:T(8,128)(2,1)S(1)} %project.2.rest_0_), channel_id=1, source_target_pairs={{0,4},{4,0},{1,5},{5,1},{2,6},{6,2},{3,7},{7,3},{8,12},{12,8},{9,1... | collective-permute-start | bytes 983048 | tf_op jit(solution)/shard_map/ppermute | solution.py:25
  146.3 3.1 %project.3 = f32[256,640]{1,0:T(8,128)S(1)} custom-call(s32[2]{0:T(128)S(1)} %get-tuple-element.33.at_ref, bf16[4,256,384]{2,1,0:T(8,128)(2,1)S(1)} %bitcast.61, bf16[8,8,80,384]{3,2,1,0:T(8,128)(2,1)} %all-gather.3.cloned.1.call-done.low_ref.high_ref, bf16[8,8,80,384]{3,2,1,0:T(8,128)(2,1)} %all-gather.3.cloned.1.call-done.low_ref.high_ref, ...), custom_call_target="tpu_custom_call" | custom-call | tf_op jit(solution)/shard_map/project/pallas_call | solution.py:159
  149.3 8.3 %collective-permute-done.12 = bf16[256,640]{1,0:T(8,128)(2,1)S(1)} collective-permute-done((bf16[256,640]{1,0:T(8,128)(2,1)S(1)}, bf16[256,640]{1,0:T(8,128)(2,1)S(1)}, u32[]{:S(2)}, u32[]{:S(2)}) %collective-permute-start.12) | collective-permute-done | bytes 327712 | tf_op jit(solution)/shard_map/ppermute | solution.py:25
  157.6 0.8 add_convert_fusion
  (44 shorter events, 0.5 us)
Async XLA Ops:
  6.5 13.5 %copy-start = (bf16[256,384]{1,0:T(8,128)(2,1)S(1)}, bf16[256,384]{1,0:T(8,128)(2,1)}, u32[]{:S(2)}) copy-start(bf16[256,384]{1,0:T(8,128)(2,1)} %refs_2_.3) | copy-start | bytes 589828
  6.5 13.5 %copy-start.1 = (bf16[256,384]{1,0:T(8,128)(2,1)S(1)}, bf16[256,384]{1,0:T(8,128)(2,1)}, u32[]{:S(2)}) copy-start(bf16[256,384]{1,0:T(8,128)(2,1)} %refs_3_.3) | copy-start | bytes 589828
  7.6 8.8 %collective-permute-start = (bf16[256,384]{1,0:T(8,128)(2,1)S(1)}, bf16[256,384]{1,0:T(8,128)(2,1)S(1)}, u32[]{:S(2)}, u32[]{:S(2)}) collective-permute-start(bf16[256,384]{1,0:T(8,128)(2,1)S(1)} %broadcast_select_fusion), channel_id=1, source_target_pairs={{0,8},{8,0},{1,9},{9,1},{2,10},{10,2},{3,11},{11,3},{4,12},{12,4},... | collective-permute-start | bytes 589832 | tf_op jit(solution)/shard_map/ppermute | solution.py:25
  9.5 10.5 %collective-permute-start.1 = (bf16[80,384]{1,0:T(8,128)(2,1)}, bf16[80,384]{1,0:T(8,128)(2,1)S(1)}, u32[]{:S(2)}, u32[]{:S(2)}) collective-permute-start(bf16[80,384]{1,0:T(8,128)(2,1)} %bitcast.72), channel_id=1, source_target_pairs={{0,0},{1,64},{2,128},{3,192},{64,1},{65,65},{66,129},{67,193},{128... | collective-permute-start | bytes 184328 | tf_op jit(solution)/shard_map/ppermute | solution.py:197
  19.6 14.7 %copy-start.2 = (bf16[256,384]{1,0:T(8,128)(2,1)S(1)}, bf16[256,384]{1,0:T(8,128)(2,1)}, u32[]{:S(2)}) copy-start(bf16[256,384]{1,0:T(8,128)(2,1)} %refs_7_.1) | copy-start | bytes 589828
  20.1 14.2 %collective-permute-start.2 = (bf16[592,384]{1,0:T(8,128)(2,1)S(1)}, bf16[592,384]{1,0:T(8,128)(2,1)S(1)}, u32[]{:S(2)}, u32[]{:S(2)}) collective-permute-start(bf16[592,384]{1,0:T(8,128)(2,1)S(1)} %pad_maximum_fusion), channel_id=1, source_target_pairs={{0,64},{64,0},{1,65},{65,1},{2,66},{66,2},{3,67},{67,3},{4,68},{68... | collective-permute-start | bytes 1363976 | tf_op jit(solution)/shard_map/ppermute | solution.py:25
  23.2 44.2 %all-to-all-start = ((bf16[4,256,384]{2,1,0:T(8,128)(2,1)}), bf16[4,256,384]{2,1,0:T(8,128)(2,1)S(1)}, u32[]{:S(2)}, u32[]{:S(2)}) async-start(bf16[4,256,384]{2,1,0:T(8,128)(2,1)} %maximum_select_fusion), calls=%async_computation | async-start | bytes 1572864 | tf_op jit(solution)/shard_map/all_to_all | solution.py:210
  30.5 104.5 %all-gather.3.cloned.1.call-start = ((), (), s32[]{:S(2)}) async-start(), calls=%async_computation.2 | async-start | bytes 4423680 | tf_op jit(solution)/shard_map/all_gather | solution.py:222
  34.3 36.5 %copy-start.5 = (bf16[592,384]{1,0:T(8,128)(2,1)}, bf16[592,384]{1,0:T(8,128)(2,1)S(1)}, u32[]{:S(2)}) copy-start(bf16[592,384]{1,0:T(8,128)(2,1)S(1)} %collective-permute-done.2) | copy-start | bytes 1363972
  34.4 27.9 %collective-permute-start.3 = (bf16[416,384]{1,0:T(8,128)(2,1)S(1)}, bf16[416,384]{1,0:T(8,128)(2,1)S(1)}, u32[]{:S(2)}, u32[]{:S(2)}) collective-permute-start(bf16[416,384]{1,0:T(8,128)(2,1)S(1)} %pad_maximum_fusion.2), channel_id=1, source_target_pairs={{0,320},{64,256},{128,448},{192,384},{256,64},{320,0},{384,192},{4... | collective-permute-start | bytes 958472 | tf_op jit(solution)/shard_map/ppermute | solution.py:184
  40.6 25.5 %collective-permute-start.4 = (bf16[416,384]{1,0:T(8,128)(2,1)S(1)}, bf16[416,384]{1,0:T(8,128)(2,1)S(1)}, u32[]{:S(2)}, u32[]{:S(2)}) collective-permute-start(bf16[416,384]{1,0:T(8,128)(2,1)S(1)} %pad_maximum_fusion.2), channel_id=1, source_target_pairs={{0,192},{64,384},{128,320},{192,0},{256,448},{320,128},{384,64},{4... | collective-permute-start | bytes 958472 | tf_op jit(solution)/shard_map/ppermute | solution.py:184
  42.5 24.9 %collective-permute-start.5 = (bf16[416,384]{1,0:T(8,128)(2,1)S(1)}, bf16[416,384]{1,0:T(8,128)(2,1)S(1)}, u32[]{:S(2)}, u32[]{:S(2)}) collective-permute-start(bf16[416,384]{1,0:T(8,128)(2,1)S(1)} %pad_maximum_fusion.2), channel_id=1, source_target_pairs={{0,448},{64,128},{128,64},{192,256},{256,192},{320,384},{384,320},... | collective-permute-start | bytes 958472 | tf_op jit(solution)/shard_map/ppermute | solution.py:184
  62.3 10.5 %copy-start.7 = (bf16[416,384]{1,0:T(8,128)(2,1)}, bf16[416,384]{1,0:T(8,128)(2,1)S(1)}, u32[]{:S(2)}) copy-start(bf16[416,384]{1,0:T(8,128)(2,1)S(1)} %collective-permute-done.3) | copy-start | bytes 958468
  66.1 2.3 %copy-start.9 = (bf16[416,384]{1,0:T(8,128)(2,1)}, bf16[416,384]{1,0:T(8,128)(2,1)S(1)}, u32[]{:S(2)}) copy-start(bf16[416,384]{1,0:T(8,128)(2,1)S(1)} %collective-permute-done.4) | copy-start | bytes 958468
  67.5 0.8 copy-start.4
  68.4 8.3 %collective-permute-start.6 = (bf16[256,384]{1,0:T(8,128)(2,1)S(1)}, bf16[256,384]{1,0:T(8,128)(2,1)S(1)}, u32[]{:S(2)}, u32[]{:S(2)}) collective-permute-start(bf16[256,384]{1,0:T(8,128)(2,1)S(1)} %dynamic-slice_bitcast_fusion), channel_id=1, source_target_pairs={{0,64},{64,0},{1,65},{65,1},{2,66},{66,2},{3,67},{67,3},{4,68},{68... | collective-permute-start | bytes 589832 | tf_op jit(solution)/shard_map/ppermute | solution.py:25
  70.8 7.9 %collective-permute-start.11 = (bf16[4,3,32,384]{3,2,1,0:T(8,128)(2,1)S(1)}, bf16[4,3,32,384]{3,2,1,0:T(8,128)(2,1)S(1)}, u32[]{:S(2)}, u32[]{:S(2)}) collective-permute-start(bf16[4,3,32,384]{3,2,1,0:T(8,128)(2,1)S(1)} %fusion), channel_id=1, source_target_pairs={{0,8},{8,0},{1,9},{9,1},{2,10},{10,2},{3,11},{11,3},{4,12},{12,4},... | collective-permute-start | bytes 884744 | tf_op jit(solution)/shard_map/ppermute | solution.py:25
  76.7 2.2 %copy-start.3 = (s32[3]{0:T(128)S(1)}, s32[3]{0:T(128)}, u32[]{:S(2)}) copy-start(s32[3]{0:T(128)} %hc_ref.3) | copy-start | bytes 40
  76.7 11.1 %collective-permute-start.7 = (bf16[512,384]{1,0:T(8,128)(2,1)S(1)}, bf16[512,384]{1,0:T(8,128)(2,1)S(1)}, u32[]{:S(2)}, u32[]{:S(2)}) collective-permute-start(bf16[512,384]{1,0:T(8,128)(2,1)S(1)} %pad_maximum_fusion.1.refs_5_), channel_id=1, source_target_pairs={{0,8},{8,0},{1,9},{9,1},{2,10},{10,2},{3,11},{11,3},{4,12},{12,4},... | collective-permute-start | bytes 1179656 | tf_op jit(solution)/shard_map/ppermute | solution.py:25
  78.8 8.9 %copy-start.6 = (bf16[592,384]{1,0:T(8,128)(2,1)S(1)}, bf16[592,384]{1,0:T(8,128)(2,1)}, u32[]{:S(2)}) copy-start(bf16[592,384]{1,0:T(8,128)(2,1)} %copy-done.5) | copy-start | bytes 1363972
  78.8 8.9 %copy-start.8 = (bf16[416,384]{1,0:T(8,128)(2,1)S(1)}, bf16[416,384]{1,0:T(8,128)(2,1)}, u32[]{:S(2)}) copy-start(bf16[416,384]{1,0:T(8,128)(2,1)} %copy-done.7) | copy-start | bytes 958468
  78.9 8.9 %copy-start.10 = (bf16[416,384]{1,0:T(8,128)(2,1)S(1)}, bf16[416,384]{1,0:T(8,128)(2,1)}, u32[]{:S(2)}) copy-start(bf16[416,384]{1,0:T(8,128)(2,1)} %copy-done.9) | copy-start | bytes 958468
  80.2 28.4 %all-to-all-start.1 = ((bf16[8,32,384]{2,1,0:T(8,128)(2,1)}), bf16[8,32,384]{2,1,0:T(8,128)(2,1)S(1)}, u32[]{:S(2)}, u32[]{:S(2)}) async-start(bf16[8,32,384]{2,1,0:T(8,128)(2,1)} %bitcast.22), calls=%async_computation.1 | async-start | bytes 393216 | tf_op jit(solution)/shard_map/all_to_all | solution.py:237
  94.7 14.4 %collective-permute-start.8 = (bf16[400,256]{1,0:T(8,128)(2,1)S(1)}, bf16[400,256]{1,0:T(8,128)(2,1)S(1)}, u32[]{:S(2)}, u32[]{:S(2)}) collective-permute-start(bf16[400,256]{1,0:T(8,128)(2,1)S(1)} %get-tuple-element.20.refs_8_), channel_id=1, source_target_pairs={{0,320},{64,256},{128,448},{192,384},{256,64},{320,0},{384,192},{4... | collective-permute-start | bytes 614408 | tf_op jit(solution)/shard_map/ppermute | solution.py:184
  97.4 18.0 %collective-permute-start.9 = (bf16[400,256]{1,0:T(8,128)(2,1)S(1)}, bf16[400,256]{1,0:T(8,128)(2,1)S(1)}, u32[]{:S(2)}, u32[]{:S(2)}) collective-permute-start(bf16[400,256]{1,0:T(8,128)(2,1)S(1)} %get-tuple-element.21), channel_id=1, source_target_pairs={{0,192},{64,384},{128,320},{192,0},{256,448},{320,128},{384,64},{4... | collective-permute-start | bytes 614408 | tf_op jit(solution)/shard_map/ppermute | solution.py:184
  102.3 17.6 %collective-permute-start.10 = (bf16[400,256]{1,0:T(8,128)(2,1)S(1)}, bf16[400,256]{1,0:T(8,128)(2,1)S(1)}, u32[]{:S(2)}, u32[]{:S(2)}) collective-permute-start(bf16[400,256]{1,0:T(8,128)(2,1)S(1)} %get-tuple-element.22), channel_id=1, source_target_pairs={{0,448},{64,128},{128,64},{192,256},{256,192},{320,384},{384,320},... | collective-permute-start | bytes 614408 | tf_op jit(solution)/shard_map/ppermute | solution.py:184
  138.0 19.6 %collective-permute-start.12 = (bf16[256,640]{1,0:T(8,128)(2,1)S(1)}, bf16[256,640]{1,0:T(8,128)(2,1)S(1)}, u32[]{:S(2)}, u32[]{:S(2)}) collective-permute-start(bf16[256,640]{1,0:T(8,128)(2,1)S(1)} %project.2.rest_0_), channel_id=1, source_target_pairs={{0,4},{4,0},{1,5},{5,1},{2,6},{6,2},{3,7},{7,3},{8,12},{12,8},{9,1... | collective-permute-start | bytes 983048 | tf_op jit(solution)/shard_map/ppermute | solution.py:25
Sparse Core Ops, SparseCore 0:
  68.5 60.4 all-gather.2
